TPU v7x, 256 devices: a whole 4x4x8 slice. The times are simulated.
256 devices in a mesh: fsdp: 4 (over y), seq: 64 (over z, x, core).
Axes of the slice: x: 4, y: 4, z: 8, core: 2. Of those that a mesh axis runs over, the one named last changes fastest.
Arguments:
- tokens: bfloat16 [16384, 8192], P('seq', 'fsdp'), may hold values from -400 to 400
- norm_gain: float32 [8192], P('fsdp'), may hold values from 0.1 to 1.9
- in_weight: bfloat16 [8192, 3, 512], P('fsdp'), may hold values from -0.0625 to 0.0625
- short_filter: float32 [512, 3, 3], P('fsdp'), may hold values from -3 to 3
- decay_reach: float32 [512, 16], P('fsdp'), may hold values from 20 to 32768
- mode_freq: float32 [512, 16], P('fsdp'), may hold values from 0.01 to 2.2
- residues: float32 [512, 16], P('fsdp'), may hold values from -1.5 to 1.5
- skip_gain: float32 [512], P('fsdp'), may hold values from -4 to 4
Outputs:
- gated_output: bfloat16 [512, 16384], P('fsdp', 'seq')
All inputs are finite; a program needn't handle non-finite values.
Results may differ from a plain program's by a relative error of at most 0.03.
Values may be sent and summed in bfloat16 or wider, within the bound.
No kernel may reach another device: no remote copies, remote signals or barrier semaphores. Data moves between devices by JAX's collectives and lax.ppermute only.
A program may use at most 192 MiB of HBM per device.

v0:
```python
import math

import jax
import jax.numpy as jnp
from jax import lax
from jax.sharding import PartitionSpec as P

D = 8192


def swapped(block, axis, stride):
    count = lax.axis_size(axis)
    route = []
    for low in range(count):
        high = low | 1 << stride
        if high != low and high < count:
            route += [(low, high), (high, low)]
    return lax.ppermute(block, axis, route)


def shifted(shard, axis, by):
    peers = lax.axis_size(axis)
    pairs = [(i, i + by) for i in range(peers) if 0 <= i + by < peers]
    return lax.ppermute(shard, axis, pairs)


def rotate(packed, rotation):
    cosine = jnp.cos(rotation)
    sine = jnp.sin(rotation)
    return jnp.stack([packed[0] * cosine - packed[1] * sine, packed[0] * sine + packed[1] * cosine])


def multiply(left_value, right_value):
    return jnp.stack(
        [
            left_value[0] * right_value[0] - left_value[1] * right_value[1],
            left_value[0] * right_value[1] + left_value[1] * right_value[0],
        ]
    )


def complex_table(extent, sign):
    products = (
        lax.broadcasted_iota(jnp.int32, (extent, extent), 0)
        * lax.broadcasted_iota(jnp.int32, (extent, extent), 1)
        % extent
    )
    rotation = sign * 2.0 * math.pi / extent * products.astype(jnp.float32)
    return jnp.stack([jnp.cos(rotation), jnp.sin(rotation)])


def combine_parts(partial_value):
    return jnp.stack(
        [partial_value[0, 0] - partial_value[1, 1], partial_value[0, 1] + partial_value[1, 0]]
    )


def last_transform(packed, sign):
    dft_table = complex_table(packed.shape[-1], sign)
    partial_value = jnp.einsum(
        "p...t,qtk->pq...k",
        packed,
        dft_table,
        precision=lax.Precision.HIGHEST,
        preferred_element_type=jnp.float32,
    )
    return combine_parts(partial_value)


def split_halves(signal, positions, length):
    rotation = -math.pi / length * positions.astype(jnp.float32)
    blank_part = jnp.zeros_like(signal)
    return jnp.stack(
        [
            jnp.stack([signal, signal * jnp.cos(rotation)]),
            jnp.stack([blank_part, signal * jnp.sin(rotation)]),
        ]
    )


def join_halves(packed, positions, length):
    rotation = math.pi / length * positions.astype(jnp.float32)
    return (packed[0, 0] + jnp.cos(rotation) * packed[0, 1] - jnp.sin(rotation) * packed[1, 1]) / (
        2.0 * length
    )


def filter_spectrum(decay_rate, mode_weight, mode_freq, freq_phase, length):
    channels = decay_rate.shape[0]
    trailing = (1,) * (freq_phase.ndim - 2)
    out_shape = (2, channels) + freq_phase.shape[2:]
    parity = jnp.array([1.0, -1.0], jnp.float32).reshape((2, 1) + trailing)

    def pick_mode(table, mode_index):
        return lax.dynamic_slice_in_dim(table, mode_index, 1, 1)

    def add_mode(mode_index, running):
        real_sum, imag_sum = running
        mode_rate = pick_mode(decay_rate, mode_index)
        mode_gain = pick_mode(mode_weight, mode_index)
        mode_turn = pick_mode(mode_freq, mode_index)
        retained = jnp.exp(-mode_rate)
        tail_factor = jnp.exp(-mode_rate * length) * parity
        end_cosine = jnp.cos(mode_turn * length)
        end_sine = jnp.sin(mode_turn * length)
        for turn_sign in (1.0, -1.0):
            phase_shift = freq_phase + turn_sign * mode_turn
            half_sine = jnp.sin(0.5 * phase_shift)
            denom_real = -jnp.expm1(-mode_rate) + 2.0 * retained * half_sine * half_sine
            denom_imag = -retained * jnp.sin(phase_shift)
            numer_real = 1.0 - tail_factor * end_cosine
            numer_imag = -turn_sign * tail_factor * end_sine
            weighting = 0.5 * mode_gain / (denom_real * denom_real + denom_imag * denom_imag)
            real_sum = real_sum + weighting * (numer_real * denom_real + numer_imag * denom_imag)
            imag_sum = imag_sum + weighting * (numer_imag * denom_real - numer_real * denom_imag)
        return (real_sum, imag_sum)

    initial = jnp.zeros(out_shape, jnp.float32)
    real_sum, imag_sum = lax.fori_loop(0, decay_rate.shape[1], add_mode, (initial, initial))
    return jnp.stack([real_sum, imag_sum])


def bit_reverse(seq_index, bit_count):
    result = jnp.zeros_like(seq_index)
    for bit_place in range(bit_count):
        result = result + ((seq_index >> bit_place & 1) << bit_count - 1 - bit_place)
    return result


def butterfly_conv(signal, decay_rate, mode_weight, mode_freq, seq_index, seq_size, length):
    block_rows = signal.shape[-1]
    local_rows = lax.iota(jnp.int32, block_rows)
    positions = seq_index * block_rows + local_rows
    packed = split_halves(signal, positions, length)
    bit_count = seq_size.bit_length() - 1
    for section_bit in reversed(range(bit_count)):
        half_span = 1 << section_bit
        partner = swapped(packed.astype(jnp.bfloat16), "seq", section_bit).astype(packed.dtype)
        upper_half = seq_index >> section_bit & 1 == 1
        rotation = -math.pi / half_span * (seq_index & half_span - 1).astype(jnp.float32)
        packed = jnp.where(upper_half, rotate(partner - packed, rotation), packed + partner)
    freq_block = bit_reverse(seq_index, bit_count)
    twiddle = 2.0 * math.pi / length * (local_rows * freq_block % length).astype(jnp.float32)
    packed = last_transform(rotate(packed, -twiddle), -1.0)
    freq_index = 2 * (freq_block + seq_size * local_rows)
    freq_phase = (
        -math.pi / length * jnp.stack([freq_index, freq_index + 1]).astype(jnp.float32)[:, None, :]
    )
    packed = multiply(
        packed, filter_spectrum(decay_rate, mode_weight, mode_freq, freq_phase, length)
    )
    packed = rotate(last_transform(packed, 1.0), twiddle)
    for section_bit in range(bit_count):
        half_span = 1 << section_bit
        partner = swapped(packed.astype(jnp.bfloat16), "seq", section_bit).astype(packed.dtype)
        upper_half = seq_index >> section_bit & 1 == 1
        rotation = math.pi / half_span * (seq_index & half_span - 1).astype(jnp.float32)
        packed = jnp.where(
            upper_half, partner - rotate(packed, rotation), packed + rotate(partner, rotation)
        )
    return join_halves(packed, positions, length)


def body(tokens, norm_gain, in_weight, short_filter, decay_reach, mode_freq, residues, skip_gain):
    inputs = tokens.astype(jnp.float32)
    row_total = lax.psum(jnp.sum(inputs * inputs, axis=1), "fsdp")
    inv_rms = lax.rsqrt(row_total / D + 1e-06)
    normed = (inputs * inv_rms[:, None] * norm_gain).astype(jnp.bfloat16)
    projected = lax.psum_scatter(
        jnp.einsum("td,dgc->cgt", normed, in_weight, preferred_element_type=jnp.float32).astype(
            jnp.bfloat16
        ),
        "fsdp",
        scatter_dimension=0,
        tiled=True,
    )
    rim_rows = shifted(projected[:, :, -2:], "seq", 1)
    extended = jnp.concatenate([rim_rows, projected], axis=2).astype(jnp.float32)
    streams = (
        short_filter[:, :, 0:1] * extended[:, :, 2:]
        + short_filter[:, :, 1:2] * extended[:, :, 1:-1]
        + short_filter[:, :, 2:3] * extended[:, :, :-2]
    )
    gate_stream = streams[:, 0]
    signal = streams[:, 1] * streams[:, 2]
    block_rows = tokens.shape[0]
    seq_size = lax.axis_size("seq")
    length = block_rows * seq_size
    seq_index = lax.axis_index("seq")
    decay_rate = 1.0 / decay_reach
    mode_weight = residues * jnp.sqrt(2.0 * decay_rate)
    long_conv = butterfly_conv(
        signal, decay_rate, mode_weight, mode_freq, seq_index, seq_size, length
    )
    return (gate_stream * (long_conv + skip_gain[:, None] * signal)).astype(jnp.bfloat16)


def solution(mesh):
    placed = (
        P("seq", "fsdp"),
        P("fsdp"),
        P("fsdp", None, None),
        P("fsdp", None, None),
        P("fsdp", None),
        P("fsdp", None),
        P("fsdp", None),
        P("fsdp"),
    )
    return jax.shard_map(
        body, mesh=mesh, in_specs=placed, out_specs=P("fsdp", "seq"), check_vma=False
    )
```

profile of v0, /device:TPU:8, one launch (start us, length us, event | category | flops | bytes accessed | tf_op | source)
XLA Modules:
  0.0 256.6 jit_solution(16470403103864742357)
XLA Ops:
  8.0 9.9 %psum.7 = f32[256]{0:T(256)S(1)} all-reduce(f32[256]{0:T(256)S(1)} %fusion.40), channel_id=1, replica_groups=mesh['fsdp'=4,'seq'=64] {'fsdp'}, use_global_device_ids=true, to_apply=%region_1.0 | all-reduce | flops 256 | bytes 2048 | tf_op jit(solution)/shard_map/psum | solution.py:166
  18.0 5.0 %convolution_convert_fusion = bf16[256,3,512]{2,0,1:T(8,128)(2,1)S(1)} fusion(bf16[2048,3,512]{2,0,1:T(8,128)(2,1)} %param.13, bf16[256,2048]{1,0:T(8,128)(2,1)} %param.11, f32[2048]{0:T(1024)} %param.12, f32[256]{0:T(256)S(1)} %add_rsqrt_fusion), kind=kOutput, calls=%fused_computation.64 | convolution fusion | flops 1613103104 | bytes 8135680 | tf_op jit(solution)/shard_map/td,dgc->cgt/dot_general | solution.py:170
  24.3 24.2 %reduce-scatter.4.cloned.1.call-done = bf16[128,768]{1,0:T(8,128)(2,1)} async-done(((bf16[512,768]{1,0:T(8,128)(2,1)}), bf16[128,768]{1,0:T(8,128)(2,1)}) %reduce-scatter.4.cloned.1.call-update) | async-done | bytes 196624
  52.7 12.8 %collective-permute-start.1 = (bf16[2,2,128,256]{3,2,1,0:T(8,128)(2,1)S(1)}, bf16[2,2,128,256]{3,2,1,0:T(8,128)(2,1)S(1)}, u32[]{:S(2)}, u32[]{:S(2)}) collective-permute-start(bf16[2,2,128,256]{3,2,1,0:T(8,128)(2,1)S(1)} %fusion.70), channel_id=1, source_target_pairs={{0,32},{32,0},{1,33},{33,1},{2,34},{34,2},{3,35},{35,3},{4,36},{36... | collective-permute-start | bytes 786440 | tf_op jit(solution)/shard_map/ppermute | solution.py:18
  65.7 7.2 %collective-permute-done.1 = bf16[2,2,128,256]{3,2,1,0:T(8,128)(2,1)S(1)} collective-permute-done((bf16[2,2,128,256]{3,2,1,0:T(8,128)(2,1)S(1)}, bf16[2,2,128,256]{3,2,1,0:T(8,128)(2,1)S(1)}, u32[]{:S(2)}, u32[]{:S(2)}) %collective-permute-start.1) | collective-permute-done | bytes 262176 | tf_op jit(solution)/shard_map/ppermute | solution.py:18
  76.5 8.9 %collective-permute-done.2 = bf16[2,2,128,256]{3,2,1,0:T(8,128)(2,1)S(1)} collective-permute-done((bf16[2,2,128,256]{3,2,1,0:T(8,128)(2,1)S(1)}, bf16[2,2,128,256]{3,2,1,0:T(8,128)(2,1)S(1)}, u32[]{:S(2)}, u32[]{:S(2)}) %collective-permute-start.2) | collective-permute-done | bytes 262176 | tf_op jit(solution)/shard_map/ppermute | solution.py:18
  86.0 7.1 %collective-permute-done.3 = bf16[2,2,128,256]{3,2,1,0:T(8,128)(2,1)S(1)} collective-permute-done((bf16[2,2,128,256]{3,2,1,0:T(8,128)(2,1)S(1)}, bf16[2,2,128,256]{3,2,1,0:T(8,128)(2,1)S(1)}, u32[]{:S(2)}, u32[]{:S(2)}) %collective-permute-start.3) | collective-permute-done | bytes 262176 | tf_op jit(solution)/shard_map/ppermute | solution.py:18
  96.5 4.8 %collective-permute-done.4 = bf16[2,2,128,256]{3,2,1,0:T(8,128)(2,1)S(1)} collective-permute-done((bf16[2,2,128,256]{3,2,1,0:T(8,128)(2,1)S(1)}, bf16[2,2,128,256]{3,2,1,0:T(8,128)(2,1)S(1)}, u32[]{:S(2)}, u32[]{:S(2)}) %collective-permute-start.4) | collective-permute-done | bytes 262176 | tf_op jit(solution)/shard_map/ppermute | solution.py:18
  101.6 4.0 %collective-permute-start.5 = (bf16[2,2,128,256]{3,2,1,0:T(8,128)(2,1)S(1)}, bf16[2,2,128,256]{3,2,1,0:T(8,128)(2,1)S(1)}, u32[]{:S(2)}, u32[]{:S(2)}) collective-permute-start(bf16[2,2,128,256]{3,2,1,0:T(8,128)(2,1)S(1)} %get-tuple-element.254), channel_id=1, source_target_pairs={{0,2},{2,0},{1,3},{3,1},{4,6},{6,4},{5,7},{7,5},{8,10},{10,8},{9,1... | collective-permute-start | bytes 786440 | tf_op jit(solution)/shard_map/ppermute | solution.py:18
  105.6 78.4 %while.17 = (s32[]{:T(128)}, f32[2,128,256]{2,1,0:T(8,128)S(1)}, f32[2,128,256]{2,1,0:T(8,128)S(1)}, f32[128,16]{0,1:T(8,128)S(1)}, f32[128,16]{0,1:T(8,128)S(1)...) while((s32[]{:T(128)}, f32[2,128,256]{2,1,0:T(8,128)S(1)}, ...), condition=%wide.region_4.5_spmd.clone.clone, body=%wide.region_3.4_spmd.clone.clone.sunk | while | flops 2755203 | bytes 1070719 | solution.py:119
  106.5 4.0 %fusion.132 = (f32[2,128,256]{2,1,0:T(8,128)S(1)}, f32[2,128,256]{2,1,0:T(8,128)S(1)}) fusion(f32[2,128,256]{2,1,0:T(8,128)S(1)} %get-tuple-element.416, f32[2,128]{1,0:T(2,128)S(1)} %get-tuple-element.395, f32[128]{0:T(128)S(1)} %get-tuple-element.396, f32[2,128]{1,0:T(2,128)S(1)} %get-tuple-element.397, f32[2,128]{1,0:T(2,128)S(1)} %get-tuple-element.398, ...), kind=kLoop, calls=%fused_computation.21.clone.1 | loop fusion | flops 2752512 | bytes 1056769 | tf_op jit(solution)/shard_map/while/body/eval_jaxpr/add | solution.py:115
  111.4 4.0 %fusion.132 = (f32[2,128,256]{2,1,0:T(8,128)S(1)}, f32[2,128,256]{2,1,0:T(8,128)S(1)}) fusion(f32[2,128,256]{2,1,0:T(8,128)S(1)} %get-tuple-element.416, f32[2,128]{1,0:T(2,128)S(1)} %get-tuple-element.395, f32[128]{0:T(128)S(1)} %get-tuple-element.396, f32[2,128]{1,0:T(2,128)S(1)} %get-tuple-element.397, f32[2,128]{1,0:T(2,128)S(1)} %get-tuple-element.398, ...), kind=kLoop, calls=%fused_computation.21.clone.1 | loop fusion | flops 2752512 | bytes 1056769 | tf_op jit(solution)/shard_map/while/body/eval_jaxpr/add | solution.py:115
  116.3 4.0 %fusion.132 = (f32[2,128,256]{2,1,0:T(8,128)S(1)}, f32[2,128,256]{2,1,0:T(8,128)S(1)}) fusion(f32[2,128,256]{2,1,0:T(8,128)S(1)} %get-tuple-element.416, f32[2,128]{1,0:T(2,128)S(1)} %get-tuple-element.395, f32[128]{0:T(128)S(1)} %get-tuple-element.396, f32[2,128]{1,0:T(2,128)S(1)} %get-tuple-element.397, f32[2,128]{1,0:T(2,128)S(1)} %get-tuple-element.398, ...), kind=kLoop, calls=%fused_computation.21.clone.1 | loop fusion | flops 2752512 | bytes 1056769 | tf_op jit(solution)/shard_map/while/body/eval_jaxpr/add | solution.py:115
  121.2 4.0 %fusion.132 = (f32[2,128,256]{2,1,0:T(8,128)S(1)}, f32[2,128,256]{2,1,0:T(8,128)S(1)}) fusion(f32[2,128,256]{2,1,0:T(8,128)S(1)} %get-tuple-element.416, f32[2,128]{1,0:T(2,128)S(1)} %get-tuple-element.395, f32[128]{0:T(128)S(1)} %get-tuple-element.396, f32[2,128]{1,0:T(2,128)S(1)} %get-tuple-element.397, f32[2,128]{1,0:T(2,128)S(1)} %get-tuple-element.398, ...), kind=kLoop, calls=%fused_computation.21.clone.1 | loop fusion | flops 2752512 | bytes 1056769 | tf_op jit(solution)/shard_map/while/body/eval_jaxpr/add | solution.py:115
  126.1 4.0 %fusion.132 = (f32[2,128,256]{2,1,0:T(8,128)S(1)}, f32[2,128,256]{2,1,0:T(8,128)S(1)}) fusion(f32[2,128,256]{2,1,0:T(8,128)S(1)} %get-tuple-element.416, f32[2,128]{1,0:T(2,128)S(1)} %get-tuple-element.395, f32[128]{0:T(128)S(1)} %get-tuple-element.396, f32[2,128]{1,0:T(2,128)S(1)} %get-tuple-element.397, f32[2,128]{1,0:T(2,128)S(1)} %get-tuple-element.398, ...), kind=kLoop, calls=%fused_computation.21.clone.1 | loop fusion | flops 2752512 | bytes 1056769 | tf_op jit(solution)/shard_map/while/body/eval_jaxpr/add | solution.py:115
  131.0 4.0 %fusion.132 = (f32[2,128,256]{2,1,0:T(8,128)S(1)}, f32[2,128,256]{2,1,0:T(8,128)S(1)}) fusion(f32[2,128,256]{2,1,0:T(8,128)S(1)} %get-tuple-element.416, f32[2,128]{1,0:T(2,128)S(1)} %get-tuple-element.395, f32[128]{0:T(128)S(1)} %get-tuple-element.396, f32[2,128]{1,0:T(2,128)S(1)} %get-tuple-element.397, f32[2,128]{1,0:T(2,128)S(1)} %get-tuple-element.398, ...), kind=kLoop, calls=%fused_computation.21.clone.1 | loop fusion | flops 2752512 | bytes 1056769 | tf_op jit(solution)/shard_map/while/body/eval_jaxpr/add | solution.py:115
  135.9 4.0 %fusion.132 = (f32[2,128,256]{2,1,0:T(8,128)S(1)}, f32[2,128,256]{2,1,0:T(8,128)S(1)}) fusion(f32[2,128,256]{2,1,0:T(8,128)S(1)} %get-tuple-element.416, f32[2,128]{1,0:T(2,128)S(1)} %get-tuple-element.395, f32[128]{0:T(128)S(1)} %get-tuple-element.396, f32[2,128]{1,0:T(2,128)S(1)} %get-tuple-element.397, f32[2,128]{1,0:T(2,128)S(1)} %get-tuple-element.398, ...), kind=kLoop, calls=%fused_computation.21.clone.1 | loop fusion | flops 2752512 | bytes 1056769 | tf_op jit(solution)/shard_map/while/body/eval_jaxpr/add | solution.py:115
  140.8 4.0 %fusion.132 = (f32[2,128,256]{2,1,0:T(8,128)S(1)}, f32[2,128,256]{2,1,0:T(8,128)S(1)}) fusion(f32[2,128,256]{2,1,0:T(8,128)S(1)} %get-tuple-element.416, f32[2,128]{1,0:T(2,128)S(1)} %get-tuple-element.395, f32[128]{0:T(128)S(1)} %get-tuple-element.396, f32[2,128]{1,0:T(2,128)S(1)} %get-tuple-element.397, f32[2,128]{1,0:T(2,128)S(1)} %get-tuple-element.398, ...), kind=kLoop, calls=%fused_computation.21.clone.1 | loop fusion | flops 2752512 | bytes 1056769 | tf_op jit(solution)/shard_map/while/body/eval_jaxpr/add | solution.py:115
  145.7 4.0 %fusion.132 = (f32[2,128,256]{2,1,0:T(8,128)S(1)}, f32[2,128,256]{2,1,0:T(8,128)S(1)}) fusion(f32[2,128,256]{2,1,0:T(8,128)S(1)} %get-tuple-element.416, f32[2,128]{1,0:T(2,128)S(1)} %get-tuple-element.395, f32[128]{0:T(128)S(1)} %get-tuple-element.396, f32[2,128]{1,0:T(2,128)S(1)} %get-tuple-element.397, f32[2,128]{1,0:T(2,128)S(1)} %get-tuple-element.398, ...), kind=kLoop, calls=%fused_computation.21.clone.1 | loop fusion | flops 2752512 | bytes 1056769 | tf_op jit(solution)/shard_map/while/body/eval_jaxpr/add | solution.py:115
  150.6 4.0 %fusion.132 = (f32[2,128,256]{2,1,0:T(8,128)S(1)}, f32[2,128,256]{2,1,0:T(8,128)S(1)}) fusion(f32[2,128,256]{2,1,0:T(8,128)S(1)} %get-tuple-element.416, f32[2,128]{1,0:T(2,128)S(1)} %get-tuple-element.395, f32[128]{0:T(128)S(1)} %get-tuple-element.396, f32[2,128]{1,0:T(2,128)S(1)} %get-tuple-element.397, f32[2,128]{1,0:T(2,128)S(1)} %get-tuple-element.398, ...), kind=kLoop, calls=%fused_computation.21.clone.1 | loop fusion | flops 2752512 | bytes 1056769 | tf_op jit(solution)/shard_map/while/body/eval_jaxpr/add | solution.py:115
  155.5 4.0 %fusion.132 = (f32[2,128,256]{2,1,0:T(8,128)S(1)}, f32[2,128,256]{2,1,0:T(8,128)S(1)}) fusion(f32[2,128,256]{2,1,0:T(8,128)S(1)} %get-tuple-element.416, f32[2,128]{1,0:T(2,128)S(1)} %get-tuple-element.395, f32[128]{0:T(128)S(1)} %get-tuple-element.396, f32[2,128]{1,0:T(2,128)S(1)} %get-tuple-element.397, f32[2,128]{1,0:T(2,128)S(1)} %get-tuple-element.398, ...), kind=kLoop, calls=%fused_computation.21.clone.1 | loop fusion | flops 2752512 | bytes 1056769 | tf_op jit(solution)/shard_map/while/body/eval_jaxpr/add | solution.py:115
  160.4 4.0 %fusion.132 = (f32[2,128,256]{2,1,0:T(8,128)S(1)}, f32[2,128,256]{2,1,0:T(8,128)S(1)}) fusion(f32[2,128,256]{2,1,0:T(8,128)S(1)} %get-tuple-element.416, f32[2,128]{1,0:T(2,128)S(1)} %get-tuple-element.395, f32[128]{0:T(128)S(1)} %get-tuple-element.396, f32[2,128]{1,0:T(2,128)S(1)} %get-tuple-element.397, f32[2,128]{1,0:T(2,128)S(1)} %get-tuple-element.398, ...), kind=kLoop, calls=%fused_computation.21.clone.1 | loop fusion | flops 2752512 | bytes 1056769 | tf_op jit(solution)/shard_map/while/body/eval_jaxpr/add | solution.py:115
  165.3 4.0 %fusion.132 = (f32[2,128,256]{2,1,0:T(8,128)S(1)}, f32[2,128,256]{2,1,0:T(8,128)S(1)}) fusion(f32[2,128,256]{2,1,0:T(8,128)S(1)} %get-tuple-element.416, f32[2,128]{1,0:T(2,128)S(1)} %get-tuple-element.395, f32[128]{0:T(128)S(1)} %get-tuple-element.396, f32[2,128]{1,0:T(2,128)S(1)} %get-tuple-element.397, f32[2,128]{1,0:T(2,128)S(1)} %get-tuple-element.398, ...), kind=kLoop, calls=%fused_computation.21.clone.1 | loop fusion | flops 2752512 | bytes 1056769 | tf_op jit(solution)/shard_map/while/body/eval_jaxpr/add | solution.py:115
  170.2 4.0 %fusion.132 = (f32[2,128,256]{2,1,0:T(8,128)S(1)}, f32[2,128,256]{2,1,0:T(8,128)S(1)}) fusion(f32[2,128,256]{2,1,0:T(8,128)S(1)} %get-tuple-element.416, f32[2,128]{1,0:T(2,128)S(1)} %get-tuple-element.395, f32[128]{0:T(128)S(1)} %get-tuple-element.396, f32[2,128]{1,0:T(2,128)S(1)} %get-tuple-element.397, f32[2,128]{1,0:T(2,128)S(1)} %get-tuple-element.398, ...), kind=kLoop, calls=%fused_computation.21.clone.1 | loop fusion | flops 2752512 | bytes 1056769 | tf_op jit(solution)/shard_map/while/body/eval_jaxpr/add | solution.py:115
  175.1 4.0 %fusion.132 = (f32[2,128,256]{2,1,0:T(8,128)S(1)}, f32[2,128,256]{2,1,0:T(8,128)S(1)}) fusion(f32[2,128,256]{2,1,0:T(8,128)S(1)} %get-tuple-element.416, f32[2,128]{1,0:T(2,128)S(1)} %get-tuple-element.395, f32[128]{0:T(128)S(1)} %get-tuple-element.396, f32[2,128]{1,0:T(2,128)S(1)} %get-tuple-element.397, f32[2,128]{1,0:T(2,128)S(1)} %get-tuple-element.398, ...), kind=kLoop, calls=%fused_computation.21.clone.1 | loop fusion | flops 2752512 | bytes 1056769 | tf_op jit(solution)/shard_map/while/body/eval_jaxpr/add | solution.py:115
  180.0 4.0 %fusion.132 = (f32[2,128,256]{2,1,0:T(8,128)S(1)}, f32[2,128,256]{2,1,0:T(8,128)S(1)}) fusion(f32[2,128,256]{2,1,0:T(8,128)S(1)} %get-tuple-element.416, f32[2,128]{1,0:T(2,128)S(1)} %get-tuple-element.395, f32[128]{0:T(128)S(1)} %get-tuple-element.396, f32[2,128]{1,0:T(2,128)S(1)} %get-tuple-element.397, f32[2,128]{1,0:T(2,128)S(1)} %get-tuple-element.398, ...), kind=kLoop, calls=%fused_computation.21.clone.1 | loop fusion | flops 2752512 | bytes 1056769 | tf_op jit(solution)/shard_map/while/body/eval_jaxpr/add | solution.py:115
  192.4 8.0 %collective-permute-done.8 = bf16[2,2,128,256]{3,2,1,0:T(8,128)(2,1)S(1)} collective-permute-done((bf16[2,2,128,256]{3,2,1,0:T(8,128)(2,1)S(1)}, bf16[2,2,128,256]{3,2,1,0:T(8,128)(2,1)S(1)}, u32[]{:S(2)}, u32[]{:S(2)}) %collective-permute-start.8) | collective-permute-done | bytes 262176 | tf_op jit(solution)/shard_map/ppermute | solution.py:18
  200.7 4.5 %collective-permute-start.9 = (bf16[2,2,128,256]{3,2,1,0:T(8,128)(2,1)S(1)}, bf16[2,2,128,256]{3,2,1,0:T(8,128)(2,1)S(1)}, u32[]{:S(2)}, u32[]{:S(2)}) collective-permute-start(bf16[2,2,128,256]{3,2,1,0:T(8,128)(2,1)S(1)} %get-tuple-element.245), channel_id=1, source_target_pairs={{0,4},{4,0},{1,5},{5,1},{2,6},{6,2},{3,7},{7,3},{8,12},{12,8},{9,1... | collective-permute-start | bytes 786440 | tf_op jit(solution)/shard_map/ppermute | solution.py:18
  205.4 5.8 %collective-permute-done.9 = bf16[2,2,128,256]{3,2,1,0:T(8,128)(2,1)S(1)} collective-permute-done((bf16[2,2,128,256]{3,2,1,0:T(8,128)(2,1)S(1)}, bf16[2,2,128,256]{3,2,1,0:T(8,128)(2,1)S(1)}, u32[]{:S(2)}, u32[]{:S(2)}) %collective-permute-start.9) | collective-permute-done | bytes 262176 | tf_op jit(solution)/shard_map/ppermute | solution.py:18
  213.0 5.6 %collective-permute-done.10 = bf16[2,2,128,256]{3,2,1,0:T(8,128)(2,1)S(1)} collective-permute-done((bf16[2,2,128,256]{3,2,1,0:T(8,128)(2,1)S(1)}, bf16[2,2,128,256]{3,2,1,0:T(8,128)(2,1)S(1)}, u32[]{:S(2)}, u32[]{:S(2)}) %collective-permute-start.10) | collective-permute-done | bytes 262176 | tf_op jit(solution)/shard_map/ppermute | solution.py:18
  222.5 9.9 %collective-permute-done.11 = bf16[2,2,128,256]{3,2,1,0:T(8,128)(2,1)S(1)} collective-permute-done((bf16[2,2,128,256]{3,2,1,0:T(8,128)(2,1)S(1)}, bf16[2,2,128,256]{3,2,1,0:T(8,128)(2,1)S(1)}, u32[]{:S(2)}, u32[]{:S(2)}) %collective-permute-start.11) | collective-permute-done | bytes 262176 | tf_op jit(solution)/shard_map/ppermute | solution.py:18
  234.7 14.1 %collective-permute-done.12 = bf16[2,2,128,256]{3,2,1,0:T(8,128)(2,1)S(1)} collective-permute-done((bf16[2,2,128,256]{3,2,1,0:T(8,128)(2,1)S(1)}, bf16[2,2,128,256]{3,2,1,0:T(8,128)(2,1)S(1)}, u32[]{:S(2)}, u32[]{:S(2)}) %collective-permute-start.12) | collective-permute-done | bytes 262176 | tf_op jit(solution)/shard_map/ppermute | solution.py:18
  (202 shorter events, 45.3 us)
Async XLA Ops:
  6.5 41.9 %reduce-scatter.4.cloned.1.call-start = ((), (), s32[]{:S(2)}) async-start(), calls=%async_computation.1 | async-start | bytes 983040
  22.9 1.3 copy-start.3
  49.8 2.2 collective-permute-start
  52.7 20.2 %collective-permute-start.1 = (bf16[2,2,128,256]{3,2,1,0:T(8,128)(2,1)S(1)}, bf16[2,2,128,256]{3,2,1,0:T(8,128)(2,1)S(1)}, u32[]{:S(2)}, u32[]{:S(2)}) collective-permute-start(bf16[2,2,128,256]{3,2,1,0:T(8,128)(2,1)S(1)} %fusion.70), channel_id=1, source_target_pairs={{0,32},{32,0},{1,33},{33,1},{2,34},{34,2},{3,35},{35,3},{4,36},{36... | collective-permute-start | bytes 786440 | tf_op jit(solution)/shard_map/ppermute | solution.py:18
  73.2 12.3 %collective-permute-start.2 = (bf16[2,2,128,256]{3,2,1,0:T(8,128)(2,1)S(1)}, bf16[2,2,128,256]{3,2,1,0:T(8,128)(2,1)S(1)}, u32[]{:S(2)}, u32[]{:S(2)}) collective-permute-start(bf16[2,2,128,256]{3,2,1,0:T(8,128)(2,1)S(1)} %get-tuple-element.260), channel_id=1, source_target_pairs={{0,16},{16,0},{1,17},{17,1},{2,18},{18,2},{3,19},{19,3},{4,20},{20... | collective-permute-start | bytes 786440 | tf_op jit(solution)/shard_map/ppermute | solution.py:18
  85.6 7.4 %collective-permute-start.3 = (bf16[2,2,128,256]{3,2,1,0:T(8,128)(2,1)S(1)}, bf16[2,2,128,256]{3,2,1,0:T(8,128)(2,1)S(1)}, u32[]{:S(2)}, u32[]{:S(2)}) collective-permute-start(bf16[2,2,128,256]{3,2,1,0:T(8,128)(2,1)S(1)} %get-tuple-element.258), channel_id=1, source_target_pairs={{0,8},{8,0},{1,9},{9,1},{2,10},{10,2},{3,11},{11,3},{4,12},{12,4},... | collective-permute-start | bytes 786440 | tf_op jit(solution)/shard_map/ppermute | solution.py:18
  93.1 3.4 %copy-start.1 = (f32[128,16]{0,1:T(8,128)S(1)}, f32[128,16]{0,1:T(8,128)}, u32[]{:S(2)}) copy-start(f32[128,16]{0,1:T(8,128)} %param.15) | copy-start | bytes 24580
  93.1 3.4 %copy-start.2 = (f32[128,16]{0,1:T(8,128)S(1)}, f32[128,16]{0,1:T(8,128)}, u32[]{:S(2)}) copy-start(f32[128,16]{0,1:T(8,128)} %param.17) | copy-start | bytes 24580
  93.3 8.0 %collective-permute-start.4 = (bf16[2,2,128,256]{3,2,1,0:T(8,128)(2,1)S(1)}, bf16[2,2,128,256]{3,2,1,0:T(8,128)(2,1)S(1)}, u32[]{:S(2)}, u32[]{:S(2)}) collective-permute-start(bf16[2,2,128,256]{3,2,1,0:T(8,128)(2,1)S(1)} %get-tuple-element.256), channel_id=1, source_target_pairs={{0,4},{4,0},{1,5},{5,1},{2,6},{6,2},{3,7},{7,3},{8,12},{12,8},{9,1... | collective-permute-start | bytes 786440 | tf_op jit(solution)/shard_map/ppermute | solution.py:18
  101.3 4.3 %copy-start = (f32[2]{0:T(128)S(1)}, f32[2]{0:T(128)}, u32[]{:S(2)}) copy-start(f32[2]{0:T(128)} %constant.398) | copy-start | bytes 28
  101.6 82.6 %collective-permute-start.5 = (bf16[2,2,128,256]{3,2,1,0:T(8,128)(2,1)S(1)}, bf16[2,2,128,256]{3,2,1,0:T(8,128)(2,1)S(1)}, u32[]{:S(2)}, u32[]{:S(2)}) collective-permute-start(bf16[2,2,128,256]{3,2,1,0:T(8,128)(2,1)S(1)} %get-tuple-element.254), channel_id=1, source_target_pairs={{0,2},{2,0},{1,3},{3,1},{4,6},{6,4},{5,7},{7,5},{8,10},{10,8},{9,1... | collective-permute-start | bytes 786440 | tf_op jit(solution)/shard_map/ppermute | solution.py:18
  184.5 2.7 %collective-permute-start.6 = (bf16[2,2,128,256]{3,2,1,0:T(8,128)(2,1)S(1)}, bf16[2,2,128,256]{3,2,1,0:T(8,128)(2,1)S(1)}, u32[]{:S(2)}, u32[]{:S(2)}) collective-permute-start(bf16[2,2,128,256]{3,2,1,0:T(8,128)(2,1)S(1)} %get-tuple-element.252), channel_id=1, source_target_pairs={{0,1},{1,0},{2,3},{3,2},{4,5},{5,4},{6,7},{7,6},{8,9},{9,8},{10,11... | collective-permute-start | bytes 786440 | tf_op jit(solution)/shard_map/ppermute | solution.py:18
  189.8 1.7 collective-permute-start.7
  191.8 8.7 %collective-permute-start.8 = (bf16[2,2,128,256]{3,2,1,0:T(8,128)(2,1)S(1)}, bf16[2,2,128,256]{3,2,1,0:T(8,128)(2,1)S(1)}, u32[]{:S(2)}, u32[]{:S(2)}) collective-permute-start(bf16[2,2,128,256]{3,2,1,0:T(8,128)(2,1)S(1)} %get-tuple-element.247), channel_id=1, source_target_pairs={{0,2},{2,0},{1,3},{3,1},{4,6},{6,4},{5,7},{7,5},{8,10},{10,8},{9,1... | collective-permute-start | bytes 786440 | tf_op jit(solution)/shard_map/ppermute | solution.py:18
  200.7 10.5 %collective-permute-start.9 = (bf16[2,2,128,256]{3,2,1,0:T(8,128)(2,1)S(1)}, bf16[2,2,128,256]{3,2,1,0:T(8,128)(2,1)S(1)}, u32[]{:S(2)}, u32[]{:S(2)}) collective-permute-start(bf16[2,2,128,256]{3,2,1,0:T(8,128)(2,1)S(1)} %get-tuple-element.245), channel_id=1, source_target_pairs={{0,4},{4,0},{1,5},{5,1},{2,6},{6,2},{3,7},{7,3},{8,12},{12,8},{9,1... | collective-permute-start | bytes 786440 | tf_op jit(solution)/shard_map/ppermute | solution.py:18
  211.4 7.3 %collective-permute-start.10 = (bf16[2,2,128,256]{3,2,1,0:T(8,128)(2,1)S(1)}, bf16[2,2,128,256]{3,2,1,0:T(8,128)(2,1)S(1)}, u32[]{:S(2)}, u32[]{:S(2)}) collective-permute-start(bf16[2,2,128,256]{3,2,1,0:T(8,128)(2,1)S(1)} %get-tuple-element.243), channel_id=1, source_target_pairs={{0,8},{8,0},{1,9},{9,1},{2,10},{10,2},{3,11},{11,3},{4,12},{12,4},... | collective-permute-start | bytes 786440 | tf_op jit(solution)/shard_map/ppermute | solution.py:18
  218.9 13.5 %collective-permute-start.11 = (bf16[2,2,128,256]{3,2,1,0:T(8,128)(2,1)S(1)}, bf16[2,2,128,256]{3,2,1,0:T(8,128)(2,1)S(1)}, u32[]{:S(2)}, u32[]{:S(2)}) collective-permute-start(bf16[2,2,128,256]{3,2,1,0:T(8,128)(2,1)S(1)} %get-tuple-element.241), channel_id=1, source_target_pairs={{0,16},{16,0},{1,17},{17,1},{2,18},{18,2},{3,19},{19,3},{4,20},{20... | collective-permute-start | bytes 786440 | tf_op jit(solution)/shard_map/ppermute | solution.py:18
  232.6 16.1 %collective-permute-start.12 = (bf16[2,2,128,256]{3,2,1,0:T(8,128)(2,1)S(1)}, bf16[2,2,128,256]{3,2,1,0:T(8,128)(2,1)S(1)}, u32[]{:S(2)}, u32[]{:S(2)}) collective-permute-start(bf16[2,2,128,256]{3,2,1,0:T(8,128)(2,1)S(1)} %get-tuple-element.239), channel_id=1, source_target_pairs={{0,32},{32,0},{1,33},{33,1},{2,34},{34,2},{3,35},{35,3},{4,36},{36... | collective-permute-start | bytes 786440 | tf_op jit(solution)/shard_map/ppermute | solution.py:18
  234.7 14.4 %copy-start.4 = (f32[128]{0:T(128)S(1)}, f32[128]{0:T(128)}, u32[]{:S(2)}) copy-start(f32[128]{0:T(128)} %param.18) | copy-start | bytes 1540
Sparse Core Ops, SparseCore 0:
  24.3 24.1 reduce-scatter.3
where the time goes:
time: 261 us; the launch traced here: 257 us
  waiting for transfers between devices  97.5 us (37%)
  other arithmetic  86.4 us (33%)
  starting transfers between devices  36.7 us (14%)
  between operations  15.6 us (6%)
  blocking collectives  9.91 us (4%)
  matrix products  7.07 us (3%)
  local copies, waits for them, and re-layouts  2.92 us (1%)
    ppermute x12, waiting for transfers between devices, swapped(): return lax.ppermute(block, axis, route)  72.5 us
    add x16, other arithmetic, add_mode(): imag_sum + weighting * (numer_imag * denom_real - numer_real * denom_imag)  63.4 us
    ppermute x12, starting transfers between devices, swapped(): return lax.ppermute(block, axis, route)  35.4 us
    unnamed x2, waiting for transfers between devices  24.2 us
    mul x16, other arithmetic, add_mode(): numer_real = 1.0 - tail_factor * end_cosine  11.8 us
    psum x1, blocking collectives, body(): row_total = lax.psum(jnp.sum(inputs * inputs, axis=1), 'fsdp')  9.91 us
  transfers between devices with their start and end apart: 14, of which 12 were waited for; matrix products, arithmetic and copies ran while one was open for 32% of the time, Pallas kernels for 0%

commit v1 on v0

v1 whole, which is shorter than its diff:
```python
import functools
import math

import jax
import jax.numpy as jnp
from jax import lax
from jax.experimental import pallas as pl
from jax.experimental.pallas import tpu as pltpu
from jax.sharding import PartitionSpec as P

F32 = jnp.float32
BF16 = jnp.bfloat16
D = 8192
MODES = 16
LANES = 128
TILE = 8
SUB = 64
STEPS = SUB // TILE
LOW = 8
RIM = 16
VMEM = pl.BlockSpec(memory_space=pltpu.VMEM)
SMEM = pl.BlockSpec(memory_space=pltpu.SMEM)


def call(kernel, out_shape, in_specs, scratch=(), limit=40 << 20):
    return pl.pallas_call(
        kernel,
        out_shape=out_shape,
        in_specs=in_specs,
        out_specs=jax.tree.map(lambda _: VMEM, out_shape),
        scratch_shapes=list(scratch),
        compiler_params=pltpu.CompilerParams(vmem_limit_bytes=limit),
    )


def shape(*dims, dtype=F32):
    return jax.ShapeDtypeStruct(dims, dtype)


def cmul(a, b):
    return a[0] * b[0] - a[1] * b[1], a[0] * b[1] + a[1] * b[0]


def turn(angle):
    cycles = jnp.floor(angle * (0.5 / math.pi) + 0.5)
    rest = angle - cycles * 6.28125
    rest = rest - cycles * 1.93500518798828125e-3
    rest = rest - cycles * 3.0199159819e-7
    return jnp.cos(rest), jnp.sin(rest)


def table_kernel(reach_ref, freq_ref, res_ref, p8_ref, r7_ref, gt_ref, p64_ref, low_ref, high_ref, h_ref):
    rate = 1.0 / reach_ref[...]
    freq = freq_ref[...]
    gain = res_ref[...] * jnp.sqrt(2.0 * rate)

    def power(n):
        size = jnp.exp(-rate * n)
        cosine, sine = turn(freq * n)
        return size * cosine, size * sine

    one = (jnp.ones_like(rate), jnp.zeros_like(rate))

    def chain(base, count):
        values = [one]
        for _ in range(count - 1):
            values.append(cmul(values[-1], base))
        return values

    ones = chain(power(1.0), TILE + 1)
    for j in range(TILE):
        for c in range(2):
            r7_ref[:, c, j, :] = ones[TILE - 1 - j][c]
            gt_ref[:, c, j, :] = gain * ones[j + 1][c]
    eights = chain(power(8.0), STEPS)
    for k in range(STEPS):
        for c in range(2):
            p8_ref[k, c] = eights[k][c]
    for q, value in enumerate(chain(power(float(SUB)), 4)):
        for c in range(2):
            p64_ref[q, c] = value[c]
    for ref, n in ((low_ref, 256.0), (high_ref, 2048.0)):
        for k, value in enumerate(chain(power(n), LOW)):
            for c in range(2):
                ref[k, c] = jnp.zeros_like(rate)
                ref[LOW + k, c] = value[c]
    taps = [jnp.zeros((TILE, LANES), F32) for _ in range(STEPS)]
    row = lax.broadcasted_iota(jnp.int32, (TILE, LANES), 0)
    for m in range(MODES):
        real = jnp.where(row == 0, gain[m : m + 1], pltpu.roll(gt_ref[m, 0], 1, 0))
        imag = jnp.where(row == 0, 0.0, pltpu.roll(gt_ref[m, 1], 1, 0))
        for k in range(STEPS):
            taps[k] = taps[k] + (eights[k][0][m : m + 1] * real - eights[k][1][m : m + 1] * imag)
    for k in range(STEPS):
        h_ref[TILE * k : TILE * k + TILE] = taps[k]


def tables(reach, freq, res):
    return call(
        table_kernel,
        (
            shape(STEPS, 2, MODES, LANES),
            shape(MODES, 2, TILE, LANES),
            shape(MODES, 2, TILE, LANES),
            shape(4, 2, MODES, LANES),
            shape(2 * LOW, 2, MODES, LANES),
            shape(2 * LOW, 2, MODES, LANES),
            shape(SUB, LANES),
        ),
        [VMEM] * 3,
    )(reach, freq, res)


def prepare_kernel(tok_ref, rim_ref, gain_ref, xg_ref, ss_ref, acc_ref):
    rows, cols = tok_ref.shape
    gain = gain_ref[...]

    def part(ref, at, to, n):
        x = ref[pl.ds(at, n), :].astype(F32)
        xg_ref[pl.ds(to, n), :] = (x * gain).astype(BF16)
        sq = x * x
        acc_ref[pl.ds(to, n), :] = sum(sq[:, i : i + LANES] for i in range(0, cols, LANES))

    for i in range(0, rows, 32):
        part(tok_ref, i, i, 32)
    part(rim_ref, 0, rows, RIM)
    acc_ref[rows + RIM :] = jnp.zeros((acc_ref.shape[0] - rows - RIM, LANES), F32)
    acc = acc_ref[...]
    high = acc.astype(BF16)
    mid = (acc - high.astype(F32)).astype(BF16)
    ones = jnp.ones((16, LANES), BF16)
    dims = (((1,), (1,)), ((), ()))
    ss_ref[...] = (
        lax.dot_general(ones, high, dims, preferred_element_type=F32)
        + lax.dot_general(ones, mid, dims, preferred_element_type=F32)
    )[:TILE]


def chunk_kernel(step, who_ref, xg_ref, ss_ref, w_ref, out_ref, ext_ref):
    part = (who_ref[0] + step) % 4
    at = pl.ds(pl.multiple_of(part * LANES, LANES), LANES)
    rows = xg_ref.shape[0] - RIM
    ext_ref[...] = jnp.zeros_like(ext_ref)
    for g in range(3):
        got = jnp.dot(xg_ref[...], w_ref[g, :, at], preferred_element_type=F32)
        out_ref[g * rows : (g + 1) * rows] = got[:rows].astype(out_ref.dtype)
        ext_ref[2 * g : 2 * g + 2] = got[rows + RIM - 2 :]
    for i in range(3):
        total = ss_ref[0:1, i * LANES : (i + 1) * LANES]
        high = total.astype(BF16).astype(F32)
        ext_ref[6 + i : 7 + i] = high
        ext_ref[9 + i : 10 + i] = total - high
    out_ref[3 * rows :] = ext_ref[...].astype(out_ref.dtype)


def signal_kernel(a_ref, b_ref, c_ref, d_ref, filt_ref, p8_ref, r7_ref, p64_ref, gate_ref, sig_ref, carry_ref, send_ref, ext_ref, u_ref):
    rows = gate_ref.shape[0]

    def summed(lo, n):
        at = pl.ds(lo, n)
        return a_ref[at, :] + (b_ref[at, :].astype(F32) + c_ref[at, :].astype(F32) + d_ref[at, :].astype(F32))

    tail = summed(3 * rows, RIM)
    inverse = [lax.rsqrt((tail[6 + i : 7 + i] + tail[9 + i : 10 + i]) * (1.0 / D) + 1e-6) for i in range(3)]
    columns = [jnp.broadcast_to(v, (LANES, LANES)).T for v in inverse]
    streams = []
    for g in range(3):
        ext_ref[g, 0:TILE] = jnp.zeros((TILE, LANES), F32)
        rim = tail[2 * g : 2 * g + 2] * columns[2][RIM - 2 : RIM]
        ext_ref[g, TILE - 2 : TILE] = rim.astype(BF16).astype(F32)
        for i in range(rows // LANES):
            value = summed(g * rows + i * LANES, LANES) * columns[i]
            ext_ref[g, pl.ds(TILE + i * LANES, LANES), :] = value.astype(BF16).astype(F32)
        taps = [filt_ref[3 * g + j : 3 * g + j + 1] for j in range(3)]
        streams.append(
            taps[0] * ext_ref[g, pl.ds(TILE, rows), :]
            + taps[1] * ext_ref[g, pl.ds(TILE - 1, rows), :]
            + taps[2] * ext_ref[g, pl.ds(TILE - 2, rows), :]
        )
        if g == 0:
            gate_ref[...] = streams[0]
    sig_ref[...] = streams[1] * streams[2]
    for q in range(rows // SUB):
        tiles = [sig_ref[pl.ds(q * SUB + TILE * k, TILE), :] for k in range(STEPS)]
        for m in range(MODES):
            real = tiles[STEPS - 1]
            imag = jnp.zeros_like(real)
            for k in range(STEPS - 1):
                real = real + p8_ref[STEPS - 1 - k, 0, m : m + 1, :] * tiles[k]
                imag = imag + p8_ref[STEPS - 1 - k, 1, m : m + 1, :] * tiles[k]
            real, imag = cmul((real, imag), (r7_ref[m, 0], r7_ref[m, 1]))
            u_ref[q, 0, m : m + 1, :] = jnp.sum(real, axis=0, keepdims=True)
            u_ref[q, 1, m : m + 1, :] = jnp.sum(imag, axis=0, keepdims=True)
    state = (jnp.zeros((MODES, LANES), F32),) * 2
    step = (p64_ref[1, 0], p64_ref[1, 1])
    for q in range(rows // SUB):
        for c in range(2):
            carry_ref[q, c] = state[c]
        state = cmul(state, step)
        state = (state[0] + u_ref[q, 0], state[1] + u_ref[q, 1])
    for i in range(LOW):
        for c in range(2):
            send_ref[i, c] = state[c].astype(send_ref.dtype)


def weighted(got_ref, table_ref, first, sign):
    real = jnp.zeros((MODES, LANES), F32)
    imag = jnp.zeros((MODES, LANES), F32)
    for i in range(LOW):
        value = (got_ref[i, 0].astype(F32), got_ref[i, 1].astype(F32))
        term = cmul(value, (table_ref[first - i, 0], table_ref[first - i, 1]))
        real, imag = real + term[0], imag + term[1]
    return real, imag


def low_kernel(who_ref, got_ref, low_ref, mine_ref, send_ref):
    mine = weighted(got_ref, low_ref, LOW - 1 + who_ref[1], 1)
    every = weighted(got_ref, low_ref, 2 * LOW - 1, 1)
    for c in range(2):
        mine_ref[c] = mine[c]
        for i in range(LOW):
            send_ref[i, c] = every[c].astype(send_ref.dtype)


def local_kernel(gate_ref, sig_ref, skip_ref, h_ref, out_ref, pad_ref):
    rows = sig_ref.shape[0]
    pad_ref[0:TILE] = jnp.zeros((TILE, LANES), F32)
    for q in range(rows // SUB):
        pad_ref[TILE:] = sig_ref[pl.ds(q * SUB, SUB), :]
        sums = [skip_ref[...] * pad_ref[pl.ds(TILE + TILE * i, TILE), :] for i in range(STEPS)]
        for b in range(TILE):
            moved = [pad_ref[pl.ds(TILE + TILE * i - b, TILE), :] for i in range(STEPS)]
            for a in range(STEPS):
                tap = h_ref[TILE * a + b : TILE * a + b + 1, :]
                for i in range(a, STEPS):
                    sums[i] = sums[i] + tap * moved[i - a]
        for i in range(STEPS):
            at = pl.ds(q * SUB + TILE * i, TILE)
            out_ref[at, :] = gate_ref[at, :] * sums[i]


def final_kernel(who_ref, got_ref, high_ref, low_ref, mine_ref, carry_ref, p64_ref, p8_ref, gt_ref, gate_ref, local_ref, out_ref, e_ref, y_ref):
    rows = gate_ref.shape[0]
    far = weighted(got_ref, high_ref, LOW - 1 + who_ref[2], 1)
    lag = LOW + who_ref[1]
    far = cmul(far, (low_ref[lag, 0], low_ref[lag, 1]))
    enter = (mine_ref[0] + far[0], mine_ref[1] + far[1])
    for q in range(rows // SUB):
        moved = cmul(enter, (p64_ref[q, 0], p64_ref[q, 1])) if q else enter
        for c in range(2):
            e_ref[c] = moved[c] + carry_ref[q, c]
        sums = [jnp.zeros((TILE, LANES), F32) for _ in range(STEPS)]
        for m in range(MODES):
            real, imag = cmul((gt_ref[m, 0], gt_ref[m, 1]), (e_ref[0, m : m + 1, :], e_ref[1, m : m + 1, :]))
            sums[0] = sums[0] + real
            for k in range(1, STEPS):
                sums[k] = sums[k] + (p8_ref[k, 0, m : m + 1, :] * real - p8_ref[k, 1, m : m + 1, :] * imag)
        for k in range(STEPS):
            at = pl.ds(q * SUB + TILE * k, TILE)
            y_ref[at, :] = local_ref[at, :] + gate_ref[at, :] * sums[k]
    out_ref[...] = y_ref[...].T.astype(BF16)


def body(tokens, norm_gain, in_weight, short_filter, decay_reach, mode_freq, residues, skip_gain):
    rows, cols = tokens.shape
    me = lax.axis_index("fsdp").astype(jnp.int32)
    block = lax.axis_index("seq").astype(jnp.int32)
    who = jnp.stack([me, block % LOW, block // LOW])
    count = lax.axis_size("seq")
    fsdp = lax.axis_size("fsdp")

    rim = lax.ppermute(tokens[rows - RIM :], "seq", [(i, i + 1) for i in range(count - 1)])
    xg, ss = call(
        prepare_kernel,
        (shape(rows + RIM, cols, dtype=BF16), shape(TILE, 3 * LANES)),
        [VMEM] * 3,
        [pltpu.VMEM((3 * LANES, LANES), F32)],
    )(tokens, rim, norm_gain[None])
    weight = jnp.transpose(in_weight, (1, 0, 2))

    def chunk(step, dtype):
        return call(
            functools.partial(chunk_kernel, step),
            shape(3 * rows + RIM, LANES, dtype=dtype),
            [SMEM] + [VMEM] * 3,
            [pltpu.VMEM((RIM, LANES), F32)],
        )(who, xg, ss, weight)

    arrived = []
    for step in (2, 1, 3):
        pairs = [(i, (i + step) % fsdp) for i in range(fsdp)]
        arrived.append(lax.ppermute(chunk(step, BF16), "fsdp", pairs))
    own = chunk(0, F32)
    p8, r7, gt, p64, low, high, taps = tables(decay_reach.T, mode_freq.T, residues.T)
    filt = jnp.transpose(short_filter, (1, 2, 0)).reshape(9, LANES)
    gate, signal, carry, send = call(
        signal_kernel,
        (shape(rows, LANES), shape(rows, LANES), shape(4, 2, MODES, LANES), shape(LOW, 2, MODES, LANES, dtype=BF16)),
        [VMEM] * 8,
        [pltpu.VMEM((3, TILE + rows, LANES), F32), pltpu.VMEM((4, 2, MODES, LANES), F32)],
    )(own, *arrived, filt, p8, r7, p64)

    near = [[LOW * g + j for j in range(LOW)] for g in range(count // LOW)]
    got = lax.all_to_all(send, "seq", 0, 0, axis_index_groups=near)
    mine, send = call(
        low_kernel,
        (shape(2, MODES, LANES), shape(LOW, 2, MODES, LANES, dtype=BF16)),
        [SMEM] + [VMEM] * 2,
    )(who, got, low)
    local = call(local_kernel, shape(rows, LANES), [VMEM] * 4, [pltpu.VMEM((TILE + SUB, LANES), F32)])(
        gate, signal, skip_gain[None], taps
    )
    far = [[g + LOW * j for j in range(count // LOW)] for g in range(LOW)]
    got = lax.all_to_all(send, "seq", 0, 0, axis_index_groups=far)
    return call(
        final_kernel,
        shape(LANES, rows, dtype=BF16),
        [SMEM] + [VMEM] * 10,
        [pltpu.VMEM((2, MODES, LANES), F32), pltpu.VMEM((rows, LANES), F32)],
    )(who, got, high, low, mine, carry, p64, p8, gt, gate, local)


def solution(mesh):
    placed = (
        P("seq", "fsdp"),
        P("fsdp"),
        P("fsdp", None, None),
        P("fsdp", None, None),
        P("fsdp", None),
        P("fsdp", None),
        P("fsdp", None),
        P("fsdp"),
    )
    return jax.shard_map(
        body, mesh=mesh, in_specs=placed, out_specs=P("fsdp", "seq"), check_vma=False
    )
```

time: 261 us -> 60.5 us (0.23)
  the two profiles are of different devices: /device:TPU:8 before, /device:TPU:1 now
where the time goes in v1:
time: 60.5 us; the launch traced here: 60.1 us
  starting transfers between devices  16.7 us (28%)
  waiting for transfers between devices  12.8 us (21%)
  Pallas kernels  11.3 us (19%)
  blocking collectives  10.7 us (18%)
  local copies, waits for them, and re-layouts  8.4 us (14%)
    all_to_all x1, blocking collectives, body(): got = lax.all_to_all(send, 'seq', 0, 0, axis_index_groups=near)  10.7 us
    all_to_all x1, starting transfers between devices, body(): got = lax.all_to_all(send, 'seq', 0, 0, axis_index_groups=far)  7.81 us
    unnamed x18, local copies, waits for them, and re-layouts  7.55 us
    all_to_all x1, waiting for transfers between devices, body(): got = lax.all_to_all(send, 'seq', 0, 0, axis_index_groups=far)  6.88 us
    pallas_call x4, Pallas kernels, chunk(): call(functools.partial(chunk_kernel, step), shape(3 * rows + RIM, LANES,...  6.38 us
    ppermute x3, waiting for transfers between devices, body(): arrived.append(lax.ppermute(chunk(step, BF16), 'fsdp', pairs))  4.71 us
    ppermute x1, starting transfers between devices, body(): lax.ppermute(tokens[rows - RIM:], 'seq', [(i, i + 1) for i in range(count...  4.5 us
    ppermute x3, starting transfers between devices, body(): arrived.append(lax.ppermute(chunk(step, BF16), 'fsdp', pairs))  4.42 us
  transfers between devices with their start and end apart: 5, of which 3 were waited for; matrix products, arithmetic and copies ran while one was open for 0% of the time, Pallas kernels for 4%

profile of v1, /device:TPU:1, one launch (start us, length us, event | category | flops | bytes accessed | tf_op | source)
XLA Modules:
  0.0 60.1 jit_solution(10813634441738284767)
XLA Ops:
  0.0 0.8 %slice.3 = bf16[16,2048]{1,0:T(8,128)(2,1)S(1)} slice(bf16[256,2048]{1,0:T(8,128)(2,1)} %tok_ref.1), slice={[240:256], [0:2048]} | slice | bytes 131072 | tf_op jit(solution)/shard_map/slice | solution.py:272
  0.8 4.5 %collective-permute-start = (bf16[16,2048]{1,0:T(8,128)(2,1)S(1)}, bf16[16,2048]{1,0:T(8,128)(2,1)S(1)}, u32[]{:S(2)}, u32[]{:S(2)}) collective-permute-start(bf16[16,2048]{1,0:T(8,128)(2,1)S(1)} %slice.3), channel_id=1, source_target_pairs={{0,1},{1,2},{2,3},{3,4},{4,5},{5,6},{6,7},{7,8},{8,9},{9,10},{10,1... | collective-permute-start | bytes 196616 | tf_op jit(solution)/shard_map/ppermute | solution.py:272
  5.4 0.1 pad_add_fusion.who_ref
  5.4 1.2 %collective-permute-done.rim_ref = bf16[16,2048]{1,0:T(8,128)(2,1)S(1)} collective-permute-done((bf16[16,2048]{1,0:T(8,128)(2,1)S(1)}, bf16[16,2048]{1,0:T(8,128)(2,1)S(1)}, u32[]{:S(2)}, u32[]{:S(2)}) %collective-permute-start) | collective-permute-done | bytes 65568 | tf_op jit(solution)/shard_map/ppermute | solution.py:272
  6.7 1.2 %copy-done.2 = bf16[256,2048]{1,0:T(8,128)(2,1)S(1)} copy-done((bf16[256,2048]{1,0:T(8,128)(2,1)S(1)}, bf16[256,2048]{1,0:T(8,128)(2,1)}, u32[]{:S(2)}) %copy-start.2) | copy-done | bytes 1048600
  7.9 0.7 %copy-done.3 = f32[2048]{0:T(1024)S(1)} copy-done((f32[2048]{0:T(1024)S(1)}, f32[2048]{0:T(1024)}, u32[]{:S(2)}) %copy-start.3) | copy-done | bytes 8216
  8.6 0.5 shard_map.82
  9.1 2.8 %copy-done = bf16[2048,3,512]{2,0,1:T(8,128)(2,1)S(1)} copy-done((bf16[2048,3,512]{2,0,1:T(8,128)(2,1)S(1)}, bf16[2048,3,512]{2,0,1:T(8,128)(2,1)}, u32[]{:S(2)}) %copy-start) | copy-done | bytes 6291480
  11.9 1.6 %shard_map.86 = bf16[784,128]{1,0:T(8,128)(2,1)S(1)} custom-call(s32[3]{0:T(128)S(1)} %pad_add_fusion.who_ref, bf16[272,2048]{1,0:T(8,128)(2,1)S(1)} %get-tuple-element.20.xg_ref, f32[8,384]{1,0:T(8,128)S(1)} %get-tuple-element.21.ss_ref, bf16[3,2048,512]{2,1,0:T(8,128)(2,1)S(1)} %bitcast.10), custom_call_target="tpu_custom_call" | custom-call | tf_op jit(solution)/shard_map/pallas_call | solution.py:282
  13.5 0.0 copy-start.8
  13.5 0.0 copy-start.4
  13.5 0.0 copy-start.5
  13.6 0.0 copy-start.6
  13.6 1.6 %shard_map.85 = bf16[784,128]{1,0:T(8,128)(2,1)S(1)} custom-call(s32[3]{0:T(128)S(1)} %pad_add_fusion.who_ref, bf16[272,2048]{1,0:T(8,128)(2,1)S(1)} %get-tuple-element.20.xg_ref, f32[8,384]{1,0:T(8,128)S(1)} %get-tuple-element.21.ss_ref, bf16[3,2048,512]{2,1,0:T(8,128)(2,1)S(1)} %bitcast.11), custom_call_target="tpu_custom_call" | custom-call | tf_op jit(solution)/shard_map/pallas_call | solution.py:282
  15.2 1.6 %shard_map.84 = bf16[784,128]{1,0:T(8,128)(2,1)S(1)} custom-call(s32[3]{0:T(128)S(1)} %pad_add_fusion.who_ref, bf16[272,2048]{1,0:T(8,128)(2,1)S(1)} %get-tuple-element.20.xg_ref, f32[8,384]{1,0:T(8,128)S(1)} %get-tuple-element.21.ss_ref, bf16[3,2048,512]{2,1,0:T(8,128)(2,1)S(1)} %bitcast.12), custom_call_target="tpu_custom_call" | custom-call | tf_op jit(solution)/shard_map/pallas_call | solution.py:282
  16.8 0.0 copy-start.7
  16.8 2.8 %collective-permute-start.3 = (bf16[784,128]{1,0:T(8,128)(2,1)S(1)}, bf16[784,128]{1,0:T(8,128)(2,1)S(1)}, u32[]{:S(2)}, u32[]{:S(2)}) collective-permute-start(bf16[784,128]{1,0:T(8,128)(2,1)S(1)} %shard_map.86), channel_id=1, source_target_pairs={{0,192},{64,0},{128,64},{192,128},{1,193},{65,1},{129,65},{193,129... | collective-permute-start | bytes 602120 | tf_op jit(solution)/shard_map/ppermute | solution.py:292
  19.6 0.0 collective-permute-start.2
  19.6 1.6 %collective-permute-start.1 = (bf16[784,128]{1,0:T(8,128)(2,1)S(1)}, bf16[784,128]{1,0:T(8,128)(2,1)S(1)}, u32[]{:S(2)}, u32[]{:S(2)}) collective-permute-start(bf16[784,128]{1,0:T(8,128)(2,1)S(1)} %shard_map.84), channel_id=1, source_target_pairs={{0,128},{64,192},{128,0},{192,64},{1,129},{65,193},{129,1},{193,65... | collective-permute-start | bytes 602120 | tf_op jit(solution)/shard_map/ppermute | solution.py:292
  21.2 0.5 shard_map.87
  21.8 0.0 copy-start.1
  21.8 2.8 %copy-done.1 = bf16[2048,3,512]{2,0,1:T(8,128)(2,1)S(1)} copy-done((bf16[2048,3,512]{2,0,1:T(8,128)(2,1)S(1)}, bf16[2048,3,512]{2,0,1:T(8,128)(2,1)}, u32[]{:S(2)}) %copy-start.1) | copy-done | bytes 6291480
  24.5 1.6 %shard_map.83.a_ref = f32[784,128]{1,0:T(8,128)S(1)} custom-call(s32[3]{0:T(128)S(1)} %pad_add_fusion.who_ref, bf16[272,2048]{1,0:T(8,128)(2,1)S(1)} %get-tuple-element.20.xg_ref, f32[8,384]{1,0:T(8,128)S(1)} %get-tuple-element.21.ss_ref, bf16[3,2048,512]{2,1,0:T(8,128)(2,1)S(1)} %bitcast.13), custom_call_target="tpu_custom_call" | custom-call | tf_op jit(solution)/shard_map/pallas_call | solution.py:282
  26.1 4.7 %collective-permute-done.2.c_ref = bf16[784,128]{1,0:T(8,128)(2,1)S(1)} collective-permute-done((bf16[784,128]{1,0:T(8,128)(2,1)S(1)}, bf16[784,128]{1,0:T(8,128)(2,1)S(1)}, u32[]{:S(2)}, u32[]{:S(2)}) %collective-permute-start.2) | collective-permute-done | bytes 200736 | tf_op jit(solution)/shard_map/ppermute | solution.py:292
  30.8 0.0 collective-permute-done.1.b_ref
  30.8 0.7 %shard_map.88 = (f32[256,128]{1,0:T(8,128)S(1)}, f32[256,128]{1,0:T(8,128)S(1)}, f32[4,2,16,128]{3,2,1,0:T(8,128)S(1)}, bf16[8,2,16,128]{3,2,1,0:T(8,128)(2,1)S(1)}) custom-call(f32[784,128]{1,0:T(8,128)S(1)} %shard_map.83.a_ref, bf16[784,128]{1,0:T(8,128)(2,1)S(1)} %collective-permute-done.1.b_ref, bf16[784,128]{1,0:T(8,128)(2,1)S(1)} %collective-permute-done.2.c_ref, ...), custom_call_target="tpu_custom_call" | custom-call | tf_op jit(solution)/shard_map/pallas_call | solution.py:296
  31.5 10.7 %all_to_all.10.got_ref = bf16[8,2,16,128]{3,2,1,0:T(8,128)(2,1)S(1)} all-to-all(bf16[8,2,16,128]{3,2,1,0:T(8,128)(2,1)S(1)} %get-tuple-element.25), channel_id=1, replica_groups={{0,1,2,3,4,5,6,7},{8,9,10,11,12,13,14,15},{16,17,18,19,20,21,22,23},{24..., dimensions={0} | all-to-all | bytes 131072 | tf_op jit(solution)/shard_map/all_to_all | solution.py:304
  42.2 1.2 %shard_map.89 = (f32[2,16,128]{2,1,0:T(8,128)S(1)}, bf16[8,2,16,128]{3,2,1,0:T(8,128)(2,1)}) custom-call(s32[3]{0:T(128)S(1)} %pad_add_fusion.who_ref, bf16[8,2,16,128]{3,2,1,0:T(8,128)(2,1)S(1)} %all_to_all.10.got_ref, f32[16,2,16,128]{3,2,1,0:T(8,128)S(1)} %get-tuple-element.26.low_ref), custom_call_target="tpu_custom_call" | custom-call | tf_op jit(solution)/shard_map/pallas_call | solution.py:305
  43.4 7.8 %all-to-all-start.1 = ((bf16[8,2,16,128]{3,2,1,0:T(8,128)(2,1)}), bf16[8,2,16,128]{3,2,1,0:T(8,128)(2,1)S(1)}, u32[]{:S(2)}, u32[]{:S(2)}) async-start(bf16[8,2,16,128]{3,2,1,0:T(8,128)(2,1)} %get-tuple-element.27), calls=%async_computation.1 | async-start | bytes 131072 | tf_op jit(solution)/shard_map/all_to_all | solution.py:314
  51.2 0.3 shard_map.90.local_ref
  51.5 6.9 %all-to-all-done.1.got_ref = bf16[8,2,16,128]{3,2,1,0:T(8,128)(2,1)S(1)} async-done(((bf16[8,2,16,128]{3,2,1,0:T(8,128)(2,1)}), bf16[8,2,16,128]{3,2,1,0:T(8,128)(2,1)S(1)}, u32[]{:S(2)}, u32[]{:S(2)}) %all-to-all-start.1) | async-done | bytes 65568 | tf_op jit(solution)/shard_map/all_to_all | solution.py:314
  58.4 1.7 %shard_map.91 = bf16[128,256]{1,0:T(8,128)(2,1)} custom-call(s32[3]{0:T(128)S(1)} %pad_add_fusion.who_ref, bf16[8,2,16,128]{3,2,1,0:T(8,128)(2,1)S(1)} %all-to-all-done.1.got_ref, f32[16,2,16,128]{3,2,1,0:T(8,128)S(1)} %get-tuple-element.28.high_ref, f32[16,2,16,128]{3,2,1,0:T(8,128)S(1)} %get-tuple-element.26.low_ref, ...), custom_call_target="tpu_custom_call" | custom-call | tf_op jit(solution)/shard_map/pallas_call | solution.py:315
  (10 shorter events, 0.0 us)
Async XLA Ops:
  0.8 5.8 %collective-permute-start = (bf16[16,2048]{1,0:T(8,128)(2,1)S(1)}, bf16[16,2048]{1,0:T(8,128)(2,1)S(1)}, u32[]{:S(2)}, u32[]{:S(2)}) collective-permute-start(bf16[16,2048]{1,0:T(8,128)(2,1)S(1)} %slice.3), channel_id=1, source_target_pairs={{0,1},{1,2},{2,3},{3,4},{4,5},{5,6},{6,7},{7,8},{8,9},{9,10},{10,1... | collective-permute-start | bytes 196616 | tf_op jit(solution)/shard_map/ppermute | solution.py:272
  6.7 1.2 %copy-start.2 = (bf16[256,2048]{1,0:T(8,128)(2,1)S(1)}, bf16[256,2048]{1,0:T(8,128)(2,1)}, u32[]{:S(2)}) copy-start(bf16[256,2048]{1,0:T(8,128)(2,1)} %tok_ref.1) | copy-start | bytes 3145732
  7.9 0.7 %copy-start.3 = (f32[2048]{0:T(1024)S(1)}, f32[2048]{0:T(1024)}, u32[]{:S(2)}) copy-start(f32[2048]{0:T(1024)} %param.9) | copy-start | bytes 24580
  9.1 2.8 %copy-start = (bf16[2048,3,512]{2,0,1:T(8,128)(2,1)S(1)}, bf16[2048,3,512]{2,0,1:T(8,128)(2,1)}, u32[]{:S(2)}) copy-start(bf16[2048,3,512]{2,0,1:T(8,128)(2,1)} %param.10) | copy-start | bytes 18874372
  13.5 7.7 %copy-start.8 = (f32[128,3,3]{0,2,1:T(4,128)S(1)}, f32[128,3,3]{0,2,1:T(4,128)}, u32[]{:S(2)}) copy-start(f32[128,3,3]{0,2,1:T(4,128)} %param.11) | copy-start | bytes 13828
  13.5 7.7 %copy-start.4 = (f32[128,16]{0,1:T(8,128)S(1)}, f32[128,16]{0,1:T(8,128)}, u32[]{:S(2)}) copy-start(f32[128,16]{0,1:T(8,128)} %param.12) | copy-start | bytes 24580
  13.5 7.7 %copy-start.5 = (f32[128,16]{0,1:T(8,128)S(1)}, f32[128,16]{0,1:T(8,128)}, u32[]{:S(2)}) copy-start(f32[128,16]{0,1:T(8,128)} %param.13) | copy-start | bytes 24580
  13.6 7.7 %copy-start.6 = (f32[128,16]{0,1:T(8,128)S(1)}, f32[128,16]{0,1:T(8,128)}, u32[]{:S(2)}) copy-start(f32[128,16]{0,1:T(8,128)} %param.14) | copy-start | bytes 24580
  16.8 34.4 %copy-start.7 = (f32[128]{0:T(128)S(1)}, f32[128]{0:T(128)}, u32[]{:S(2)}) copy-start(f32[128]{0:T(128)} %param.15) | copy-start | bytes 1540
  16.8 9.3 %collective-permute-start.3 = (bf16[784,128]{1,0:T(8,128)(2,1)S(1)}, bf16[784,128]{1,0:T(8,128)(2,1)S(1)}, u32[]{:S(2)}, u32[]{:S(2)}) collective-permute-start(bf16[784,128]{1,0:T(8,128)(2,1)S(1)} %shard_map.86), channel_id=1, source_target_pairs={{0,192},{64,0},{128,64},{192,128},{1,193},{65,1},{129,65},{193,129... | collective-permute-start | bytes 602120 | tf_op jit(solution)/shard_map/ppermute | solution.py:292
  19.6 11.3 %collective-permute-start.2 = (bf16[784,128]{1,0:T(8,128)(2,1)S(1)}, bf16[784,128]{1,0:T(8,128)(2,1)S(1)}, u32[]{:S(2)}, u32[]{:S(2)}) collective-permute-start(bf16[784,128]{1,0:T(8,128)(2,1)S(1)} %shard_map.85), channel_id=1, source_target_pairs={{0,64},{64,128},{128,192},{192,0},{1,65},{65,129},{129,193},{193,1... | collective-permute-start | bytes 602120 | tf_op jit(solution)/shard_map/ppermute | solution.py:292
  19.6 11.3 %collective-permute-start.1 = (bf16[784,128]{1,0:T(8,128)(2,1)S(1)}, bf16[784,128]{1,0:T(8,128)(2,1)S(1)}, u32[]{:S(2)}, u32[]{:S(2)}) collective-permute-start(bf16[784,128]{1,0:T(8,128)(2,1)S(1)} %shard_map.84), channel_id=1, source_target_pairs={{0,128},{64,192},{128,0},{192,64},{1,129},{65,193},{129,1},{193,65... | collective-permute-start | bytes 602120 | tf_op jit(solution)/shard_map/ppermute | solution.py:292
  21.8 2.8 %copy-start.1 = (bf16[2048,3,512]{2,0,1:T(8,128)(2,1)S(1)}, bf16[2048,3,512]{2,0,1:T(8,128)(2,1)}, u32[]{:S(2)}) copy-start(bf16[2048,3,512]{2,0,1:T(8,128)(2,1)} %param.10) | copy-start | bytes 18874372
  43.4 15.0 %all-to-all-start.1 = ((bf16[8,2,16,128]{3,2,1,0:T(8,128)(2,1)}), bf16[8,2,16,128]{3,2,1,0:T(8,128)(2,1)S(1)}, u32[]{:S(2)}, u32[]{:S(2)}) async-start(bf16[8,2,16,128]{3,2,1,0:T(8,128)(2,1)} %get-tuple-element.27), calls=%async_computation.1 | async-start | bytes 131072 | tf_op jit(solution)/shard_map/all_to_all | solution.py:314

commit v2 on v1

v2 whole, which is shorter than its diff:
```python
import math

import jax
import jax.numpy as jnp
from jax import lax
from jax.experimental import pallas as pl
from jax.experimental.pallas import tpu as pltpu
from jax.sharding import PartitionSpec as P

F32 = jnp.float32
BF16 = jnp.bfloat16
D = 8192
MODES = 16
LANES = 128
TILE = 8
SUB = 64
STEPS = SUB // TILE
LOW = 8
PLANES = 8
HEAD = 2 * MODES
TAIL = HEAD + 4
EXTRA = 16
WIRE = 48
VMEM = pl.BlockSpec(memory_space=pltpu.VMEM)
HBM = pl.BlockSpec(memory_space=pltpu.HBM)


def call(kernel, out_shape, operands, scratch=(), limit=16 << 20, flops=0, places=None):
    moved = sum(math.prod(v.shape) * v.dtype.itemsize for v in (*operands, *jax.tree.leaves(out_shape)))
    return pl.pallas_call(
        kernel,
        out_shape=out_shape,
        in_specs=places or [VMEM] * len(operands),
        out_specs=jax.tree.map(lambda _: VMEM, out_shape),
        scratch_shapes=list(scratch),
        compiler_params=pltpu.CompilerParams(vmem_limit_bytes=limit),
        cost_estimate=pl.CostEstimate(flops=flops, bytes_accessed=moved, transcendentals=0),
    )(*operands)


def shape(*dims, dtype=F32):
    return jax.ShapeDtypeStruct(dims, dtype)


def cmul(a, b):
    return a[0] * b[0] - a[1] * b[1], a[0] * b[1] + a[1] * b[0]


def turn(angle):
    cycles = jnp.floor(angle * (0.5 / math.pi) + 0.5)
    rest = angle - cycles * 6.28125
    rest = rest - cycles * 1.93500518798828125e-3
    rest = rest - cycles * 3.0199159819e-7
    return jnp.cos(rest), jnp.sin(rest)


def table_kernel(
    reach_ref, freq_ref, res_ref, p8_ref, r7_ref, gt_ref, p64_ref, mine_ref, all_ref, far_ref, plane_ref, h_ref, before_ref, power_ref
):
    rate = 1.0 / reach_ref[...]
    freq = freq_ref[...]
    gain = res_ref[...] * jnp.sqrt(2.0 * rate)
    block = lax.axis_index("seq")
    place = lax.rem(block, LOW)
    plane = lax.div(block, LOW)

    def power(n):
        size = jnp.exp(-rate * n)
        cosine, sine = turn(freq * n)
        return size * cosine, size * sine

    one = (jnp.ones_like(rate), jnp.zeros_like(rate))

    def chain(base, count):
        values = [one]
        for _ in range(count - 1):
            values.append(cmul(values[-1], base))
        return values

    ones = chain(power(1.0), TILE + 1)
    for j in range(TILE):
        for c in range(2):
            r7_ref[:, c, j, :] = ones[TILE - 1 - j][c]
            gt_ref[:, c, j, :] = gain * ones[j + 1][c]
    eights = chain(power(8.0), STEPS)
    for k in range(STEPS):
        for c in range(2):
            p8_ref[k, c] = eights[k][c]
    for q, value in enumerate(chain(power(float(SUB)), 4)):
        for c in range(2):
            p64_ref[q, c] = value[c]
    blocks = chain(power(256.0), LOW)
    for k, value in enumerate(blocks):
        for c in range(2):
            power_ref[k, c] = jnp.zeros_like(rate)
            power_ref[LOW + k, c] = value[c]
    for i in range(LOW):
        for c in range(2):
            mine_ref[i, c] = power_ref[LOW - 1 - i + place, c]
            all_ref[i, c] = blocks[LOW - 1 - i][c]
    unit, far = power(1.0), power(2048.0)
    size = jnp.exp(2.0 * rate)
    back = (size * unit[0], -size * unit[1])
    twice = cmul(back, back)
    last = cmul(blocks[1], back)
    earlier = cmul(last, back)
    rows = (
        (power_ref[LOW + place, 0], power_ref[LOW + place, 1]),
        (power_ref[LOW - 1 + place, 0], power_ref[LOW - 1 + place, 1]),
        far,
        last,
        earlier,
        cmul(last, blocks[LOW - 1]),
        cmul(earlier, blocks[LOW - 1]),
        back,
        twice,
    )
    for i, value in enumerate(rows):
        for c in range(2):
            plane_ref[i, c] = value[c]
    for k, value in enumerate(chain(far, PLANES)):
        for c in range(2):
            power_ref[LOW + k, c] = value[c]
    for i in range(PLANES):
        for c in range(2):
            far_ref[i, c] = power_ref[LOW - 1 - i + plane, c]
    before_ref[...] = jnp.sum(gain * back[0], axis=0, keepdims=True)
    taps = [jnp.zeros((TILE, LANES), F32) for _ in range(STEPS)]
    row = lax.broadcasted_iota(jnp.int32, (TILE, LANES), 0)
    for m in range(MODES):
        real = jnp.where(row == 0, gain[m : m + 1], pltpu.roll(gt_ref[m, 0], 1, 0))
        imag = jnp.where(row == 0, 0.0, pltpu.roll(gt_ref[m, 1], 1, 0))
        for k in range(STEPS):
            taps[k] = taps[k] + (eights[k][0][m : m + 1] * real - eights[k][1][m : m + 1] * imag)
    for k in range(STEPS):
        h_ref[TILE * k : TILE * k + TILE] = taps[k]


def project_kernel(
    tok_hbm, gain_hbm, w_hbm, two_ref, one_ref, three_ref, own_ref,
    tok_ref, gain_ref, w_ref, xg_ref, acc_ref, ext_ref, got_ref, sems, w_sems,
):
    rows, cols = tok_ref.shape
    outs = {2: two_ref, 1: one_ref, 3: three_ref, 0: own_ref}
    pieces = 4
    span = rows // pieces
    gain_copy = pltpu.make_async_copy(gain_hbm, gain_ref, sems.at[0])
    gain_copy.start()
    tok_copies = []
    for i in range(pieces):
        at = pl.ds(i * span, span)
        tok_copies.append(pltpu.make_async_copy(tok_hbm.at[at], tok_ref.at[at], sems.at[1 + i]))
        tok_copies[-1].start(priority=i % 2)
    w_copies = [pltpu.make_async_copy(w_hbm.at[g], w_ref.at[g], w_sems.at[g]) for g in range(3)]
    w_copies[0].start(priority=0)
    w_copies[1].start(priority=1)
    gain_copy.wait()
    gain = gain_ref[...]
    for i in range(pieces):
        tok_copies[i].wait()
        if i == 1:
            w_copies[2].start(priority=0)
        for lo in range(i * span, (i + 1) * span, 32):
            x = tok_ref[pl.ds(lo, 32), :].astype(F32)
            xg_ref[pl.ds(lo, 32), :] = (x * gain).astype(BF16)
            sq = x * x
            acc_ref[pl.ds(lo, 32), :] = sum(sq[:, j : j + LANES] for j in range(0, cols, LANES))
    acc = acc_ref[...]
    high = acc.astype(BF16)
    mid = (acc - high.astype(F32)).astype(BF16)
    ones = jnp.ones((16, LANES), BF16)
    dims = (((1,), (1,)), ((), ()))
    total = (
        lax.dot_general(ones, high, dims, preferred_element_type=F32)
        + lax.dot_general(ones, mid, dims, preferred_element_type=F32)
    )[:1]
    ext_ref[...] = jnp.zeros_like(ext_ref)
    for i in range(rows // LANES):
        value = total[:, i * LANES : (i + 1) * LANES]
        high = value.astype(BF16).astype(F32)
        ext_ref[i : i + 1] = high
        ext_ref[2 + i : 3 + i] = value - high
    for out in outs.values():
        out[3 * rows :] = ext_ref[...].astype(out.dtype)
    me = lax.axis_index("fsdp")
    for g in range(3):
        w_copies[g].wait()
        got_ref[...] = jnp.dot(xg_ref[...], w_ref[g], preferred_element_type=F32)
        for d, out in outs.items():
            at = pl.ds(pl.multiple_of(lax.rem(me + d, 4) * LANES, LANES), LANES)
            out[g * rows : (g + 1) * rows] = got_ref[:, at].astype(out.dtype)


def local(sig_ref, skip_ref, h_ref, out_ref, pad_ref):
    pad_ref[0:TILE] = jnp.zeros((TILE, LANES), F32)
    for q in range(sig_ref.shape[0] // SUB):
        pad_ref[TILE:] = sig_ref[pl.ds(q * SUB, SUB), :]
        sums = [skip_ref[...] * pad_ref[pl.ds(TILE + TILE * i, TILE), :] for i in range(STEPS)]
        for b in range(TILE):
            moved = [pad_ref[pl.ds(TILE + TILE * i - b, TILE), :] for i in range(STEPS)]
            for a in range(STEPS):
                tap = h_ref[TILE * a + b : TILE * a + b + 1, :]
                for i in range(a, STEPS):
                    sums[i] = sums[i] + tap * moved[i - a]
        for i in range(STEPS):
            out_ref[pl.ds(q * SUB + TILE * i, TILE), :] = sums[i]


def signal_kernel(
    a_ref, b_ref, c_ref, d_ref, filt_ref, p8_ref, r7_ref, p64_ref, skip_ref, h_ref,
    gate_ref, local_ref, carry_ref, send_ref, head_ref, ext_ref, u_ref, wire_ref, sig_ref, pad_ref,
):
    rows = gate_ref.shape[0]
    subs = rows // SUB

    def summed(lo, n):
        at = pl.ds(lo, n)
        return a_ref[at, :] + (b_ref[at, :].astype(F32) + c_ref[at, :].astype(F32) + d_ref[at, :].astype(F32))

    tail = summed(3 * rows, EXTRA)
    inverse = [lax.rsqrt((tail[i : i + 1] + tail[2 + i : 3 + i]) * (1.0 / D) + 1e-6) for i in range(rows // LANES)]
    columns = [jnp.broadcast_to(v, (LANES, LANES)).T for v in inverse]
    streams = []
    for g in range(3):
        ext_ref[g, 0:TILE] = jnp.zeros((TILE, LANES), F32)
        for i in range(rows // LANES):
            value = summed(g * rows + i * LANES, LANES) * columns[i]
            ext_ref[g, pl.ds(TILE + i * LANES, LANES), :] = value.astype(BF16).astype(F32)
        taps = [filt_ref[3 * g + j : 3 * g + j + 1] for j in range(3)]
        streams.append(
            taps[0] * ext_ref[g, pl.ds(TILE, rows), :]
            + taps[1] * ext_ref[g, pl.ds(TILE - 1, rows), :]
            + taps[2] * ext_ref[g, pl.ds(TILE - 2, rows), :]
        )
        if g == 0:
            gate_ref[...] = streams[0]
    for g in range(3):
        head_ref[2 * g : 2 * g + 2] = streams[g][:2]
    head_ref[6:] = jnp.zeros((2, LANES), F32)
    signal = streams[1] * streams[2]
    row = lax.broadcasted_iota(jnp.int32, (rows, LANES), 0)
    sig_ref[...] = jnp.where(row < 2, 0.0, signal)
    wire_ref[HEAD:] = jnp.zeros((WIRE - HEAD, LANES), F32)
    for i, (g, at) in enumerate(((1, 0), (2, 0), (1, rows - 2), (2, rows - 2), (0, rows - 2))):
        wire_ref[HEAD + 2 * i : HEAD + 2 * i + 2] = ext_ref[g, TILE + at : TILE + at + 2]
    tiles = [[sig_ref[pl.ds(q * SUB + TILE * k, TILE), :] for k in range(STEPS)] for q in range(subs)]
    for m in range(MODES):
        real = [tiles[q][STEPS - 1] for q in range(subs)]
        imag = [None] * subs
        for k in range(STEPS - 1):
            by = [p8_ref[STEPS - 1 - k, c, m : m + 1, :] for c in range(2)]
            for q in range(subs):
                real[q] = real[q] + by[0] * tiles[q][k]
                term = by[1] * tiles[q][k]
                imag[q] = term if k == 0 else imag[q] + term
        for q in range(subs):
            turned = cmul((real[q], imag[q]), (r7_ref[m, 0], r7_ref[m, 1]))
            for c in range(2):
                u_ref[q, c, m : m + 1, :] = jnp.sum(turned[c], axis=0, keepdims=True)
    state = (jnp.zeros((MODES, LANES), F32),) * 2
    step = (p64_ref[1, 0], p64_ref[1, 1])
    for q in range(subs):
        for c in range(2):
            carry_ref[q, c] = state[c]
        state = cmul(state, step)
        state = (state[0] + u_ref[q, 0], state[1] + u_ref[q, 1])
    for c in range(2):
        wire_ref[MODES * c : MODES * (c + 1)] = state[c]
    wire = wire_ref[...].astype(send_ref.dtype)
    for i in range(LOW):
        send_ref[i] = wire
    local(sig_ref, skip_ref, h_ref, local_ref, pad_ref)


def edges(filt_ref, first, rim):
    def stream(g, own, old):
        taps = [filt_ref[3 * g + j : 3 * g + j + 1] for j in range(3)]
        return (
            taps[0] * own[0] + taps[1] * old[1] + taps[2] * old[0],
            taps[0] * own[1] + taps[1] * own[0] + taps[2] * old[1],
        )

    keys = stream(1, first[:2], rim[:2])
    values = stream(2, first[2:], rim[2:4])
    return keys[0] * values[0], keys[1] * values[1]


def lines(ref, at, count):
    return [ref[at + i : at + i + 1] for i in range(count)]


def impulses(plane_ref, at, pair):
    return [plane_ref[at, c] * pair[0] + plane_ref[at + 1, c] * pair[1] for c in range(2)]


def gathered(got_ref, wide_ref, plane_ref, at, filt_ref, tables, alone):
    zero = jnp.zeros((MODES, LANES), F32)
    sums = [[zero, zero] for _ in tables]
    for i in range(got_ref.shape[0]):
        wide_ref[i] = got_ref[i].astype(F32)
        value = [wide_ref[i, 0:MODES], wide_ref[i, MODES:HEAD]]
        if i or alone:
            rim = lines(wide_ref.at[i - 1], TAIL, 4) if i else [0.0] * 4
            extra = impulses(plane_ref, at, edges(filt_ref, lines(wide_ref.at[i], HEAD, 4), rim))
            value = [value[0] + extra[0], value[1] + extra[1]]
        for total, table_ref in zip(sums, tables):
            term = cmul(value, (table_ref[i, 0], table_ref[i, 1]))
            total[0], total[1] = total[0] + term[0], total[1] + term[1]
    return sums


def plane_kernel(got_ref, mine_tab_ref, all_tab_ref, plane_ref, filt_ref, mine_ref, rim_ref, send_ref, wide_ref, wire_ref):
    mine, total = gathered(got_ref, wide_ref, plane_ref, 3, filt_ref, (mine_tab_ref, all_tab_ref), False)
    place = lax.rem(lax.axis_index("seq"), LOW)
    near = wide_ref[jnp.maximum(place - 1, 0), TAIL : TAIL + TILE]
    rim_ref[0] = jnp.where(place > 0, near, 0.0)
    rim_ref[1] = wide_ref[0, HEAD : HEAD + TILE]
    for c in range(2):
        mine_ref[c] = mine[c]
        wire_ref[c * MODES : (c + 1) * MODES] = total[c]
    wire_ref[HEAD:TAIL] = wide_ref[0, HEAD:TAIL]
    wire_ref[TAIL:] = wide_ref[LOW - 1, TAIL:]
    wire = wire_ref[...].astype(send_ref.dtype)
    for i in range(PLANES):
        send_ref[i] = wire


def final_kernel(
    got_ref, far_tab_ref, rim_ref, plane_ref, filt_ref, mine_ref, carry_ref, p64_ref, p8_ref, gt_ref, gate_ref, local_ref,
    head_ref, skip_ref, before_ref, out_ref, wide_ref, e_ref, y_ref, fix_ref,
):
    rows = gate_ref.shape[0]
    subs = rows // SUB
    (far,) = gathered(got_ref, wide_ref, plane_ref, 5, filt_ref, (far_tab_ref,), True)
    far = cmul(far, (plane_ref[0, 0], plane_ref[0, 1]))
    block = lax.axis_index("seq")
    place, plane = lax.rem(block, LOW), lax.div(block, LOW)
    old = jnp.where(plane > 0, wide_ref[jnp.maximum(plane - 1, 0), TAIL : TAIL + TILE], 0.0)
    extra = impulses(plane_ref, 3, edges(filt_ref, lines(rim_ref.at[1], 0, 4), [old[i : i + 1] for i in range(4)]))
    near = cmul(extra, (plane_ref[1, 0], plane_ref[1, 1]))
    rim = rim_ref[0] + jnp.where(place > 0, 0.0, old)
    old = {1: (rim[0:1], rim[1:2]), 2: (rim[2:3], rim[3:4]), 0: (rim[4:5], rim[5:6])}
    late = {}
    for g in range(3):
        taps = [filt_ref[3 * g + j : 3 * g + j + 1] for j in range(3)]
        late[g] = (taps[1] * old[g][1] + taps[2] * old[g][0], taps[2] * old[g][1])
    pair = [
        (head_ref[2 + i : 3 + i] + late[1][i]) * (head_ref[4 + i : 5 + i] + late[2][i]) for i in range(2)
    ]
    own = impulses(plane_ref, 7, pair)
    enter = [mine_ref[c] + near[c] + far[c] + own[c] for c in range(2)]
    fix_ref[...] = jnp.zeros_like(fix_ref)
    for i in range(2):
        fix_ref[0, i : i + 1] = late[0][i]
        fix_ref[1, i : i + 1] = skip_ref[...] * pair[i]
    fix_ref[1, 0:1] -= before_ref[...] * pair[1]
    for q in range(subs):
        moved = cmul(enter, (p64_ref[q, 0], p64_ref[q, 1])) if q else enter
        for c in range(2):
            e_ref[q, c] = moved[c] + carry_ref[q, c]
    sums = [[None] * STEPS for _ in range(subs)]
    for m in range(MODES):
        table = (gt_ref[m, 0], gt_ref[m, 1])
        value = [cmul(table, (e_ref[q, 0, m : m + 1, :], e_ref[q, 1, m : m + 1, :])) for q in range(subs)]
        for k in range(STEPS):
            if k:
                by = [p8_ref[k, c, m : m + 1, :] for c in range(2)]
            for q in range(subs):
                term = by[0] * value[q][0] - by[1] * value[q][1] if k else value[q][0]
                sums[q][k] = term if m == 0 else sums[q][k] + term
    for q in range(subs):
        for k in range(STEPS):
            at = pl.ds(q * SUB + TILE * k, TILE)
            gate, conv = gate_ref[at, :], local_ref[at, :] + sums[q][k]
            if q == 0 and k == 0:
                gate, conv = gate + fix_ref[0], conv + fix_ref[1]
            y_ref[at, :] = gate * conv
    out_ref[...] = y_ref[...].T.astype(BF16)


def body(tokens, norm_gain, in_weight, short_filter, decay_reach, mode_freq, residues, skip_gain):
    rows, cols = tokens.shape
    fsdp = lax.axis_size("fsdp")
    state = shape(2, MODES, LANES)

    packed = 3 * rows + EXTRA
    weight = jnp.transpose(in_weight, (1, 0, 2))
    block = shape(packed, LANES, dtype=BF16)
    *sent, own = call(
        project_kernel,
        (block, block, block, shape(packed, LANES)),
        (tokens, pltpu.with_memory_space_constraint(norm_gain[None], pltpu.HBM), weight),
        [
            pltpu.VMEM((rows, cols), BF16),
            pltpu.VMEM((1, cols), F32),
            pltpu.VMEM((3, cols, 4 * LANES), BF16),
            pltpu.VMEM((rows, cols), BF16),
            pltpu.VMEM((rows, LANES), F32),
            pltpu.VMEM((EXTRA, LANES), F32),
            pltpu.VMEM((rows, 4 * LANES), F32),
            pltpu.SemaphoreType.DMA((5,)),
            pltpu.SemaphoreType.DMA((3,)),
        ],
        limit=52 << 20,
        flops=2 * rows * cols * 12 * LANES,
        places=[HBM] * 3,
    )
    arrived = [
        lax.ppermute(part, "fsdp", [(i, (i + step) % fsdp) for i in range(fsdp)])
        for step, part in zip((2, 1, 3), sent)
    ]
    p8, r7, gt, p64, mine_tab, all_tab, far_tab, plane_tab, taps, before = call(
        table_kernel,
        (
            shape(STEPS, 2, MODES, LANES),
            shape(MODES, 2, TILE, LANES),
            shape(MODES, 2, TILE, LANES),
            shape(4, 2, MODES, LANES),
            shape(LOW, 2, MODES, LANES),
            shape(LOW, 2, MODES, LANES),
            shape(PLANES, 2, MODES, LANES),
            shape(9, 2, MODES, LANES),
            shape(SUB, LANES),
            shape(1, LANES),
        ),
        (decay_reach.T, mode_freq.T, residues.T),
        [pltpu.VMEM((2 * LOW, 2, MODES, LANES), F32)],
        flops=1 << 27,
    )
    filt = jnp.transpose(short_filter, (1, 2, 0)).reshape(9, LANES)
    skip = skip_gain[None]
    wire = shape(LOW, WIRE, LANES, dtype=BF16)
    gate, local_part, carry, send, head = call(
        signal_kernel,
        (shape(rows, LANES), shape(rows, LANES), shape(4, 2, MODES, LANES), wire, shape(TILE, LANES)),
        (own, *arrived, filt, p8, r7, p64, skip, taps),
        [
            pltpu.VMEM((3, TILE + rows, LANES), F32),
            pltpu.VMEM((4, 2, MODES, LANES), F32),
            pltpu.VMEM((WIRE, LANES), F32),
            pltpu.VMEM((rows, LANES), F32),
            pltpu.VMEM((TILE + SUB, LANES), F32),
        ],
        flops=1 << 27,
    )
    plane = [[LOW * g + j for j in range(LOW)] for g in range(PLANES)]
    got = lax.all_to_all(send, "seq", 0, 0, axis_index_groups=plane)
    mine, rim, send = call(
        plane_kernel,
        (state, shape(2, TILE, LANES), wire),
        (got, mine_tab, all_tab, plane_tab, filt),
        [pltpu.VMEM((LOW, WIRE, LANES), F32), pltpu.VMEM((WIRE, LANES), F32)],
        flops=1 << 24,
    )
    line = [[LOW * j + g for j in range(PLANES)] for g in range(LOW)]
    got = lax.all_to_all(send, "seq", 0, 0, axis_index_groups=line)
    return call(
        final_kernel,
        shape(LANES, rows, dtype=BF16),
        (got, far_tab, rim, plane_tab, filt, mine, carry, p64, p8, gt, gate, local_part, head, skip, before),
        [
            pltpu.VMEM((PLANES, WIRE, LANES), F32),
            pltpu.VMEM((4, 2, MODES, LANES), F32),
            pltpu.VMEM((rows, LANES), F32),
            pltpu.VMEM((2, TILE, LANES), F32),
        ],
        flops=1 << 27,
    )


def solution(mesh):
    placed = (
        P("seq", "fsdp"),
        P("fsdp"),
        P("fsdp", None, None),
        P("fsdp", None, None),
        P("fsdp", None),
        P("fsdp", None),
        P("fsdp", None),
        P("fsdp"),
    )
    return jax.shard_map(
        body, mesh=mesh, in_specs=placed, out_specs=P("fsdp", "seq"), check_vma=False
    )
```

time: 60.5 us -> 46.8 us (0.77)
  the two profiles are of different devices: /device:TPU:1 before, /device:TPU:8 now
where the time goes in v2:
time: 46.8 us; the launch traced here: 46.6 us
  blocking collectives  26.9 us (57%)
  waiting for transfers between devices  7.79 us (17%)
  Pallas kernels  7.45 us (16%)
  starting transfers between devices  4.41 us (9%)
    all_to_all x1, blocking collectives, body(): got = lax.all_to_all(send, 'seq', 0, 0, axis_index_groups=line)  17 us
    all_to_all x1, blocking collectives, body(): got = lax.all_to_all(send, 'seq', 0, 0, axis_index_groups=plane)  9.9 us
    ppermute x3, waiting for transfers between devices, body(): lax.ppermute(part, 'fsdp', [(i, (i + step) % fsdp) for i in range(fsdp)])  7.79 us
    pallas_call x5, Pallas kernels, call(): pl.pallas_call(kernel, out_shape=out_shape, in_specs=places or [VMEM] * l...  7.45 us
    ppermute x3, starting transfers between devices, body(): lax.ppermute(part, 'fsdp', [(i, (i + step) % fsdp) for i in range(fsdp)])  4.41 us
  transfers between devices with their start and end apart: 3, of which 2 were waited for; matrix products, arithmetic and copies ran while one was open for 0% of the time, Pallas kernels for 1%

profile of v2, /device:TPU:8, one launch (start us, length us, event | category | flops | bytes accessed | tf_op | source)
XLA Modules:
  0.0 46.6 jit_solution(4683050704522233803)
XLA Ops:
  0.0 0.0 copy-start.4
  0.0 0.0 copy-start.3
  0.0 0.0 copy-start.2
  0.0 0.0 copy-start.1
  0.0 0.0 copy-start
  0.0 4.7 %shard_map.82 = (bf16[784,128]{1,0:T(8,128)(2,1)S(1)}, bf16[784,128]{1,0:T(8,128)(2,1)S(1)}, bf16[784,128]{1,0:T(8,128)(2,1)S(1)}, f32[784,128]{1,0:T(8,128)S(1)}) custom-call(bf16[256,2048]{1,0:T(8,128)(2,1)} %tok_hbm.1, f32[1,2048]{1,0:T(1,128)} %bitcast.13, bf16[3,2048,512]{2,1,0:T(8,128)(2,1)} %bitcast.12), custom_call_target="tpu_custom_call" | custom-call | flops 1610612736 | bytes 8351744 | tf_op jit(solution)/shard_map/pallas_call | solution.py:30
  4.7 2.4 %collective-permute-start = (bf16[784,128]{1,0:T(8,128)(2,1)S(1)}, bf16[784,128]{1,0:T(8,128)(2,1)S(1)}, u32[]{:S(2)}, u32[]{:S(2)}) collective-permute-start(bf16[784,128]{1,0:T(8,128)(2,1)S(1)} %get-tuple-element.28), channel_id=1, source_target_pairs={{0,128},{64,192},{128,0},{192,64},{1,129},{65,193},{129,1},{193,65... | collective-permute-start | bytes 602120 | tf_op jit(solution)/shard_map/ppermute | solution.py:409
  7.1 1.3 %collective-permute-start.1 = (bf16[784,128]{1,0:T(8,128)(2,1)S(1)}, bf16[784,128]{1,0:T(8,128)(2,1)S(1)}, u32[]{:S(2)}, u32[]{:S(2)}) collective-permute-start(bf16[784,128]{1,0:T(8,128)(2,1)S(1)} %get-tuple-element.29), channel_id=1, source_target_pairs={{0,64},{64,128},{128,192},{192,0},{1,65},{65,129},{129,193},{193,1... | collective-permute-start | bytes 602120 | tf_op jit(solution)/shard_map/ppermute | solution.py:409
  8.4 0.7 %collective-permute-start.2 = (bf16[784,128]{1,0:T(8,128)(2,1)S(1)}, bf16[784,128]{1,0:T(8,128)(2,1)S(1)}, u32[]{:S(2)}, u32[]{:S(2)}) collective-permute-start(bf16[784,128]{1,0:T(8,128)(2,1)S(1)} %get-tuple-element.30), channel_id=1, source_target_pairs={{0,192},{64,0},{128,64},{192,128},{1,193},{65,1},{129,65},{193,129... | collective-permute-start | bytes 602120 | tf_op jit(solution)/shard_map/ppermute | solution.py:409
  9.1 0.0 copy-done.4
  9.1 0.0 copy-done.3
  9.1 0.0 copy-done.2
  9.1 0.0 copy-done.1
  9.1 0.5 %shard_map.83 = (f32[8,2,16,128]{3,2,1,0:T(8,128)S(1)}, f32[16,2,8,128]{3,2,1,0:T(8,128)S(1)}, f32[16,2,8,128]{3,2,1,0:T(8,128)S(1)}, f32[4,2,16,128]{3,2,1,0:T(...) custom-call(f32[16,128]{1,0:T(8,128)S(1)} %bitcast.9, ...), custom_call_target="tpu_custom_call" | custom-call | flops 134217728 | bytes 1057280 | tf_op jit(solution)/shard_map/pallas_call | solution.py:30
  9.7 4.5 %collective-permute-done.b_ref = bf16[784,128]{1,0:T(8,128)(2,1)S(1)} collective-permute-done((bf16[784,128]{1,0:T(8,128)(2,1)S(1)}, bf16[784,128]{1,0:T(8,128)(2,1)S(1)}, u32[]{:S(2)}, u32[]{:S(2)}) %collective-permute-start) | collective-permute-done | bytes 200736 | tf_op jit(solution)/shard_map/ppermute | solution.py:409
  14.2 3.2 %collective-permute-done.1.c_ref = bf16[784,128]{1,0:T(8,128)(2,1)S(1)} collective-permute-done((bf16[784,128]{1,0:T(8,128)(2,1)S(1)}, bf16[784,128]{1,0:T(8,128)(2,1)S(1)}, u32[]{:S(2)}, u32[]{:S(2)}) %collective-permute-start.1) | collective-permute-done | bytes 200736 | tf_op jit(solution)/shard_map/ppermute | solution.py:409
  17.4 0.0 collective-permute-done.2.d_ref
  17.5 0.0 copy-done
  17.5 1.0 %shard_map.84 = (f32[256,128]{1,0:T(8,128)S(1)}, f32[256,128]{1,0:T(8,128)S(1)}, f32[4,2,16,128]{3,2,1,0:T(8,128)S(1)}, bf16[8,48,128]{2,1,0:T(8,128)(2,1)S(1)}, f32[8,128]{1,0:T(8,128)S(1)}) custom-call(f32[784,128]{1,0:T(8,128)S(1)} %get-tuple-element.27.a_ref, bf16[784,128]{1,0:T(8,128)(2,1)S(1)} %collective-permute-done.b_ref, ...), custom_call_target="tpu_custom_call" | custom-call | flops 134217728 | bytes 1799168 | tf_op jit(solution)/shard_map/pallas_call | solution.py:30
  18.5 9.9 %all_to_all.10.got_ref = bf16[8,48,128]{2,1,0:T(8,128)(2,1)S(1)} all-to-all(bf16[8,48,128]{2,1,0:T(8,128)(2,1)S(1)} %get-tuple-element.35), channel_id=1, replica_groups={{0,1,2,3,4,5,6,7},{8,9,10,11,12,13,14,15},{16,17,18,19,20,21,22,23},{24..., dimensions={0} | all-to-all | bytes 196608 | tf_op jit(solution)/shard_map/all_to_all | solution.py:447
  28.3 0.1 shard_map.85
  28.5 17.0 %all_to_all.11.got_ref = bf16[8,48,128]{2,1,0:T(8,128)(2,1)S(1)} all-to-all(bf16[8,48,128]{2,1,0:T(8,128)(2,1)S(1)} %get-tuple-element.39), channel_id=1, replica_groups={{0,8,16,24,32,40,48,56},{1,9,17,25,33,41,49,57},{2,10,18,26,34,42,50,58..., dimensions={0} | all-to-all | bytes 196608 | tf_op jit(solution)/shard_map/all_to_all | solution.py:456
  45.5 1.2 %shard_map.86 = bf16[128,256]{1,0:T(8,128)(2,1)} custom-call(bf16[8,48,128]{2,1,0:T(8,128)(2,1)S(1)} %all_to_all.11.got_ref, f32[8,2,16,128]{3,2,1,0:T(8,128)S(1)} %get-tuple-element.40.far_tab_ref, f32[2,8,128]{2,1,0:T(8,128)S(1)} %get-tuple-element.41.rim_ref, f32[9,2,16,128]{3,2,1,0:T(8,128)S(1)} %get-tuple-element.38.plane_ref, ...), custom_call_target="tpu_custom_call" | custom-call | flops 134217728 | bytes 1132032 | tf_op jit(solution)/shard_map/pallas_call | solution.py:30
  (1 shorter events, 0.0 us)
Async XLA Ops:
  0.0 9.1 %copy-start.4 = (f32[128,3,3]{0,2,1:T(4,128)S(1)}, f32[128,3,3]{0,2,1:T(4,128)}, u32[]{:S(2)}) copy-start(f32[128,3,3]{0,2,1:T(4,128)} %param.11) | copy-start | bytes 13828
  0.0 9.1 %copy-start.3 = (f32[128,16]{0,1:T(8,128)S(1)}, f32[128,16]{0,1:T(8,128)}, u32[]{:S(2)}) copy-start(f32[128,16]{0,1:T(8,128)} %param.14) | copy-start | bytes 24580
  0.0 9.1 %copy-start.2 = (f32[128,16]{0,1:T(8,128)S(1)}, f32[128,16]{0,1:T(8,128)}, u32[]{:S(2)}) copy-start(f32[128,16]{0,1:T(8,128)} %param.13) | copy-start | bytes 24580
  0.0 9.1 %copy-start.1 = (f32[128,16]{0,1:T(8,128)S(1)}, f32[128,16]{0,1:T(8,128)}, u32[]{:S(2)}) copy-start(f32[128,16]{0,1:T(8,128)} %param.12) | copy-start | bytes 24580
  0.0 17.4 %copy-start = (f32[128]{0:T(128)S(1)}, f32[128]{0:T(128)}, u32[]{:S(2)}) copy-start(f32[128]{0:T(128)} %param.15) | copy-start | bytes 1540
  4.7 9.5 %collective-permute-start = (bf16[784,128]{1,0:T(8,128)(2,1)S(1)}, bf16[784,128]{1,0:T(8,128)(2,1)S(1)}, u32[]{:S(2)}, u32[]{:S(2)}) collective-permute-start(bf16[784,128]{1,0:T(8,128)(2,1)S(1)} %get-tuple-element.28), channel_id=1, source_target_pairs={{0,128},{64,192},{128,0},{192,64},{1,129},{65,193},{129,1},{193,65... | collective-permute-start | bytes 602120 | tf_op jit(solution)/shard_map/ppermute | solution.py:409
  7.1 10.4 %collective-permute-start.1 = (bf16[784,128]{1,0:T(8,128)(2,1)S(1)}, bf16[784,128]{1,0:T(8,128)(2,1)S(1)}, u32[]{:S(2)}, u32[]{:S(2)}) collective-permute-start(bf16[784,128]{1,0:T(8,128)(2,1)S(1)} %get-tuple-element.29), channel_id=1, source_target_pairs={{0,64},{64,128},{128,192},{192,0},{1,65},{65,129},{129,193},{193,1... | collective-permute-start | bytes 602120 | tf_op jit(solution)/shard_map/ppermute | solution.py:409
  8.4 9.0 %collective-permute-start.2 = (bf16[784,128]{1,0:T(8,128)(2,1)S(1)}, bf16[784,128]{1,0:T(8,128)(2,1)S(1)}, u32[]{:S(2)}, u32[]{:S(2)}) collective-permute-start(bf16[784,128]{1,0:T(8,128)(2,1)S(1)} %get-tuple-element.30), channel_id=1, source_target_pairs={{0,192},{64,0},{128,64},{192,128},{1,193},{65,1},{129,65},{193,129... | collective-permute-start | bytes 602120 | tf_op jit(solution)/shard_map/ppermute | solution.py:409

commit v3 on v2

--- a/solution.py
+++ b/solution.py
@@ -137,11 +137,12 @@
 
 
 def project_kernel(
-    tok_hbm, gain_hbm, w_hbm, two_ref, one_ref, three_ref, own_ref,
+    tok_hbm, gain_hbm, w_hbm, own_ref, one_ref, two_ref, three_ref, own_gate, one_gate, two_gate, three_gate,
     tok_ref, gain_ref, w_ref, xg_ref, acc_ref, ext_ref, got_ref, sems, w_sems,
 ):
     rows, cols = tok_ref.shape
-    outs = {2: two_ref, 1: one_ref, 3: three_ref, 0: own_ref}
+    outs = (own_ref, one_ref, two_ref, three_ref)
+    gates = (own_gate, one_gate, two_gate, three_gate)
     pieces = 4
     span = rows // pieces
     gain_copy = pltpu.make_async_copy(gain_hbm, gain_ref, sems.at[0])
@@ -151,7 +152,7 @@
         at = pl.ds(i * span, span)
         tok_copies.append(pltpu.make_async_copy(tok_hbm.at[at], tok_ref.at[at], sems.at[1 + i]))
         tok_copies[-1].start(priority=i % 2)
-    w_copies = [pltpu.make_async_copy(w_hbm.at[g], w_ref.at[g], w_sems.at[g]) for g in range(3)]
+    w_copies = [pltpu.make_async_copy(w_hbm.at[(g + 1) % 3], w_ref.at[g], w_sems.at[g]) for g in range(3)]
     w_copies[0].start(priority=0)
     w_copies[1].start(priority=1)
     gain_copy.wait()
@@ -180,18 +181,21 @@
         high = value.astype(BF16).astype(F32)
         ext_ref[i : i + 1] = high
         ext_ref[2 + i : 3 + i] = value - high
-    for out in outs.values():
-        out[3 * rows :] = ext_ref[...].astype(out.dtype)
     me = lax.axis_index("fsdp")
     for g in range(3):
         w_copies[g].wait()
         got_ref[...] = jnp.dot(xg_ref[...], w_ref[g], preferred_element_type=F32)
-        for d, out in outs.items():
+        for d in range(4):
             at = pl.ds(pl.multiple_of(lax.rem(me + d, 4) * LANES, LANES), LANES)
-            out[g * rows : (g + 1) * rows] = got_ref[:, at].astype(out.dtype)
-
-
-def local(sig_ref, skip_ref, h_ref, out_ref, pad_ref):
+            if g < 2:
+                outs[d][g * rows : (g + 1) * rows] = got_ref[:, at].astype(outs[d].dtype)
+            else:
+                gates[d][...] = got_ref[:, at].astype(gates[d].dtype)
+                ext_ref[4:6] = got_ref[rows - 2 : rows, at]
+                outs[d][2 * rows :] = ext_ref[...].astype(outs[d].dtype)
+
+
+def local_kernel(sig_ref, skip_ref, h_ref, _, out_ref, pad_ref):
     pad_ref[0:TILE] = jnp.zeros((TILE, LANES), F32)
     for q in range(sig_ref.shape[0] // SUB):
         pad_ref[TILE:] = sig_ref[pl.ds(q * SUB, SUB), :]
@@ -206,43 +210,48 @@
             out_ref[pl.ds(q * SUB + TILE * i, TILE), :] = sums[i]
 
 
+def summed(refs, lo, n):
+    at = pl.ds(lo, n)
+    return refs[0][at, :] + (refs[1][at, :].astype(F32) + refs[2][at, :].astype(F32) + refs[3][at, :].astype(F32))
+
+
+def stream(refs, lo, scale_ref, filt_ref, g, ext_ref):
+    rows = scale_ref.shape[0]
+    ext_ref[0:TILE] = jnp.zeros((TILE, LANES), F32)
+    for i in range(0, rows, LANES):
+        value = summed(refs, lo + i, LANES) * scale_ref[pl.ds(i, LANES), :]
+        ext_ref[pl.ds(TILE + i, LANES), :] = value.astype(BF16).astype(F32)
+    taps = [filt_ref[3 * g + j : 3 * g + j + 1] for j in range(3)]
+    return (
+        taps[0] * ext_ref[pl.ds(TILE, rows), :]
+        + taps[1] * ext_ref[pl.ds(TILE - 1, rows), :]
+        + taps[2] * ext_ref[pl.ds(TILE - 2, rows), :]
+    )
+
+
 def signal_kernel(
-    a_ref, b_ref, c_ref, d_ref, filt_ref, p8_ref, r7_ref, p64_ref, skip_ref, h_ref,
-    gate_ref, local_ref, carry_ref, send_ref, head_ref, ext_ref, u_ref, wire_ref, sig_ref, pad_ref,
+    a_ref, b_ref, c_ref, d_ref, filt_ref, p8_ref, r7_ref, p64_ref,
+    scale_ref, sig_ref, carry_ref, send_ref, head_ref, ext_ref, u_ref, wire_ref,
 ):
-    rows = gate_ref.shape[0]
+    rows = sig_ref.shape[0]
     subs = rows // SUB
-
-    def summed(lo, n):
-        at = pl.ds(lo, n)
-        return a_ref[at, :] + (b_ref[at, :].astype(F32) + c_ref[at, :].astype(F32) + d_ref[at, :].astype(F32))
-
-    tail = summed(3 * rows, EXTRA)
-    inverse = [lax.rsqrt((tail[i : i + 1] + tail[2 + i : 3 + i]) * (1.0 / D) + 1e-6) for i in range(rows // LANES)]
-    columns = [jnp.broadcast_to(v, (LANES, LANES)).T for v in inverse]
-    streams = []
-    for g in range(3):
-        ext_ref[g, 0:TILE] = jnp.zeros((TILE, LANES), F32)
-        for i in range(rows // LANES):
-            value = summed(g * rows + i * LANES, LANES) * columns[i]
-            ext_ref[g, pl.ds(TILE + i * LANES, LANES), :] = value.astype(BF16).astype(F32)
-        taps = [filt_ref[3 * g + j : 3 * g + j + 1] for j in range(3)]
-        streams.append(
-            taps[0] * ext_ref[g, pl.ds(TILE, rows), :]
-            + taps[1] * ext_ref[g, pl.ds(TILE - 1, rows), :]
-            + taps[2] * ext_ref[g, pl.ds(TILE - 2, rows), :]
-        )
-        if g == 0:
-            gate_ref[...] = streams[0]
-    for g in range(3):
+    refs = (a_ref, b_ref, c_ref, d_ref)
+    tail = summed(refs, 2 * rows, EXTRA)
+    for i in range(rows // LANES):
+        inverse = lax.rsqrt((tail[i : i + 1] + tail[2 + i : 3 + i]) * (1.0 / D) + 1e-6)
+        scale_ref[pl.ds(i * LANES, LANES), :] = jnp.broadcast_to(inverse, (LANES, LANES)).T
+    streams = [stream(refs, g * rows, scale_ref, filt_ref, 1 + g, ext_ref.at[g]) for g in range(2)]
+    head_ref[...] = jnp.zeros_like(head_ref)
+    for g in range(2):
         head_ref[2 * g : 2 * g + 2] = streams[g][:2]
-    head_ref[6:] = jnp.zeros((2, LANES), F32)
-    signal = streams[1] * streams[2]
+    signal = streams[0] * streams[1]
     row = lax.broadcasted_iota(jnp.int32, (rows, LANES), 0)
     sig_ref[...] = jnp.where(row < 2, 0.0, signal)
     wire_ref[HEAD:] = jnp.zeros((WIRE - HEAD, LANES), F32)
-    for i, (g, at) in enumerate(((1, 0), (2, 0), (1, rows - 2), (2, rows - 2), (0, rows - 2))):
+    for i, (g, at) in enumerate(((0, 0), (1, 0), (0, rows - 2), (1, rows - 2))):
         wire_ref[HEAD + 2 * i : HEAD + 2 * i + 2] = ext_ref[g, TILE + at : TILE + at + 2]
+    gate = tail[4:6] * scale_ref[rows - 2 :]
+    wire_ref[TAIL + 4 : TAIL + 6] = gate.astype(BF16).astype(F32)
     tiles = [[sig_ref[pl.ds(q * SUB + TILE * k, TILE), :] for k in range(STEPS)] for q in range(subs)]
     for m in range(MODES):
         real = [tiles[q][STEPS - 1] for q in range(subs)]
@@ -269,7 +278,6 @@
     wire = wire_ref[...].astype(send_ref.dtype)
     for i in range(LOW):
         send_ref[i] = wire
-    local(sig_ref, skip_ref, h_ref, local_ref, pad_ref)
 
 
 def edges(filt_ref, first, rim):
@@ -307,6 +315,10 @@
             term = cmul(value, (table_ref[i, 0], table_ref[i, 1]))
             total[0], total[1] = total[0] + term[0], total[1] + term[1]
     return sums
+
+
+def gate_kernel(a_ref, b_ref, c_ref, d_ref, scale_ref, filt_ref, gate_ref, ext_ref):
+    gate_ref[...] = stream((a_ref, b_ref, c_ref, d_ref), 0, scale_ref, filt_ref, 0, ext_ref)
 
 
 def plane_kernel(got_ref, mine_tab_ref, all_tab_ref, plane_ref, filt_ref, mine_ref, rim_ref, send_ref, wide_ref, wire_ref):
@@ -345,7 +357,7 @@
         taps = [filt_ref[3 * g + j : 3 * g + j + 1] for j in range(3)]
         late[g] = (taps[1] * old[g][1] + taps[2] * old[g][0], taps[2] * old[g][1])
     pair = [
-        (head_ref[2 + i : 3 + i] + late[1][i]) * (head_ref[4 + i : 5 + i] + late[2][i]) for i in range(2)
+        (head_ref[i : i + 1] + late[1][i]) * (head_ref[2 + i : 3 + i] + late[2][i]) for i in range(2)
     ]
     own = impulses(plane_ref, 7, pair)
     enter = [mine_ref[c] + near[c] + far[c] + own[c] for c in range(2)]
@@ -383,12 +395,19 @@
     fsdp = lax.axis_size("fsdp")
     state = shape(2, MODES, LANES)
 
-    packed = 3 * rows + EXTRA
+    packed = 2 * rows + EXTRA
     weight = jnp.transpose(in_weight, (1, 0, 2))
     block = shape(packed, LANES, dtype=BF16)
-    *sent, own = call(
+
+    def exchange(own, *parts):
+        sent = {
+            d: lax.ppermute(parts[d - 1], "fsdp", [(i, (i + d) % fsdp) for i in range(fsdp)]) for d in (2, 1, 3)
+        }
+        return own, sent[1], sent[2], sent[3]
+
+    products = call(
         project_kernel,
-        (block, block, block, shape(packed, LANES)),
+        (shape(packed, LANES), block, block, block, shape(rows, LANES), *[shape(rows, LANES, dtype=BF16)] * 3),
         (tokens, pltpu.with_memory_space_constraint(norm_gain[None], pltpu.HBM), weight),
         [
             pltpu.VMEM((rows, cols), BF16),
@@ -405,10 +424,8 @@
         flops=2 * rows * cols * 12 * LANES,
         places=[HBM] * 3,
     )
-    arrived = [
-        lax.ppermute(part, "fsdp", [(i, (i + step) % fsdp) for i in range(fsdp)])
-        for step, part in zip((2, 1, 3), sent)
-    ]
+    pair = exchange(*products[:4])
+    gates = exchange(*products[4:])
     p8, r7, gt, p64, mine_tab, all_tab, far_tab, plane_tab, taps, before = call(
         table_kernel,
         (
@@ -430,16 +447,14 @@
     filt = jnp.transpose(short_filter, (1, 2, 0)).reshape(9, LANES)
     skip = skip_gain[None]
     wire = shape(LOW, WIRE, LANES, dtype=BF16)
-    gate, local_part, carry, send, head = call(
+    scale, signal, carry, send, head = call(
         signal_kernel,
         (shape(rows, LANES), shape(rows, LANES), shape(4, 2, MODES, LANES), wire, shape(TILE, LANES)),
-        (own, *arrived, filt, p8, r7, p64, skip, taps),
+        (*pair, filt, p8, r7, p64),
         [
-            pltpu.VMEM((3, TILE + rows, LANES), F32),
+            pltpu.VMEM((2, TILE + rows, LANES), F32),
             pltpu.VMEM((4, 2, MODES, LANES), F32),
             pltpu.VMEM((WIRE, LANES), F32),
-            pltpu.VMEM((rows, LANES), F32),
-            pltpu.VMEM((TILE + SUB, LANES), F32),
         ],
         flops=1 << 27,
     )
@@ -450,6 +465,20 @@
         (state, shape(2, TILE, LANES), wire),
         (got, mine_tab, all_tab, plane_tab, filt),
         [pltpu.VMEM((LOW, WIRE, LANES), F32), pltpu.VMEM((WIRE, LANES), F32)],
+        flops=1 << 24,
+    )
+    local_part = call(
+        local_kernel,
+        shape(rows, LANES),
+        (signal, skip, taps, rim),
+        [pltpu.VMEM((TILE + SUB, LANES), F32)],
+        flops=1 << 27,
+    )
+    gate = call(
+        gate_kernel,
+        shape(rows, LANES),
+        (*gates, scale, filt),
+        [pltpu.VMEM((TILE + rows, LANES), F32)],
         flops=1 << 24,
     )
     line = [[LOW * j + g for j in range(PLANES)] for g in range(LOW)]

time: 46.8 us -> 45 us (0.962)
  blocking collectives: 26.9 us -> 9.89 us
  starting transfers between devices: 4.41 us -> 17.9 us
  waiting for transfers between devices: 7.79 us -> 8.74 us
  Pallas kernels: 7.45 us -> 8.11 us
    all_to_all x1 -> x0, blocking collectives: 17 us -> none  [body(): got = lax.all_to_all(send, 'seq', 0, 0, axis_index_groups=line)]
    all_to_all x0 -> x1, starting transfers between devices: none -> 8.47 us  [body(): got = lax.all_to_all(send, 'seq', 0, 0, axis_index_groups=line)]
    ppermute x3 -> x6, starting transfers between devices: 4.41 us -> 9.43 us  [exchange(): lax.ppermute(parts[d - 1], 'fsdp', [(i, (i + d) % fsdp) for i in range(fs...]
    pallas_call x5 -> x7, Pallas kernels: 7.45 us -> 8.11 us  [call(): pl.pallas_call(kernel, out_shape=out_shape, in_specs=places or [VMEM] * l...]
    all_to_all x0 -> x1, waiting for transfers between devices: none -> 0.55 us  [body(): got = lax.all_to_all(send, 'seq', 0, 0, axis_index_groups=line)]
    ppermute x3 -> x6, waiting for transfers between devices: 7.79 us -> 8.18 us  [exchange(): lax.ppermute(parts[d - 1], 'fsdp', [(i, (i + d) % fsdp) for i in range(fs...]
  transfers between devices with their start and end apart: 3 -> 7, of which waited for: 2 -> 6; matrix products, arithmetic and copies ran while one was open for 0% -> 0% of each run, Pallas kernels for 1% -> 2%
where the time goes in v3:
time: 45 us; the launch traced here: 44.7 us
  starting transfers between devices  17.9 us (40%)
  blocking collectives  9.89 us (22%)
  waiting for transfers between devices  8.74 us (19%)
  Pallas kernels  8.11 us (18%)
    all_to_all x1, blocking collectives, body(): got = lax.all_to_all(send, 'seq', 0, 0, axis_index_groups=plane)  9.89 us
    ppermute x6, starting transfers between devices, exchange(): lax.ppermute(parts[d - 1], 'fsdp', [(i, (i + d) % fsdp) for i in range(fs...  9.43 us
    all_to_all x1, starting transfers between devices, body(): got = lax.all_to_all(send, 'seq', 0, 0, axis_index_groups=line)  8.47 us
    ppermute x6, waiting for transfers between devices, exchange(): lax.ppermute(parts[d - 1], 'fsdp', [(i, (i + d) % fsdp) for i in range(fs...  8.18 us
    pallas_call x7, Pallas kernels, call(): pl.pallas_call(kernel, out_shape=out_shape, in_specs=places or [VMEM] * l...  8.11 us
  transfers between devices with their start and end apart: 7, of which 6 were waited for; matrix products, arithmetic and copies ran while one was open for 0% of the time, Pallas kernels for 2%

profile of v3, /device:TPU:8, one launch (start us, length us, event | category | flops | bytes accessed | tf_op | source)
XLA Modules:
  0.0 44.7 jit_solution(10224723636751067988)
XLA Ops:
  0.0 0.0 copy-start.4
  0.0 0.0 copy-start.3
  0.0 0.0 copy-start.2
  0.0 0.0 copy-start.1
  0.0 0.0 copy-start
  0.0 4.7 %shard_map.82 = (f32[528,128]{1,0:T(8,128)S(1)}, bf16[528,128]{1,0:T(8,128)(2,1)S(1)}, bf16[528,128]{1,0:T(8,128)(2,1)S(1)}, bf16[528,128]{1,0:T(8,128)(2,1)S(1)...) custom-call(bf16[256,2048]{1,0:T(8,128)(2,1)} %tok_hbm.1, ...), custom_call_target="tpu_custom_call" | custom-call | flops 1610612736 | bytes 8351744 | tf_op jit(solution)/shard_map/pallas_call | solution.py:30
  4.7 1.6 %collective-permute-start = (bf16[528,128]{1,0:T(8,128)(2,1)S(1)}, bf16[528,128]{1,0:T(8,128)(2,1)S(1)}, u32[]{:S(2)}, u32[]{:S(2)}) collective-permute-start(bf16[528,128]{1,0:T(8,128)(2,1)S(1)} %get-tuple-element.32), channel_id=1, source_target_pairs={{0,64},{64,128},{128,192},{192,0},{1,65},{65,129},{129,193},{193,1... | collective-permute-start | bytes 405512 | tf_op jit(solution)/shard_map/ppermute | solution.py:404
  6.4 2.7 %collective-permute-start.1 = (bf16[528,128]{1,0:T(8,128)(2,1)S(1)}, bf16[528,128]{1,0:T(8,128)(2,1)S(1)}, u32[]{:S(2)}, u32[]{:S(2)}) collective-permute-start(bf16[528,128]{1,0:T(8,128)(2,1)S(1)} %get-tuple-element.33), channel_id=1, source_target_pairs={{0,128},{64,192},{128,0},{192,64},{1,129},{65,193},{129,1},{193,65... | collective-permute-start | bytes 405512 | tf_op jit(solution)/shard_map/ppermute | solution.py:404
  9.0 0.7 %collective-permute-start.2 = (bf16[528,128]{1,0:T(8,128)(2,1)S(1)}, bf16[528,128]{1,0:T(8,128)(2,1)S(1)}, u32[]{:S(2)}, u32[]{:S(2)}) collective-permute-start(bf16[528,128]{1,0:T(8,128)(2,1)S(1)} %get-tuple-element.34), channel_id=1, source_target_pairs={{0,192},{64,0},{128,64},{192,128},{1,193},{65,1},{129,65},{193,129... | collective-permute-start | bytes 405512 | tf_op jit(solution)/shard_map/ppermute | solution.py:404
  9.7 0.0 copy-done.4
  9.7 0.0 copy-done.3
  9.7 0.0 copy-done.2
  9.8 0.0 copy-done.1
  9.8 0.5 %shard_map.83 = (f32[8,2,16,128]{3,2,1,0:T(8,128)S(1)}, f32[16,2,8,128]{3,2,1,0:T(8,128)S(1)}, f32[16,2,8,128]{3,2,1,0:T(8,128)S(1)}, f32[4,2,16,128]{3,2,1,0:T(...) custom-call(f32[16,128]{1,0:T(8,128)S(1)} %bitcast.9, ...), custom_call_target="tpu_custom_call" | custom-call | flops 134217728 | bytes 1057280 | tf_op jit(solution)/shard_map/pallas_call | solution.py:30
  10.3 0.0 collective-permute-done.b_ref
  10.3 4.0 %collective-permute-done.1.c_ref = bf16[528,128]{1,0:T(8,128)(2,1)S(1)} collective-permute-done((bf16[528,128]{1,0:T(8,128)(2,1)S(1)}, bf16[528,128]{1,0:T(8,128)(2,1)S(1)}, u32[]{:S(2)}, u32[]{:S(2)}) %collective-permute-start.1) | collective-permute-done | bytes 135200 | tf_op jit(solution)/shard_map/ppermute | solution.py:404
  14.4 0.8 %collective-permute-done.2.d_ref = bf16[528,128]{1,0:T(8,128)(2,1)S(1)} collective-permute-done((bf16[528,128]{1,0:T(8,128)(2,1)S(1)}, bf16[528,128]{1,0:T(8,128)(2,1)S(1)}, u32[]{:S(2)}, u32[]{:S(2)}) %collective-permute-start.2) | collective-permute-done | bytes 135200 | tf_op jit(solution)/shard_map/ppermute | solution.py:404
  15.2 0.6 %shard_map.84 = (f32[256,128]{1,0:T(8,128)S(1)}, f32[256,128]{1,0:T(8,128)S(1)}, f32[4,2,16,128]{3,2,1,0:T(8,128)S(1)}, bf16[8,48,128]{2,1,0:T(8,128)(2,1)S(1)}, f32[8,128]{1,0:T(8,128)S(1)}) custom-call(f32[528,128]{1,0:T(8,128)S(1)} %get-tuple-element.31.a_ref, bf16[528,128]{1,0:T(8,128)(2,1)S(1)} %collective-permute-done.b_ref, ...), custom_call_target="tpu_custom_call" | custom-call | flops 134217728 | bytes 1438208 | tf_op jit(solution)/shard_map/pallas_call | solution.py:30
  15.8 9.9 %all_to_all.10.got_ref = bf16[8,48,128]{2,1,0:T(8,128)(2,1)S(1)} all-to-all(bf16[8,48,128]{2,1,0:T(8,128)(2,1)S(1)} %get-tuple-element.38), channel_id=1, replica_groups={{0,1,2,3,4,5,6,7},{8,9,10,11,12,13,14,15},{16,17,18,19,20,21,22,23},{24..., dimensions={0} | all-to-all | bytes 196608 | tf_op jit(solution)/shard_map/all_to_all | solution.py:462
  25.7 0.7 %shard_map.85 = (f32[2,16,128]{2,1,0:T(8,128)S(1)}, f32[2,8,128]{2,1,0:T(8,128)S(1)}, bf16[8,48,128]{2,1,0:T(8,128)(2,1)}) custom-call(bf16[8,48,128]{2,1,0:T(8,128)(2,1)S(1)} %all_to_all.10.got_ref, f32[8,2,16,128]{3,2,1,0:T(8,128)S(1)} %get-tuple-element.39.mine_tab_ref, f32[8,2,16,128]{3,2,1,0:T(8,128)S(1)} %get-tuple-element.40.all_tab_ref, ...), custom_call_target="tpu_custom_call" | custom-call | flops 16777216 | bytes 635392 | tf_op jit(solution)/shard_map/pallas_call | solution.py:30
  26.4 8.5 %all-to-all-start.1 = ((bf16[8,48,128]{2,1,0:T(8,128)(2,1)}), bf16[8,48,128]{2,1,0:T(8,128)(2,1)S(1)}, u32[]{:S(2)}, u32[]{:S(2)}) async-start(bf16[8,48,128]{2,1,0:T(8,128)(2,1)} %get-tuple-element.42), calls=%async_computation.1 | async-start | bytes 196608 | tf_op jit(solution)/shard_map/all_to_all | solution.py:485
  34.9 1.3 %collective-permute-start.3 = (bf16[256,128]{1,0:T(8,128)(2,1)S(1)}, bf16[256,128]{1,0:T(8,128)(2,1)S(1)}, u32[]{:S(2)}, u32[]{:S(2)}) collective-permute-start(bf16[256,128]{1,0:T(8,128)(2,1)S(1)} %get-tuple-element.49), channel_id=1, source_target_pairs={{0,64},{64,128},{128,192},{192,0},{1,65},{65,129},{129,193},{193,1... | collective-permute-start | bytes 196616 | tf_op jit(solution)/shard_map/ppermute | solution.py:404
  36.1 1.6 %collective-permute-start.4 = (bf16[256,128]{1,0:T(8,128)(2,1)S(1)}, bf16[256,128]{1,0:T(8,128)(2,1)S(1)}, u32[]{:S(2)}, u32[]{:S(2)}) collective-permute-start(bf16[256,128]{1,0:T(8,128)(2,1)S(1)} %get-tuple-element.50), channel_id=1, source_target_pairs={{0,128},{64,192},{128,0},{192,64},{1,129},{65,193},{129,1},{193,65... | collective-permute-start | bytes 196616 | tf_op jit(solution)/shard_map/ppermute | solution.py:404
  37.7 1.6 %collective-permute-start.5 = (bf16[256,128]{1,0:T(8,128)(2,1)S(1)}, bf16[256,128]{1,0:T(8,128)(2,1)S(1)}, u32[]{:S(2)}, u32[]{:S(2)}) collective-permute-start(bf16[256,128]{1,0:T(8,128)(2,1)S(1)} %get-tuple-element.51), channel_id=1, source_target_pairs={{0,192},{64,0},{128,64},{192,128},{1,193},{65,1},{129,65},{193,129... | collective-permute-start | bytes 196616 | tf_op jit(solution)/shard_map/ppermute | solution.py:404
  39.3 0.1 collective-permute-done.3.b_ref
  39.4 2.6 %collective-permute-done.4.c_ref = bf16[256,128]{1,0:T(8,128)(2,1)S(1)} collective-permute-done((bf16[256,128]{1,0:T(8,128)(2,1)S(1)}, bf16[256,128]{1,0:T(8,128)(2,1)S(1)}, u32[]{:S(2)}, u32[]{:S(2)}) %collective-permute-start.4) | collective-permute-done | bytes 65568 | tf_op jit(solution)/shard_map/ppermute | solution.py:404
  42.0 0.6 %collective-permute-done.5.d_ref = bf16[256,128]{1,0:T(8,128)(2,1)S(1)} collective-permute-done((bf16[256,128]{1,0:T(8,128)(2,1)S(1)}, bf16[256,128]{1,0:T(8,128)(2,1)S(1)}, u32[]{:S(2)}, u32[]{:S(2)}) %collective-permute-start.5) | collective-permute-done | bytes 65568 | tf_op jit(solution)/shard_map/ppermute | solution.py:404
  42.6 0.1 shard_map.86.gate_ref
  42.7 0.0 copy-done
  42.7 0.3 shard_map.87.local_ref
  43.0 0.6 %all-to-all-done.1.got_ref = bf16[8,48,128]{2,1,0:T(8,128)(2,1)S(1)} async-done(((bf16[8,48,128]{2,1,0:T(8,128)(2,1)}), bf16[8,48,128]{2,1,0:T(8,128)(2,1)S(1)}, u32[]{:S(2)}, u32[]{:S(2)}) %all-to-all-start.1) | async-done | bytes 98336 | tf_op jit(solution)/shard_map/all_to_all | solution.py:485
  43.6 1.1 %shard_map.88 = bf16[128,256]{1,0:T(8,128)(2,1)} custom-call(bf16[8,48,128]{2,1,0:T(8,128)(2,1)S(1)} %all-to-all-done.1.got_ref, f32[8,2,16,128]{3,2,1,0:T(8,128)S(1)} %get-tuple-element.43.far_tab_ref, f32[2,8,128]{2,1,0:T(8,128)S(1)} %get-tuple-element.44._.rim_ref, f32[9,2,16,128]{3,2,1,0:T(8,128)S(1)} %get-tuple-element.41.plane_ref, ...), custom_call_target="tpu_custom_call" | custom-call | flops 134217728 | bytes 1132032 | tf_op jit(solution)/shard_map/pallas_call | solution.py:30
  (1 shorter events, 0.0 us)
Async XLA Ops:
  0.0 9.7 %copy-start.4 = (f32[128,3,3]{0,2,1:T(4,128)S(1)}, f32[128,3,3]{0,2,1:T(4,128)}, u32[]{:S(2)}) copy-start(f32[128,3,3]{0,2,1:T(4,128)} %param.11) | copy-start | bytes 13828
  0.0 9.7 %copy-start.3 = (f32[128,16]{0,1:T(8,128)S(1)}, f32[128,16]{0,1:T(8,128)}, u32[]{:S(2)}) copy-start(f32[128,16]{0,1:T(8,128)} %param.14) | copy-start | bytes 24580
  0.0 9.7 %copy-start.2 = (f32[128,16]{0,1:T(8,128)S(1)}, f32[128,16]{0,1:T(8,128)}, u32[]{:S(2)}) copy-start(f32[128,16]{0,1:T(8,128)} %param.13) | copy-start | bytes 24580
  0.0 9.8 %copy-start.1 = (f32[128,16]{0,1:T(8,128)S(1)}, f32[128,16]{0,1:T(8,128)}, u32[]{:S(2)}) copy-start(f32[128,16]{0,1:T(8,128)} %param.12) | copy-start | bytes 24580
  0.0 42.7 %copy-start = (f32[128]{0:T(128)S(1)}, f32[128]{0:T(128)}, u32[]{:S(2)}) copy-start(f32[128]{0:T(128)} %param.15) | copy-start | bytes 1540
  4.7 5.6 %collective-permute-start = (bf16[528,128]{1,0:T(8,128)(2,1)S(1)}, bf16[528,128]{1,0:T(8,128)(2,1)S(1)}, u32[]{:S(2)}, u32[]{:S(2)}) collective-permute-start(bf16[528,128]{1,0:T(8,128)(2,1)S(1)} %get-tuple-element.32), channel_id=1, source_target_pairs={{0,64},{64,128},{128,192},{192,0},{1,65},{65,129},{129,193},{193,1... | collective-permute-start | bytes 405512 | tf_op jit(solution)/shard_map/ppermute | solution.py:404
  6.4 8.0 %collective-permute-start.1 = (bf16[528,128]{1,0:T(8,128)(2,1)S(1)}, bf16[528,128]{1,0:T(8,128)(2,1)S(1)}, u32[]{:S(2)}, u32[]{:S(2)}) collective-permute-start(bf16[528,128]{1,0:T(8,128)(2,1)S(1)} %get-tuple-element.33), channel_id=1, source_target_pairs={{0,128},{64,192},{128,0},{192,64},{1,129},{65,193},{129,1},{193,65... | collective-permute-start | bytes 405512 | tf_op jit(solution)/shard_map/ppermute | solution.py:404
  9.0 6.1 %collective-permute-start.2 = (bf16[528,128]{1,0:T(8,128)(2,1)S(1)}, bf16[528,128]{1,0:T(8,128)(2,1)S(1)}, u32[]{:S(2)}, u32[]{:S(2)}) collective-permute-start(bf16[528,128]{1,0:T(8,128)(2,1)S(1)} %get-tuple-element.34), channel_id=1, source_target_pairs={{0,192},{64,0},{128,64},{192,128},{1,193},{65,1},{129,65},{193,129... | collective-permute-start | bytes 405512 | tf_op jit(solution)/shard_map/ppermute | solution.py:404
  26.4 17.2 %all-to-all-start.1 = ((bf16[8,48,128]{2,1,0:T(8,128)(2,1)}), bf16[8,48,128]{2,1,0:T(8,128)(2,1)S(1)}, u32[]{:S(2)}, u32[]{:S(2)}) async-start(bf16[8,48,128]{2,1,0:T(8,128)(2,1)} %get-tuple-element.42), calls=%async_computation.1 | async-start | bytes 196608 | tf_op jit(solution)/shard_map/all_to_all | solution.py:485
  34.9 4.5 %collective-permute-start.3 = (bf16[256,128]{1,0:T(8,128)(2,1)S(1)}, bf16[256,128]{1,0:T(8,128)(2,1)S(1)}, u32[]{:S(2)}, u32[]{:S(2)}) collective-permute-start(bf16[256,128]{1,0:T(8,128)(2,1)S(1)} %get-tuple-element.49), channel_id=1, source_target_pairs={{0,64},{64,128},{128,192},{192,0},{1,65},{65,129},{129,193},{193,1... | collective-permute-start | bytes 196616 | tf_op jit(solution)/shard_map/ppermute | solution.py:404
  36.1 5.8 %collective-permute-start.4 = (bf16[256,128]{1,0:T(8,128)(2,1)S(1)}, bf16[256,128]{1,0:T(8,128)(2,1)S(1)}, u32[]{:S(2)}, u32[]{:S(2)}) collective-permute-start(bf16[256,128]{1,0:T(8,128)(2,1)S(1)} %get-tuple-element.50), channel_id=1, source_target_pairs={{0,128},{64,192},{128,0},{192,64},{1,129},{65,193},{129,1},{193,65... | collective-permute-start | bytes 196616 | tf_op jit(solution)/shard_map/ppermute | solution.py:404
  37.7 4.9 %collective-permute-start.5 = (bf16[256,128]{1,0:T(8,128)(2,1)S(1)}, bf16[256,128]{1,0:T(8,128)(2,1)S(1)}, u32[]{:S(2)}, u32[]{:S(2)}) collective-permute-start(bf16[256,128]{1,0:T(8,128)(2,1)S(1)} %get-tuple-element.51), channel_id=1, source_target_pairs={{0,192},{64,0},{128,64},{192,128},{1,193},{65,1},{129,65},{193,129... | collective-permute-start | bytes 196616 | tf_op jit(solution)/shard_map/ppermute | solution.py:404

commit v4 on v3

--- a/solution.py
+++ b/solution.py
@@ -164,8 +164,21 @@
         for lo in range(i * span, (i + 1) * span, 32):
             x = tok_ref[pl.ds(lo, 32), :].astype(F32)
             xg_ref[pl.ds(lo, 32), :] = (x * gain).astype(BF16)
-            sq = x * x
-            acc_ref[pl.ds(lo, 32), :] = sum(sq[:, j : j + LANES] for j in range(0, cols, LANES))
+    me = lax.axis_index("fsdp")
+    for g in range(3):
+        w_copies[g].wait()
+        got_ref[...] = jnp.dot(xg_ref[...], w_ref[g], preferred_element_type=F32)
+        if g == 0:
+            for lo in range(0, rows, 32):
+                x = tok_ref[pl.ds(lo, 32), :].astype(F32)
+                sq = x * x
+                acc_ref[pl.ds(lo, 32), :] = sum(sq[:, j : j + LANES] for j in range(0, cols, LANES))
+        for d in range(4):
+            at = pl.ds(pl.multiple_of(lax.rem(me + d, 4) * LANES, LANES), LANES)
+            if g < 2:
+                outs[d][g * rows : (g + 1) * rows] = got_ref[:, at].astype(outs[d].dtype)
+            else:
+                gates[d][...] = got_ref[:, at].astype(gates[d].dtype)
     acc = acc_ref[...]
     high = acc.astype(BF16)
     mid = (acc - high.astype(F32)).astype(BF16)
@@ -181,18 +194,10 @@
         high = value.astype(BF16).astype(F32)
         ext_ref[i : i + 1] = high
         ext_ref[2 + i : 3 + i] = value - high
-    me = lax.axis_index("fsdp")
-    for g in range(3):
-        w_copies[g].wait()
-        got_ref[...] = jnp.dot(xg_ref[...], w_ref[g], preferred_element_type=F32)
-        for d in range(4):
-            at = pl.ds(pl.multiple_of(lax.rem(me + d, 4) * LANES, LANES), LANES)
-            if g < 2:
-                outs[d][g * rows : (g + 1) * rows] = got_ref[:, at].astype(outs[d].dtype)
-            else:
-                gates[d][...] = got_ref[:, at].astype(gates[d].dtype)
-                ext_ref[4:6] = got_ref[rows - 2 : rows, at]
-                outs[d][2 * rows :] = ext_ref[...].astype(outs[d].dtype)
+    for d in range(4):
+        at = pl.ds(pl.multiple_of(lax.rem(me + d, 4) * LANES, LANES), LANES)
+        ext_ref[4:6] = got_ref[rows - 2 : rows, at]
+        outs[d][2 * rows :] = ext_ref[...].astype(outs[d].dtype)
 
 
 def local_kernel(sig_ref, skip_ref, h_ref, _, out_ref, pad_ref):
@@ -317,7 +322,7 @@
     return sums
 
 
-def gate_kernel(a_ref, b_ref, c_ref, d_ref, scale_ref, filt_ref, gate_ref, ext_ref):
+def gate_kernel(a_ref, b_ref, c_ref, d_ref, scale_ref, filt_ref, _, gate_ref, ext_ref):
     gate_ref[...] = stream((a_ref, b_ref, c_ref, d_ref), 0, scale_ref, filt_ref, 0, ext_ref)
 
 
@@ -477,7 +482,7 @@
     gate = call(
         gate_kernel,
         shape(rows, LANES),
-        (*gates, scale, filt),
+        (*gates, scale, filt, local_part),
         [pltpu.VMEM((TILE + rows, LANES), F32)],
         flops=1 << 24,
     )

time: 45 us -> 44.9 us (level)
  no operation moved by 1% of the time
where the time goes in v4:
time: 44.9 us; the launch traced here: 44.7 us
  starting transfers between devices  17.9 us (40%)
  blocking collectives  9.9 us (22%)
  waiting for transfers between devices  8.74 us (19%)
  Pallas kernels  8.02 us (18%)
    all_to_all x1, blocking collectives, body(): got = lax.all_to_all(send, 'seq', 0, 0, axis_index_groups=plane)  9.9 us
    ppermute x6, starting transfers between devices, exchange(): lax.ppermute(parts[d - 1], 'fsdp', [(i, (i + d) % fsdp) for i in range(fs...  9.43 us
    all_to_all x1, starting transfers between devices, body(): got = lax.all_to_all(send, 'seq', 0, 0, axis_index_groups=line)  8.46 us
    pallas_call x7, Pallas kernels, call(): pl.pallas_call(kernel, out_shape=out_shape, in_specs=places or [VMEM] * l...  8.02 us
    ppermute x6, waiting for transfers between devices, exchange(): lax.ppermute(parts[d - 1], 'fsdp', [(i, (i + d) % fsdp) for i in range(fs...  7.83 us
    all_to_all x1, waiting for transfers between devices, body(): got = lax.all_to_all(send, 'seq', 0, 0, axis_index_groups=line)  0.91 us
  transfers between devices with their start and end apart: 7, of which 6 were waited for; matrix products, arithmetic and copies ran while one was open for 0% of the time, Pallas kernels for 2%

profile of v4, /device:TPU:8, one launch (start us, length us, event | category | flops | bytes accessed | tf_op | source)
XLA Modules:
  0.0 44.7 jit_solution(16587256202068429835)
XLA Ops:
  0.0 0.0 copy-start.4
  0.0 0.0 copy-start.3
  0.0 0.0 copy-start.2
  0.0 0.0 copy-start.1
  0.0 0.0 copy-start
  0.0 4.6 %shard_map.82 = (f32[528,128]{1,0:T(8,128)S(1)}, bf16[528,128]{1,0:T(8,128)(2,1)S(1)}, bf16[528,128]{1,0:T(8,128)(2,1)S(1)}, bf16[528,128]{1,0:T(8,128)(2,1)S(1)...) custom-call(bf16[256,2048]{1,0:T(8,128)(2,1)} %tok_hbm.1, ...), custom_call_target="tpu_custom_call" | custom-call | flops 1610612736 | bytes 8351744 | tf_op jit(solution)/shard_map/pallas_call | solution.py:30
  4.6 1.6 %collective-permute-start = (bf16[528,128]{1,0:T(8,128)(2,1)S(1)}, bf16[528,128]{1,0:T(8,128)(2,1)S(1)}, u32[]{:S(2)}, u32[]{:S(2)}) collective-permute-start(bf16[528,128]{1,0:T(8,128)(2,1)S(1)} %get-tuple-element.32), channel_id=1, source_target_pairs={{0,64},{64,128},{128,192},{192,0},{1,65},{65,129},{129,193},{193,1... | collective-permute-start | bytes 405512 | tf_op jit(solution)/shard_map/ppermute | solution.py:409
  6.3 2.7 %collective-permute-start.1 = (bf16[528,128]{1,0:T(8,128)(2,1)S(1)}, bf16[528,128]{1,0:T(8,128)(2,1)S(1)}, u32[]{:S(2)}, u32[]{:S(2)}) collective-permute-start(bf16[528,128]{1,0:T(8,128)(2,1)S(1)} %get-tuple-element.33), channel_id=1, source_target_pairs={{0,128},{64,192},{128,0},{192,64},{1,129},{65,193},{129,1},{193,65... | collective-permute-start | bytes 405512 | tf_op jit(solution)/shard_map/ppermute | solution.py:409
  9.0 0.7 %collective-permute-start.2 = (bf16[528,128]{1,0:T(8,128)(2,1)S(1)}, bf16[528,128]{1,0:T(8,128)(2,1)S(1)}, u32[]{:S(2)}, u32[]{:S(2)}) collective-permute-start(bf16[528,128]{1,0:T(8,128)(2,1)S(1)} %get-tuple-element.34), channel_id=1, source_target_pairs={{0,192},{64,0},{128,64},{192,128},{1,193},{65,1},{129,65},{193,129... | collective-permute-start | bytes 405512 | tf_op jit(solution)/shard_map/ppermute | solution.py:409
  9.7 0.0 copy-done.4
  9.7 0.0 copy-done.3
  9.7 0.0 copy-done.2
  9.7 0.0 copy-done.1
  9.7 0.5 %shard_map.83 = (f32[8,2,16,128]{3,2,1,0:T(8,128)S(1)}, f32[16,2,8,128]{3,2,1,0:T(8,128)S(1)}, f32[16,2,8,128]{3,2,1,0:T(8,128)S(1)}, f32[4,2,16,128]{3,2,1,0:T(...) custom-call(f32[16,128]{1,0:T(8,128)S(1)} %bitcast.9, ...), custom_call_target="tpu_custom_call" | custom-call | flops 134217728 | bytes 1057280 | tf_op jit(solution)/shard_map/pallas_call | solution.py:30
  10.2 0.1 collective-permute-done.b_ref
  10.3 4.0 %collective-permute-done.1.c_ref = bf16[528,128]{1,0:T(8,128)(2,1)S(1)} collective-permute-done((bf16[528,128]{1,0:T(8,128)(2,1)S(1)}, bf16[528,128]{1,0:T(8,128)(2,1)S(1)}, u32[]{:S(2)}, u32[]{:S(2)}) %collective-permute-start.1) | collective-permute-done | bytes 135200 | tf_op jit(solution)/shard_map/ppermute | solution.py:409
  14.3 0.8 %collective-permute-done.2.d_ref = bf16[528,128]{1,0:T(8,128)(2,1)S(1)} collective-permute-done((bf16[528,128]{1,0:T(8,128)(2,1)S(1)}, bf16[528,128]{1,0:T(8,128)(2,1)S(1)}, u32[]{:S(2)}, u32[]{:S(2)}) %collective-permute-start.2) | collective-permute-done | bytes 135200 | tf_op jit(solution)/shard_map/ppermute | solution.py:409
  15.1 0.6 %shard_map.84 = (f32[256,128]{1,0:T(8,128)S(1)}, f32[256,128]{1,0:T(8,128)S(1)}, f32[4,2,16,128]{3,2,1,0:T(8,128)S(1)}, bf16[8,48,128]{2,1,0:T(8,128)(2,1)S(1)}, f32[8,128]{1,0:T(8,128)S(1)}) custom-call(f32[528,128]{1,0:T(8,128)S(1)} %get-tuple-element.31.a_ref, bf16[528,128]{1,0:T(8,128)(2,1)S(1)} %collective-permute-done.b_ref, ...), custom_call_target="tpu_custom_call" | custom-call | flops 134217728 | bytes 1438208 | tf_op jit(solution)/shard_map/pallas_call | solution.py:30
  15.7 9.9 %all_to_all.10.got_ref = bf16[8,48,128]{2,1,0:T(8,128)(2,1)S(1)} all-to-all(bf16[8,48,128]{2,1,0:T(8,128)(2,1)S(1)} %get-tuple-element.38), channel_id=1, replica_groups={{0,1,2,3,4,5,6,7},{8,9,10,11,12,13,14,15},{16,17,18,19,20,21,22,23},{24..., dimensions={0} | all-to-all | bytes 196608 | tf_op jit(solution)/shard_map/all_to_all | solution.py:467
  25.6 0.7 %shard_map.85 = (f32[2,16,128]{2,1,0:T(8,128)S(1)}, f32[2,8,128]{2,1,0:T(8,128)S(1)}, bf16[8,48,128]{2,1,0:T(8,128)(2,1)}) custom-call(bf16[8,48,128]{2,1,0:T(8,128)(2,1)S(1)} %all_to_all.10.got_ref, f32[8,2,16,128]{3,2,1,0:T(8,128)S(1)} %get-tuple-element.39.mine_tab_ref, f32[8,2,16,128]{3,2,1,0:T(8,128)S(1)} %get-tuple-element.40.all_tab_ref, ...), custom_call_target="tpu_custom_call" | custom-call | flops 16777216 | bytes 635392 | tf_op jit(solution)/shard_map/pallas_call | solution.py:30
  26.3 8.5 %all-to-all-start.1 = ((bf16[8,48,128]{2,1,0:T(8,128)(2,1)}), bf16[8,48,128]{2,1,0:T(8,128)(2,1)S(1)}, u32[]{:S(2)}, u32[]{:S(2)}) async-start(bf16[8,48,128]{2,1,0:T(8,128)(2,1)} %get-tuple-element.42), calls=%async_computation.1 | async-start | bytes 196608 | tf_op jit(solution)/shard_map/all_to_all | solution.py:490
  34.8 1.3 %collective-permute-start.3 = (bf16[256,128]{1,0:T(8,128)(2,1)S(1)}, bf16[256,128]{1,0:T(8,128)(2,1)S(1)}, u32[]{:S(2)}, u32[]{:S(2)}) collective-permute-start(bf16[256,128]{1,0:T(8,128)(2,1)S(1)} %get-tuple-element.49), channel_id=1, source_target_pairs={{0,64},{64,128},{128,192},{192,0},{1,65},{65,129},{129,193},{193,1... | collective-permute-start | bytes 196616 | tf_op jit(solution)/shard_map/ppermute | solution.py:409
  36.1 1.6 %collective-permute-start.4 = (bf16[256,128]{1,0:T(8,128)(2,1)S(1)}, bf16[256,128]{1,0:T(8,128)(2,1)S(1)}, u32[]{:S(2)}, u32[]{:S(2)}) collective-permute-start(bf16[256,128]{1,0:T(8,128)(2,1)S(1)} %get-tuple-element.50), channel_id=1, source_target_pairs={{0,128},{64,192},{128,0},{192,64},{1,129},{65,193},{129,1},{193,65... | collective-permute-start | bytes 196616 | tf_op jit(solution)/shard_map/ppermute | solution.py:409
  37.6 1.6 %collective-permute-start.5 = (bf16[256,128]{1,0:T(8,128)(2,1)S(1)}, bf16[256,128]{1,0:T(8,128)(2,1)S(1)}, u32[]{:S(2)}, u32[]{:S(2)}) collective-permute-start(bf16[256,128]{1,0:T(8,128)(2,1)S(1)} %get-tuple-element.51), channel_id=1, source_target_pairs={{0,192},{64,0},{128,64},{192,128},{1,193},{65,1},{129,65},{193,129... | collective-permute-start | bytes 196616 | tf_op jit(solution)/shard_map/ppermute | solution.py:409
  39.2 0.0 copy-done
  39.2 0.3 shard_map.86._.local_ref
  39.5 0.0 collective-permute-done.3.b_ref
  39.6 2.3 %collective-permute-done.4.c_ref = bf16[256,128]{1,0:T(8,128)(2,1)S(1)} collective-permute-done((bf16[256,128]{1,0:T(8,128)(2,1)S(1)}, bf16[256,128]{1,0:T(8,128)(2,1)S(1)}, u32[]{:S(2)}, u32[]{:S(2)}) %collective-permute-start.4) | collective-permute-done | bytes 65568 | tf_op jit(solution)/shard_map/ppermute | solution.py:409
  41.9 0.6 %collective-permute-done.5.d_ref = bf16[256,128]{1,0:T(8,128)(2,1)S(1)} collective-permute-done((bf16[256,128]{1,0:T(8,128)(2,1)S(1)}, bf16[256,128]{1,0:T(8,128)(2,1)S(1)}, u32[]{:S(2)}, u32[]{:S(2)}) %collective-permute-start.5) | collective-permute-done | bytes 65568 | tf_op jit(solution)/shard_map/ppermute | solution.py:409
  42.5 0.1 shard_map.87.gate_ref
  42.6 0.9 %all-to-all-done.1.got_ref = bf16[8,48,128]{2,1,0:T(8,128)(2,1)S(1)} async-done(((bf16[8,48,128]{2,1,0:T(8,128)(2,1)}), bf16[8,48,128]{2,1,0:T(8,128)(2,1)S(1)}, u32[]{:S(2)}, u32[]{:S(2)}) %all-to-all-start.1) | async-done | bytes 98336 | tf_op jit(solution)/shard_map/all_to_all | solution.py:490
  43.5 1.1 %shard_map.88 = bf16[128,256]{1,0:T(8,128)(2,1)} custom-call(bf16[8,48,128]{2,1,0:T(8,128)(2,1)S(1)} %all-to-all-done.1.got_ref, f32[8,2,16,128]{3,2,1,0:T(8,128)S(1)} %get-tuple-element.43.far_tab_ref, f32[2,8,128]{2,1,0:T(8,128)S(1)} %get-tuple-element.44._.rim_ref, f32[9,2,16,128]{3,2,1,0:T(8,128)S(1)} %get-tuple-element.41.plane_ref, ...), custom_call_target="tpu_custom_call" | custom-call | flops 134217728 | bytes 1132032 | tf_op jit(solution)/shard_map/pallas_call | solution.py:30
  (1 shorter events, 0.0 us)
Async XLA Ops:
  0.0 9.7 %copy-start.4 = (f32[128,3,3]{0,2,1:T(4,128)S(1)}, f32[128,3,3]{0,2,1:T(4,128)}, u32[]{:S(2)}) copy-start(f32[128,3,3]{0,2,1:T(4,128)} %param.11) | copy-start | bytes 13828
  0.0 9.7 %copy-start.3 = (f32[128,16]{0,1:T(8,128)S(1)}, f32[128,16]{0,1:T(8,128)}, u32[]{:S(2)}) copy-start(f32[128,16]{0,1:T(8,128)} %param.14) | copy-start | bytes 24580
  0.0 9.7 %copy-start.2 = (f32[128,16]{0,1:T(8,128)S(1)}, f32[128,16]{0,1:T(8,128)}, u32[]{:S(2)}) copy-start(f32[128,16]{0,1:T(8,128)} %param.13) | copy-start | bytes 24580
  0.0 9.7 %copy-start.1 = (f32[128,16]{0,1:T(8,128)S(1)}, f32[128,16]{0,1:T(8,128)}, u32[]{:S(2)}) copy-start(f32[128,16]{0,1:T(8,128)} %param.12) | copy-start | bytes 24580
  0.0 39.2 %copy-start = (f32[128]{0:T(128)S(1)}, f32[128]{0:T(128)}, u32[]{:S(2)}) copy-start(f32[128]{0:T(128)} %param.15) | copy-start | bytes 1540
  4.6 5.6 %collective-permute-start = (bf16[528,128]{1,0:T(8,128)(2,1)S(1)}, bf16[528,128]{1,0:T(8,128)(2,1)S(1)}, u32[]{:S(2)}, u32[]{:S(2)}) collective-permute-start(bf16[528,128]{1,0:T(8,128)(2,1)S(1)} %get-tuple-element.32), channel_id=1, source_target_pairs={{0,64},{64,128},{128,192},{192,0},{1,65},{65,129},{129,193},{193,1... | collective-permute-start | bytes 405512 | tf_op jit(solution)/shard_map/ppermute | solution.py:409
  6.3 8.0 %collective-permute-start.1 = (bf16[528,128]{1,0:T(8,128)(2,1)S(1)}, bf16[528,128]{1,0:T(8,128)(2,1)S(1)}, u32[]{:S(2)}, u32[]{:S(2)}) collective-permute-start(bf16[528,128]{1,0:T(8,128)(2,1)S(1)} %get-tuple-element.33), channel_id=1, source_target_pairs={{0,128},{64,192},{128,0},{192,64},{1,129},{65,193},{129,1},{193,65... | collective-permute-start | bytes 405512 | tf_op jit(solution)/shard_map/ppermute | solution.py:409
  9.0 6.1 %collective-permute-start.2 = (bf16[528,128]{1,0:T(8,128)(2,1)S(1)}, bf16[528,128]{1,0:T(8,128)(2,1)S(1)}, u32[]{:S(2)}, u32[]{:S(2)}) collective-permute-start(bf16[528,128]{1,0:T(8,128)(2,1)S(1)} %get-tuple-element.34), channel_id=1, source_target_pairs={{0,192},{64,0},{128,64},{192,128},{1,193},{65,1},{129,65},{193,129... | collective-permute-start | bytes 405512 | tf_op jit(solution)/shard_map/ppermute | solution.py:409
  26.3 17.2 %all-to-all-start.1 = ((bf16[8,48,128]{2,1,0:T(8,128)(2,1)}), bf16[8,48,128]{2,1,0:T(8,128)(2,1)S(1)}, u32[]{:S(2)}, u32[]{:S(2)}) async-start(bf16[8,48,128]{2,1,0:T(8,128)(2,1)} %get-tuple-element.42), calls=%async_computation.1 | async-start | bytes 196608 | tf_op jit(solution)/shard_map/all_to_all | solution.py:490
  34.8 4.8 %collective-permute-start.3 = (bf16[256,128]{1,0:T(8,128)(2,1)S(1)}, bf16[256,128]{1,0:T(8,128)(2,1)S(1)}, u32[]{:S(2)}, u32[]{:S(2)}) collective-permute-start(bf16[256,128]{1,0:T(8,128)(2,1)S(1)} %get-tuple-element.49), channel_id=1, source_target_pairs={{0,64},{64,128},{128,192},{192,0},{1,65},{65,129},{129,193},{193,1... | collective-permute-start | bytes 196616 | tf_op jit(solution)/shard_map/ppermute | solution.py:409
  36.1 5.8 %collective-permute-start.4 = (bf16[256,128]{1,0:T(8,128)(2,1)S(1)}, bf16[256,128]{1,0:T(8,128)(2,1)S(1)}, u32[]{:S(2)}, u32[]{:S(2)}) collective-permute-start(bf16[256,128]{1,0:T(8,128)(2,1)S(1)} %get-tuple-element.50), channel_id=1, source_target_pairs={{0,128},{64,192},{128,0},{192,64},{1,129},{65,193},{129,1},{193,65... | collective-permute-start | bytes 196616 | tf_op jit(solution)/shard_map/ppermute | solution.py:409
  37.6 4.9 %collective-permute-start.5 = (bf16[256,128]{1,0:T(8,128)(2,1)S(1)}, bf16[256,128]{1,0:T(8,128)(2,1)S(1)}, u32[]{:S(2)}, u32[]{:S(2)}) collective-permute-start(bf16[256,128]{1,0:T(8,128)(2,1)S(1)} %get-tuple-element.51), channel_id=1, source_target_pairs={{0,192},{64,0},{128,64},{192,128},{1,193},{65,1},{129,65},{193,129... | collective-permute-start | bytes 196616 | tf_op jit(solution)/shard_map/ppermute | solution.py:409

commit v5 on v4

--- a/solution.py
+++ b/solution.py
@@ -280,9 +280,7 @@
         state = (state[0] + u_ref[q, 0], state[1] + u_ref[q, 1])
     for c in range(2):
         wire_ref[MODES * c : MODES * (c + 1)] = state[c]
-    wire = wire_ref[...].astype(send_ref.dtype)
-    for i in range(LOW):
-        send_ref[i] = wire
+    send_ref[...] = wire_ref[...].astype(send_ref.dtype)
 
 
 def edges(filt_ref, first, rim):
@@ -306,11 +304,10 @@
     return [plane_ref[at, c] * pair[0] + plane_ref[at + 1, c] * pair[1] for c in range(2)]
 
 
-def gathered(got_ref, wide_ref, plane_ref, at, filt_ref, tables, alone):
+def gathered(wide_ref, plane_ref, at, filt_ref, tables, alone):
     zero = jnp.zeros((MODES, LANES), F32)
     sums = [[zero, zero] for _ in tables]
-    for i in range(got_ref.shape[0]):
-        wide_ref[i] = got_ref[i].astype(F32)
+    for i in range(wide_ref.shape[0]):
         value = [wide_ref[i, 0:MODES], wide_ref[i, MODES:HEAD]]
         if i or alone:
             rim = lines(wide_ref.at[i - 1], TAIL, 4) if i else [0.0] * 4
@@ -326,9 +323,17 @@
     gate_ref[...] = stream((a_ref, b_ref, c_ref, d_ref), 0, scale_ref, filt_ref, 0, ext_ref)
 
 
-def plane_kernel(got_ref, mine_tab_ref, all_tab_ref, plane_ref, filt_ref, mine_ref, rim_ref, send_ref, wide_ref, wire_ref):
-    mine, total = gathered(got_ref, wide_ref, plane_ref, 3, filt_ref, (mine_tab_ref, all_tab_ref), False)
+def plane_kernel(
+    here_ref, next_ref, across_ref, before_ref, mine_tab_ref, all_tab_ref, plane_ref, filt_ref,
+    mine_ref, rim_ref, send_ref, wide_ref, wire_ref,
+):
     place = lax.rem(lax.axis_index("seq"), LOW)
+    chip, core = lax.div(place, 2), lax.rem(place, 2)
+    for i, ref in enumerate((here_ref, next_ref, across_ref, before_ref)):
+        first = 2 * lax.rem(chip + i, LOW // 2)
+        wide_ref[first + core] = ref[0].astype(F32)
+        wide_ref[first + 1 - core] = ref[1].astype(F32)
+    mine, total = gathered(wide_ref, plane_ref, 3, filt_ref, (mine_tab_ref, all_tab_ref), False)
     near = wide_ref[jnp.maximum(place - 1, 0), TAIL : TAIL + TILE]
     rim_ref[0] = jnp.where(place > 0, near, 0.0)
     rim_ref[1] = wide_ref[0, HEAD : HEAD + TILE]
@@ -348,7 +353,9 @@
 ):
     rows = gate_ref.shape[0]
     subs = rows // SUB
-    (far,) = gathered(got_ref, wide_ref, plane_ref, 5, filt_ref, (far_tab_ref,), True)
+    for i in range(PLANES):
+        wide_ref[i] = got_ref[i].astype(F32)
+    (far,) = gathered(wide_ref, plane_ref, 5, filt_ref, (far_tab_ref,), True)
     far = cmul(far, (plane_ref[0, 0], plane_ref[0, 1]))
     block = lax.axis_index("seq")
     place, plane = lax.rem(block, LOW), lax.div(block, LOW)
@@ -454,7 +461,10 @@
     wire = shape(LOW, WIRE, LANES, dtype=BF16)
     scale, signal, carry, send, head = call(
         signal_kernel,
-        (shape(rows, LANES), shape(rows, LANES), shape(4, 2, MODES, LANES), wire, shape(TILE, LANES)),
+        (
+            shape(rows, LANES), shape(rows, LANES), shape(4, 2, MODES, LANES),
+            shape(WIRE, LANES, dtype=BF16), shape(TILE, LANES),
+        ),
         (*pair, filt, p8, r7, p64),
         [
             pltpu.VMEM((2, TILE + rows, LANES), F32),
@@ -463,12 +473,17 @@
         ],
         flops=1 << 27,
     )
-    plane = [[LOW * g + j for j in range(LOW)] for g in range(PLANES)]
-    got = lax.all_to_all(send, "seq", 0, 0, axis_index_groups=plane)
+    blocks = range(LOW * PLANES)
+    here = jnp.stack([send, lax.ppermute(send, "seq", [(i, i ^ 1) for i in blocks])])
+
+    def ahead(d):
+        return lax.ppermute(here, "seq", [(i, i // LOW * LOW + (i - 2 * d) % LOW) for i in blocks])
+
+    near = [ahead(d) for d in (2, 1, 3)]
     mine, rim, send = call(
         plane_kernel,
         (state, shape(2, TILE, LANES), wire),
-        (got, mine_tab, all_tab, plane_tab, filt),
+        (here, near[1], near[0], near[2], mine_tab, all_tab, plane_tab, filt),
         [pltpu.VMEM((LOW, WIRE, LANES), F32), pltpu.VMEM((WIRE, LANES), F32)],
         flops=1 << 24,
     )

time: 44.9 us -> 44.5 us (level)
  blocking collectives: 9.9 us -> 0 us
  starting transfers between devices: 17.9 us -> 23.6 us
  waiting for transfers between devices: 8.74 us -> 12.3 us
    all_to_all x1 -> x0, blocking collectives: 9.9 us -> none  [body(): got = lax.all_to_all(send, 'seq', 0, 0, axis_index_groups=plane)]
    ppermute x0 -> x4, starting transfers between devices: none -> 5.75 us  [the longest x3 5.66 us: ahead(): lax.ppermute(here, 'seq', [(i, i // LOW * LOW + (i - 2 * d) % LOW) for i...]
    ppermute x0 -> x4, waiting for transfers between devices: none -> 3.55 us  [the longest x3 2.39 us: ahead(): lax.ppermute(here, 'seq', [(i, i // LOW * LOW + (i - 2 * d) % LOW) for i...]
  transfers between devices with their start and end apart: 7 -> 11, of which waited for: 6 -> 9; matrix products, arithmetic and copies ran while one was open for 0% -> 0% of each run, Pallas kernels for 2% -> 2%
where the time goes in v5:
time: 44.5 us; the launch traced here: 44.1 us
  starting transfers between devices  23.6 us (53%)
  waiting for transfers between devices  12.3 us (28%)
  Pallas kernels  8.01 us (18%)
    ppermute x6, starting transfers between devices, exchange(): lax.ppermute(parts[d - 1], 'fsdp', [(i, (i + d) % fsdp) for i in range(fs...  9.43 us
    all_to_all x1, starting transfers between devices, body(): got = lax.all_to_all(send, 'seq', 0, 0, axis_index_groups=line)  8.47 us
    pallas_call x7, Pallas kernels, call(): pl.pallas_call(kernel, out_shape=out_shape, in_specs=places or [VMEM] * l...  8.01 us
    ppermute x6, waiting for transfers between devices, exchange(): lax.ppermute(parts[d - 1], 'fsdp', [(i, (i + d) % fsdp) for i in range(fs...  7.83 us
    ppermute x3, starting transfers between devices, ahead(): lax.ppermute(here, 'seq', [(i, i // LOW * LOW + (i - 2 * d) % LOW) for i...  5.66 us
    ppermute x3, waiting for transfers between devices, ahead(): lax.ppermute(here, 'seq', [(i, i // LOW * LOW + (i - 2 * d) % LOW) for i...  2.39 us
    ppermute x1, waiting for transfers between devices, body(): lax.ppermute(send, 'seq', [(i, i ^ 1) for i in blocks])  1.16 us
    all_to_all x1, waiting for transfers between devices, body(): got = lax.all_to_all(send, 'seq', 0, 0, axis_index_groups=line)  0.91 us
  transfers between devices with their start and end apart: 11, of which 9 were waited for; matrix products, arithmetic and copies ran while one was open for 0% of the time, Pallas kernels for 2%

profile of v5, /device:TPU:8, one launch (start us, length us, event | category | flops | bytes accessed | tf_op | source)
XLA Modules:
  0.0 44.1 jit_solution(8105792846364506990)
XLA Ops:
  0.0 0.0 copy-start.1
  0.0 0.0 copy-start
  0.0 4.6 %shard_map.82 = (f32[528,128]{1,0:T(8,128)S(1)}, bf16[528,128]{1,0:T(8,128)(2,1)S(1)}, bf16[528,128]{1,0:T(8,128)(2,1)S(1)}, bf16[528,128]{1,0:T(8,128)(2,1)S(1)...) custom-call(bf16[256,2048]{1,0:T(8,128)(2,1)} %tok_hbm.1, ...), custom_call_target="tpu_custom_call" | custom-call | flops 1610612736 | bytes 8351744 | tf_op jit(solution)/shard_map/pallas_call | solution.py:30
  4.6 1.6 %collective-permute-start = (bf16[528,128]{1,0:T(8,128)(2,1)S(1)}, bf16[528,128]{1,0:T(8,128)(2,1)S(1)}, u32[]{:S(2)}, u32[]{:S(2)}) collective-permute-start(bf16[528,128]{1,0:T(8,128)(2,1)S(1)} %get-tuple-element.32), channel_id=1, source_target_pairs={{0,64},{64,128},{128,192},{192,0},{1,65},{65,129},{129,193},{193,1... | collective-permute-start | bytes 405512 | tf_op jit(solution)/shard_map/ppermute | solution.py:416
  6.3 2.7 %collective-permute-start.1 = (bf16[528,128]{1,0:T(8,128)(2,1)S(1)}, bf16[528,128]{1,0:T(8,128)(2,1)S(1)}, u32[]{:S(2)}, u32[]{:S(2)}) collective-permute-start(bf16[528,128]{1,0:T(8,128)(2,1)S(1)} %get-tuple-element.33), channel_id=1, source_target_pairs={{0,128},{64,192},{128,0},{192,64},{1,129},{65,193},{129,1},{193,65... | collective-permute-start | bytes 405512 | tf_op jit(solution)/shard_map/ppermute | solution.py:416
  9.0 0.7 %collective-permute-start.2 = (bf16[528,128]{1,0:T(8,128)(2,1)S(1)}, bf16[528,128]{1,0:T(8,128)(2,1)S(1)}, u32[]{:S(2)}, u32[]{:S(2)}) collective-permute-start(bf16[528,128]{1,0:T(8,128)(2,1)S(1)} %get-tuple-element.34), channel_id=1, source_target_pairs={{0,192},{64,0},{128,64},{192,128},{1,193},{65,1},{129,65},{193,129... | collective-permute-start | bytes 405512 | tf_op jit(solution)/shard_map/ppermute | solution.py:416
  9.7 0.0 copy-done.3
  9.7 0.5 %shard_map.83 = (f32[8,2,16,128]{3,2,1,0:T(8,128)S(1)}, f32[16,2,8,128]{3,2,1,0:T(8,128)S(1)}, f32[16,2,8,128]{3,2,1,0:T(8,128)S(1)}, f32[4,2,16,128]{3,2,1,0:T(...) custom-call(f32[16,128]{1,0:T(8,128)S(1)} %bitcast.12, ...), custom_call_target="tpu_custom_call" | custom-call | flops 134217728 | bytes 1057280 | tf_op jit(solution)/shard_map/pallas_call | solution.py:30
  10.2 0.1 collective-permute-done.b_ref
  10.3 4.0 %collective-permute-done.1.c_ref = bf16[528,128]{1,0:T(8,128)(2,1)S(1)} collective-permute-done((bf16[528,128]{1,0:T(8,128)(2,1)S(1)}, bf16[528,128]{1,0:T(8,128)(2,1)S(1)}, u32[]{:S(2)}, u32[]{:S(2)}) %collective-permute-start.1) | collective-permute-done | bytes 135200 | tf_op jit(solution)/shard_map/ppermute | solution.py:416
  14.3 0.8 %collective-permute-done.2.d_ref = bf16[528,128]{1,0:T(8,128)(2,1)S(1)} collective-permute-done((bf16[528,128]{1,0:T(8,128)(2,1)S(1)}, bf16[528,128]{1,0:T(8,128)(2,1)S(1)}, u32[]{:S(2)}, u32[]{:S(2)}) %collective-permute-start.2) | collective-permute-done | bytes 135200 | tf_op jit(solution)/shard_map/ppermute | solution.py:416
  15.1 0.6 %shard_map.84 = (f32[256,128]{1,0:T(8,128)S(1)}, f32[256,128]{1,0:T(8,128)S(1)}, f32[4,2,16,128]{3,2,1,0:T(8,128)S(1)}, bf16[48,128]{1,0:T(8,128)(2,1)S(1)}, f32[8,128]{1,0:T(8,128)S(1)}) custom-call(f32[528,128]{1,0:T(8,128)S(1)} %get-tuple-element.31.a_ref, bf16[528,128]{1,0:T(8,128)(2,1)S(1)} %collective-permute-done.b_ref, ...), custom_call_target="tpu_custom_call" | custom-call | flops 134217728 | bytes 1352192 | tf_op jit(solution)/shard_map/pallas_call | solution.py:30
  15.7 0.1 collective-permute-start.3
  15.8 1.2 %collective-permute-done.3 = bf16[48,128]{1,0:T(8,128)(2,1)S(1)} collective-permute-done((bf16[48,128]{1,0:T(8,128)(2,1)S(1)}, bf16[48,128]{1,0:T(8,128)(2,1)S(1)}, u32[]{:S(2)}, u32[]{:S(2)}) %collective-permute-start.3) | collective-permute-done | bytes 12320 | tf_op jit(solution)/shard_map/ppermute | solution.py:477
  16.9 1.5 %collective-permute-start.6 = (bf16[2,48,128]{2,1,0:T(8,128)(2,1)S(1)}, bf16[2,48,128]{2,1,0:T(8,128)(2,1)S(1)}, u32[]{:S(2)}, u32[]{:S(2)}) collective-permute-start(bf16[2,48,128]{2,1,0:T(8,128)(2,1)S(1)} %pad_maximum_fusion.here_ref), channel_id=1, source_target_pairs={{0,2},{1,3},{2,4},{3,5},{4,6},{5,7},{6,0},{7,1},{8,10},{9,11},{10,... | collective-permute-start | bytes 73736 | tf_op jit(solution)/shard_map/ppermute | solution.py:480
  18.4 2.7 %collective-permute-start.5 = (bf16[2,48,128]{2,1,0:T(8,128)(2,1)S(1)}, bf16[2,48,128]{2,1,0:T(8,128)(2,1)S(1)}, u32[]{:S(2)}, u32[]{:S(2)}) collective-permute-start(bf16[2,48,128]{2,1,0:T(8,128)(2,1)S(1)} %pad_maximum_fusion.here_ref), channel_id=1, source_target_pairs={{0,4},{1,5},{2,6},{3,7},{4,0},{5,1},{6,2},{7,3},{8,12},{9,13},{10,... | collective-permute-start | bytes 73736 | tf_op jit(solution)/shard_map/ppermute | solution.py:480
  21.2 1.4 %collective-permute-start.4 = (bf16[2,48,128]{2,1,0:T(8,128)(2,1)S(1)}, bf16[2,48,128]{2,1,0:T(8,128)(2,1)S(1)}, u32[]{:S(2)}, u32[]{:S(2)}) collective-permute-start(bf16[2,48,128]{2,1,0:T(8,128)(2,1)S(1)} %pad_maximum_fusion.here_ref), channel_id=1, source_target_pairs={{0,6},{1,7},{2,0},{3,1},{4,2},{5,3},{6,4},{7,5},{8,14},{9,15},{10,... | collective-permute-start | bytes 73736 | tf_op jit(solution)/shard_map/ppermute | solution.py:480
  22.6 0.0 collective-permute-done.6.before_ref
  22.6 1.2 %collective-permute-done.5.across_ref = bf16[2,48,128]{2,1,0:T(8,128)(2,1)S(1)} collective-permute-done((bf16[2,48,128]{2,1,0:T(8,128)(2,1)S(1)}, bf16[2,48,128]{2,1,0:T(8,128)(2,1)S(1)}, u32[]{:S(2)}, u32[]{:S(2)}) %collective-permute-start.5) | collective-permute-done | bytes 24608 | tf_op jit(solution)/shard_map/ppermute | solution.py:480
  23.8 1.2 %collective-permute-done.4.next_ref = bf16[2,48,128]{2,1,0:T(8,128)(2,1)S(1)} collective-permute-done((bf16[2,48,128]{2,1,0:T(8,128)(2,1)S(1)}, bf16[2,48,128]{2,1,0:T(8,128)(2,1)S(1)}, u32[]{:S(2)}, u32[]{:S(2)}) %collective-permute-start.4) | collective-permute-done | bytes 24608 | tf_op jit(solution)/shard_map/ppermute | solution.py:480
  25.0 0.7 %shard_map.85 = (f32[2,16,128]{2,1,0:T(8,128)S(1)}, f32[2,8,128]{2,1,0:T(8,128)S(1)}, bf16[8,48,128]{2,1,0:T(8,128)(2,1)}) custom-call(bf16[2,48,128]{2,1,0:T(8,128)(2,1)S(1)} %pad_maximum_fusion.here_ref, bf16[2,48,128]{2,1,0:T(8,128)(2,1)S(1)} %collective-permute-done.4.next_ref, bf16[2,48,128]{2,1,0:T(8,128)(2,1)S(1)} %collective-permute-done.5.across_ref, ...), custom_call_target="tpu_custom_call" | custom-call | flops 16777216 | bytes 635392 | tf_op jit(solution)/shard_map/pallas_call | solution.py:30
  25.7 8.5 %all-to-all-start = ((bf16[8,48,128]{2,1,0:T(8,128)(2,1)}), bf16[8,48,128]{2,1,0:T(8,128)(2,1)S(1)}, u32[]{:S(2)}, u32[]{:S(2)}) async-start(bf16[8,48,128]{2,1,0:T(8,128)(2,1)} %get-tuple-element.42), calls=%async_computation | async-start | bytes 196608 | tf_op jit(solution)/shard_map/all_to_all | solution.py:505
  34.2 1.3 %collective-permute-start.7 = (bf16[256,128]{1,0:T(8,128)(2,1)S(1)}, bf16[256,128]{1,0:T(8,128)(2,1)S(1)}, u32[]{:S(2)}, u32[]{:S(2)}) collective-permute-start(bf16[256,128]{1,0:T(8,128)(2,1)S(1)} %get-tuple-element.49), channel_id=1, source_target_pairs={{0,64},{64,128},{128,192},{192,0},{1,65},{65,129},{129,193},{193,1... | collective-permute-start | bytes 196616 | tf_op jit(solution)/shard_map/ppermute | solution.py:416
  35.5 1.6 %collective-permute-start.8 = (bf16[256,128]{1,0:T(8,128)(2,1)S(1)}, bf16[256,128]{1,0:T(8,128)(2,1)S(1)}, u32[]{:S(2)}, u32[]{:S(2)}) collective-permute-start(bf16[256,128]{1,0:T(8,128)(2,1)S(1)} %get-tuple-element.50), channel_id=1, source_target_pairs={{0,128},{64,192},{128,0},{192,64},{1,129},{65,193},{129,1},{193,65... | collective-permute-start | bytes 196616 | tf_op jit(solution)/shard_map/ppermute | solution.py:416
  37.1 1.6 %collective-permute-start.9 = (bf16[256,128]{1,0:T(8,128)(2,1)S(1)}, bf16[256,128]{1,0:T(8,128)(2,1)S(1)}, u32[]{:S(2)}, u32[]{:S(2)}) collective-permute-start(bf16[256,128]{1,0:T(8,128)(2,1)S(1)} %get-tuple-element.51), channel_id=1, source_target_pairs={{0,192},{64,0},{128,64},{192,128},{1,193},{65,1},{129,65},{193,129... | collective-permute-start | bytes 196616 | tf_op jit(solution)/shard_map/ppermute | solution.py:416
  38.6 0.3 shard_map.86._.local_ref
  39.0 0.0 collective-permute-done.7.b_ref
  39.0 2.3 %collective-permute-done.8.c_ref = bf16[256,128]{1,0:T(8,128)(2,1)S(1)} collective-permute-done((bf16[256,128]{1,0:T(8,128)(2,1)S(1)}, bf16[256,128]{1,0:T(8,128)(2,1)S(1)}, u32[]{:S(2)}, u32[]{:S(2)}) %collective-permute-start.8) | collective-permute-done | bytes 65568 | tf_op jit(solution)/shard_map/ppermute | solution.py:416
  41.3 0.6 %collective-permute-done.9.d_ref = bf16[256,128]{1,0:T(8,128)(2,1)S(1)} collective-permute-done((bf16[256,128]{1,0:T(8,128)(2,1)S(1)}, bf16[256,128]{1,0:T(8,128)(2,1)S(1)}, u32[]{:S(2)}, u32[]{:S(2)}) %collective-permute-start.9) | collective-permute-done | bytes 65568 | tf_op jit(solution)/shard_map/ppermute | solution.py:416
  41.9 0.1 shard_map.87.gate_ref
  42.0 0.9 %all-to-all-done.got_ref = bf16[8,48,128]{2,1,0:T(8,128)(2,1)S(1)} async-done(((bf16[8,48,128]{2,1,0:T(8,128)(2,1)}), bf16[8,48,128]{2,1,0:T(8,128)(2,1)S(1)}, u32[]{:S(2)}, u32[]{:S(2)}) %all-to-all-start) | async-done | bytes 98336 | tf_op jit(solution)/shard_map/all_to_all | solution.py:505
  42.9 1.1 %shard_map.88 = bf16[128,256]{1,0:T(8,128)(2,1)} custom-call(bf16[8,48,128]{2,1,0:T(8,128)(2,1)S(1)} %all-to-all-done.got_ref, f32[8,2,16,128]{3,2,1,0:T(8,128)S(1)} %get-tuple-element.43.far_tab_ref, f32[2,8,128]{2,1,0:T(8,128)S(1)} %get-tuple-element.44._.rim_ref, f32[9,2,16,128]{3,2,1,0:T(8,128)S(1)} %get-tuple-element.41.plane_ref, ...), custom_call_target="tpu_custom_call" | custom-call | flops 134217728 | bytes 1132032 | tf_op jit(solution)/shard_map/pallas_call | solution.py:30
  (9 shorter events, 0.0 us)
Async XLA Ops:
  0.0 9.7 %copy-start.4 = (f32[128,3,3]{0,2,1:T(4,128)S(1)}, f32[128,3,3]{0,2,1:T(4,128)}, u32[]{:S(2)}) copy-start(f32[128,3,3]{0,2,1:T(4,128)} %param.11) | copy-start | bytes 13828
  0.0 9.7 %copy-start.3 = (f32[128,16]{0,1:T(8,128)S(1)}, f32[128,16]{0,1:T(8,128)}, u32[]{:S(2)}) copy-start(f32[128,16]{0,1:T(8,128)} %param.14) | copy-start | bytes 24580
  0.0 9.7 %copy-start.2 = (f32[128,16]{0,1:T(8,128)S(1)}, f32[128,16]{0,1:T(8,128)}, u32[]{:S(2)}) copy-start(f32[128,16]{0,1:T(8,128)} %param.13) | copy-start | bytes 24580
  0.0 9.7 %copy-start.1 = (f32[128,16]{0,1:T(8,128)S(1)}, f32[128,16]{0,1:T(8,128)}, u32[]{:S(2)}) copy-start(f32[128,16]{0,1:T(8,128)} %param.12) | copy-start | bytes 24580
  0.0 38.6 %copy-start = (f32[128]{0:T(128)S(1)}, f32[128]{0:T(128)}, u32[]{:S(2)}) copy-start(f32[128]{0:T(128)} %param.15) | copy-start | bytes 1540
  4.6 5.6 %collective-permute-start = (bf16[528,128]{1,0:T(8,128)(2,1)S(1)}, bf16[528,128]{1,0:T(8,128)(2,1)S(1)}, u32[]{:S(2)}, u32[]{:S(2)}) collective-permute-start(bf16[528,128]{1,0:T(8,128)(2,1)S(1)} %get-tuple-element.32), channel_id=1, source_target_pairs={{0,64},{64,128},{128,192},{192,0},{1,65},{65,129},{129,193},{193,1... | collective-permute-start | bytes 405512 | tf_op jit(solution)/shard_map/ppermute | solution.py:416
  6.3 8.0 %collective-permute-start.1 = (bf16[528,128]{1,0:T(8,128)(2,1)S(1)}, bf16[528,128]{1,0:T(8,128)(2,1)S(1)}, u32[]{:S(2)}, u32[]{:S(2)}) collective-permute-start(bf16[528,128]{1,0:T(8,128)(2,1)S(1)} %get-tuple-element.33), channel_id=1, source_target_pairs={{0,128},{64,192},{128,0},{192,64},{1,129},{65,193},{129,1},{193,65... | collective-permute-start | bytes 405512 | tf_op jit(solution)/shard_map/ppermute | solution.py:416
  9.0 6.1 %collective-permute-start.2 = (bf16[528,128]{1,0:T(8,128)(2,1)S(1)}, bf16[528,128]{1,0:T(8,128)(2,1)S(1)}, u32[]{:S(2)}, u32[]{:S(2)}) collective-permute-start(bf16[528,128]{1,0:T(8,128)(2,1)S(1)} %get-tuple-element.34), channel_id=1, source_target_pairs={{0,192},{64,0},{128,64},{192,128},{1,193},{65,1},{129,65},{193,129... | collective-permute-start | bytes 405512 | tf_op jit(solution)/shard_map/ppermute | solution.py:416
  15.7 1.3 %collective-permute-start.3 = (bf16[48,128]{1,0:T(8,128)(2,1)S(1)}, bf16[48,128]{1,0:T(8,128)(2,1)S(1)}, u32[]{:S(2)}, u32[]{:S(2)}) collective-permute-start(bf16[48,128]{1,0:T(8,128)(2,1)S(1)} %get-tuple-element.38), channel_id=1, source_target_pairs={{0,1},{1,0},{2,3},{3,2},{4,5},{5,4},{6,7},{7,6},{8,9},{9,8},{10,11... | collective-permute-start | bytes 36872 | tf_op jit(solution)/shard_map/ppermute | solution.py:477
  16.9 5.7 %collective-permute-start.6 = (bf16[2,48,128]{2,1,0:T(8,128)(2,1)S(1)}, bf16[2,48,128]{2,1,0:T(8,128)(2,1)S(1)}, u32[]{:S(2)}, u32[]{:S(2)}) collective-permute-start(bf16[2,48,128]{2,1,0:T(8,128)(2,1)S(1)} %pad_maximum_fusion.here_ref), channel_id=1, source_target_pairs={{0,2},{1,3},{2,4},{3,5},{4,6},{5,7},{6,0},{7,1},{8,10},{9,11},{10,... | collective-permute-start | bytes 73736 | tf_op jit(solution)/shard_map/ppermute | solution.py:480
  18.4 5.3 %collective-permute-start.5 = (bf16[2,48,128]{2,1,0:T(8,128)(2,1)S(1)}, bf16[2,48,128]{2,1,0:T(8,128)(2,1)S(1)}, u32[]{:S(2)}, u32[]{:S(2)}) collective-permute-start(bf16[2,48,128]{2,1,0:T(8,128)(2,1)S(1)} %pad_maximum_fusion.here_ref), channel_id=1, source_target_pairs={{0,4},{1,5},{2,6},{3,7},{4,0},{5,1},{6,2},{7,3},{8,12},{9,13},{10,... | collective-permute-start | bytes 73736 | tf_op jit(solution)/shard_map/ppermute | solution.py:480
  21.2 3.8 %collective-permute-start.4 = (bf16[2,48,128]{2,1,0:T(8,128)(2,1)S(1)}, bf16[2,48,128]{2,1,0:T(8,128)(2,1)S(1)}, u32[]{:S(2)}, u32[]{:S(2)}) collective-permute-start(bf16[2,48,128]{2,1,0:T(8,128)(2,1)S(1)} %pad_maximum_fusion.here_ref), channel_id=1, source_target_pairs={{0,6},{1,7},{2,0},{3,1},{4,2},{5,3},{6,4},{7,5},{8,14},{9,15},{10,... | collective-permute-start | bytes 73736 | tf_op jit(solution)/shard_map/ppermute | solution.py:480
  25.7 17.2 %all-to-all-start = ((bf16[8,48,128]{2,1,0:T(8,128)(2,1)}), bf16[8,48,128]{2,1,0:T(8,128)(2,1)S(1)}, u32[]{:S(2)}, u32[]{:S(2)}) async-start(bf16[8,48,128]{2,1,0:T(8,128)(2,1)} %get-tuple-element.42), calls=%async_computation | async-start | bytes 196608 | tf_op jit(solution)/shard_map/all_to_all | solution.py:505
  34.2 4.8 %collective-permute-start.7 = (bf16[256,128]{1,0:T(8,128)(2,1)S(1)}, bf16[256,128]{1,0:T(8,128)(2,1)S(1)}, u32[]{:S(2)}, u32[]{:S(2)}) collective-permute-start(bf16[256,128]{1,0:T(8,128)(2,1)S(1)} %get-tuple-element.49), channel_id=1, source_target_pairs={{0,64},{64,128},{128,192},{192,0},{1,65},{65,129},{129,193},{193,1... | collective-permute-start | bytes 196616 | tf_op jit(solution)/shard_map/ppermute | solution.py:416
  35.5 5.8 %collective-permute-start.8 = (bf16[256,128]{1,0:T(8,128)(2,1)S(1)}, bf16[256,128]{1,0:T(8,128)(2,1)S(1)}, u32[]{:S(2)}, u32[]{:S(2)}) collective-permute-start(bf16[256,128]{1,0:T(8,128)(2,1)S(1)} %get-tuple-element.50), channel_id=1, source_target_pairs={{0,128},{64,192},{128,0},{192,64},{1,129},{65,193},{129,1},{193,65... | collective-permute-start | bytes 196616 | tf_op jit(solution)/shard_map/ppermute | solution.py:416
  37.1 4.9 %collective-permute-start.9 = (bf16[256,128]{1,0:T(8,128)(2,1)S(1)}, bf16[256,128]{1,0:T(8,128)(2,1)S(1)}, u32[]{:S(2)}, u32[]{:S(2)}) collective-permute-start(bf16[256,128]{1,0:T(8,128)(2,1)S(1)} %get-tuple-element.51), channel_id=1, source_target_pairs={{0,192},{64,0},{128,64},{192,128},{1,193},{65,1},{129,65},{193,129... | collective-permute-start | bytes 196616 | tf_op jit(solution)/shard_map/ppermute | solution.py:416

commit v6 on v5

--- a/solution.py
+++ b/solution.py
@@ -167,7 +167,7 @@
     me = lax.axis_index("fsdp")
     for g in range(3):
         w_copies[g].wait()
-        got_ref[...] = jnp.dot(xg_ref[...], w_ref[g], preferred_element_type=F32)
+        got_ref[...] = jnp.dot(xg_ref[...], w_ref[g], preferred_element_type=F32).astype(BF16)
         if g == 0:
             for lo in range(0, rows, 32):
                 x = tok_ref[pl.ds(lo, 32), :].astype(F32)
@@ -176,9 +176,9 @@
         for d in range(4):
             at = pl.ds(pl.multiple_of(lax.rem(me + d, 4) * LANES, LANES), LANES)
             if g < 2:
-                outs[d][g * rows : (g + 1) * rows] = got_ref[:, at].astype(outs[d].dtype)
+                outs[d][g * rows : (g + 1) * rows] = got_ref[:, at]
             else:
-                gates[d][...] = got_ref[:, at].astype(gates[d].dtype)
+                gates[d][...] = got_ref[:, at]
     acc = acc_ref[...]
     high = acc.astype(BF16)
     mid = (acc - high.astype(F32)).astype(BF16)
@@ -196,7 +196,7 @@
         ext_ref[2 + i : 3 + i] = value - high
     for d in range(4):
         at = pl.ds(pl.multiple_of(lax.rem(me + d, 4) * LANES, LANES), LANES)
-        ext_ref[4:6] = got_ref[rows - 2 : rows, at]
+        ext_ref[4:6] = got_ref[rows - EXTRA :, at].astype(F32)[EXTRA - 2 :]
         outs[d][2 * rows :] = ext_ref[...].astype(outs[d].dtype)
 
 
@@ -217,7 +217,7 @@
 
 def summed(refs, lo, n):
     at = pl.ds(lo, n)
-    return refs[0][at, :] + (refs[1][at, :].astype(F32) + refs[2][at, :].astype(F32) + refs[3][at, :].astype(F32))
+    return refs[0][at, :].astype(F32) + (refs[1][at, :].astype(F32) + refs[2][at, :].astype(F32) + refs[3][at, :].astype(F32))
 
 
 def stream(refs, lo, scale_ref, filt_ref, g, ext_ref):
@@ -419,7 +419,7 @@
 
     products = call(
         project_kernel,
-        (shape(packed, LANES), block, block, block, shape(rows, LANES), *[shape(rows, LANES, dtype=BF16)] * 3),
+        ([block] * 4 + [shape(rows, LANES, dtype=BF16)] * 4),
         (tokens, pltpu.with_memory_space_constraint(norm_gain[None], pltpu.HBM), weight),
         [
             pltpu.VMEM((rows, cols), BF16),
@@ -428,7 +428,7 @@
             pltpu.VMEM((rows, cols), BF16),
             pltpu.VMEM((rows, LANES), F32),
             pltpu.VMEM((EXTRA, LANES), F32),
-            pltpu.VMEM((rows, 4 * LANES), F32),
+            pltpu.VMEM((rows, 4 * LANES), BF16),
             pltpu.SemaphoreType.DMA((5,)),
             pltpu.SemaphoreType.DMA((3,)),
         ],

time: 44.5 us -> 45.7 us (1.027)
  local copies, waits for them, and re-layouts: 0.03 us -> 1.26 us
    unnamed x10 -> x12, local copies, waits for them, and re-layouts: 0.02 us -> 1.26 us
where the time goes in v6:
time: 45.7 us; the launch traced here: 45.2 us
  starting transfers between devices  23.6 us (52%)
  waiting for transfers between devices  12.3 us (27%)
  Pallas kernels  7.98 us (17%)
  local copies, waits for them, and re-layouts  1.26 us (3%)
    ppermute x6, starting transfers between devices, exchange(): lax.ppermute(parts[d - 1], 'fsdp', [(i, (i + d) % fsdp) for i in range(fs...  9.42 us
    all_to_all x1, starting transfers between devices, body(): got = lax.all_to_all(send, 'seq', 0, 0, axis_index_groups=line)  8.47 us
    pallas_call x7, Pallas kernels, call(): pl.pallas_call(kernel, out_shape=out_shape, in_specs=places or [VMEM] * l...  7.98 us
    ppermute x6, waiting for transfers between devices, exchange(): lax.ppermute(parts[d - 1], 'fsdp', [(i, (i + d) % fsdp) for i in range(fs...  7.84 us
    ppermute x3, starting transfers between devices, ahead(): lax.ppermute(here, 'seq', [(i, i // LOW * LOW + (i - 2 * d) % LOW) for i...  5.65 us
    ppermute x3, waiting for transfers between devices, ahead(): lax.ppermute(here, 'seq', [(i, i // LOW * LOW + (i - 2 * d) % LOW) for i...  2.39 us
    unnamed x12, local copies, waits for them, and re-layouts  1.26 us
    ppermute x1, waiting for transfers between devices, body(): lax.ppermute(send, 'seq', [(i, i ^ 1) for i in blocks])  1.16 us
  transfers between devices with their start and end apart: 11, of which 9 were waited for; matrix products, arithmetic and copies ran while one was open for 0% of the time, Pallas kernels for 2%

profile of v6, /device:TPU:8, one launch (start us, length us, event | category | flops | bytes accessed | tf_op | source)
XLA Modules:
  0.0 45.2 jit_solution(8853495483038266028)
XLA Ops:
  0.0 1.2 %copy-done = bf16[256,2048]{1,0:T(8,128)(2,1)S(1)} copy-done((bf16[256,2048]{1,0:T(8,128)(2,1)S(1)}, bf16[256,2048]{1,0:T(8,128)(2,1)}, u32[]{:S(2)}) %copy-start) | copy-done | bytes 1048600
  1.3 4.6 %shard_map.82 = (bf16[528,128]{1,0:T(8,128)(2,1)S(1)}, bf16[528,128]{1,0:T(8,128)(2,1)S(1)}, bf16[528,128]{1,0:T(8,128)(2,1)S(1)}, bf16[528,128]{1,0:T(8,128)(2,...) custom-call(bf16[256,2048]{1,0:T(8,128)(2,1)S(1)} %copy-done, ...), custom_call_target="tpu_custom_call" | custom-call | flops 1610612736 | bytes 8151040 | tf_op jit(solution)/shard_map/pallas_call | solution.py:30
  5.8 1.7 %collective-permute-start = (bf16[528,128]{1,0:T(8,128)(2,1)S(1)}, bf16[528,128]{1,0:T(8,128)(2,1)S(1)}, u32[]{:S(2)}, u32[]{:S(2)}) collective-permute-start(bf16[528,128]{1,0:T(8,128)(2,1)S(1)} %get-tuple-element.32), channel_id=1, source_target_pairs={{0,64},{64,128},{128,192},{192,0},{1,65},{65,129},{129,193},{193,1... | collective-permute-start | bytes 405512 | tf_op jit(solution)/shard_map/ppermute | solution.py:416
  7.5 2.7 %collective-permute-start.1 = (bf16[528,128]{1,0:T(8,128)(2,1)S(1)}, bf16[528,128]{1,0:T(8,128)(2,1)S(1)}, u32[]{:S(2)}, u32[]{:S(2)}) collective-permute-start(bf16[528,128]{1,0:T(8,128)(2,1)S(1)} %get-tuple-element.33), channel_id=1, source_target_pairs={{0,128},{64,192},{128,0},{192,64},{1,129},{65,193},{129,1},{193,65... | collective-permute-start | bytes 405512 | tf_op jit(solution)/shard_map/ppermute | solution.py:416
  10.2 0.7 %collective-permute-start.2 = (bf16[528,128]{1,0:T(8,128)(2,1)S(1)}, bf16[528,128]{1,0:T(8,128)(2,1)S(1)}, u32[]{:S(2)}, u32[]{:S(2)}) collective-permute-start(bf16[528,128]{1,0:T(8,128)(2,1)S(1)} %get-tuple-element.34), channel_id=1, source_target_pairs={{0,192},{64,0},{128,64},{192,128},{1,193},{65,1},{129,65},{193,129... | collective-permute-start | bytes 405512 | tf_op jit(solution)/shard_map/ppermute | solution.py:416
  10.8 0.0 copy-done.5
  10.8 0.0 copy-done.3
  10.9 0.5 %shard_map.83 = (f32[8,2,16,128]{3,2,1,0:T(8,128)S(1)}, f32[16,2,8,128]{3,2,1,0:T(8,128)S(1)}, f32[16,2,8,128]{3,2,1,0:T(8,128)S(1)}, f32[4,2,16,128]{3,2,1,0:T(...) custom-call(f32[16,128]{1,0:T(8,128)S(1)} %bitcast.12, ...), custom_call_target="tpu_custom_call" | custom-call | flops 134217728 | bytes 1057280 | tf_op jit(solution)/shard_map/pallas_call | solution.py:30
  11.4 0.1 collective-permute-done.b_ref
  11.5 4.0 %collective-permute-done.1.c_ref = bf16[528,128]{1,0:T(8,128)(2,1)S(1)} collective-permute-done((bf16[528,128]{1,0:T(8,128)(2,1)S(1)}, bf16[528,128]{1,0:T(8,128)(2,1)S(1)}, u32[]{:S(2)}, u32[]{:S(2)}) %collective-permute-start.1) | collective-permute-done | bytes 135200 | tf_op jit(solution)/shard_map/ppermute | solution.py:416
  15.5 0.7 %collective-permute-done.2.d_ref = bf16[528,128]{1,0:T(8,128)(2,1)S(1)} collective-permute-done((bf16[528,128]{1,0:T(8,128)(2,1)S(1)}, bf16[528,128]{1,0:T(8,128)(2,1)S(1)}, u32[]{:S(2)}, u32[]{:S(2)}) %collective-permute-start.2) | collective-permute-done | bytes 135200 | tf_op jit(solution)/shard_map/ppermute | solution.py:416
  16.2 0.6 %shard_map.84 = (f32[256,128]{1,0:T(8,128)S(1)}, f32[256,128]{1,0:T(8,128)S(1)}, f32[4,2,16,128]{3,2,1,0:T(8,128)S(1)}, bf16[48,128]{1,0:T(8,128)(2,1)S(1)}, f32[8,128]{1,0:T(8,128)S(1)}) custom-call(bf16[528,128]{1,0:T(8,128)(2,1)S(1)} %get-tuple-element.31.a_ref, bf16[528,128]{1,0:T(8,128)(2,1)S(1)} %collective-permute-done.b_ref, ...), custom_call_target="tpu_custom_call" | custom-call | flops 134217728 | bytes 1217024 | tf_op jit(solution)/shard_map/pallas_call | solution.py:30
  16.8 0.1 collective-permute-start.3
  16.9 1.2 %collective-permute-done.3 = bf16[48,128]{1,0:T(8,128)(2,1)S(1)} collective-permute-done((bf16[48,128]{1,0:T(8,128)(2,1)S(1)}, bf16[48,128]{1,0:T(8,128)(2,1)S(1)}, u32[]{:S(2)}, u32[]{:S(2)}) %collective-permute-start.3) | collective-permute-done | bytes 12320 | tf_op jit(solution)/shard_map/ppermute | solution.py:477
  18.1 1.5 %collective-permute-start.6 = (bf16[2,48,128]{2,1,0:T(8,128)(2,1)S(1)}, bf16[2,48,128]{2,1,0:T(8,128)(2,1)S(1)}, u32[]{:S(2)}, u32[]{:S(2)}) collective-permute-start(bf16[2,48,128]{2,1,0:T(8,128)(2,1)S(1)} %pad_maximum_fusion.here_ref), channel_id=1, source_target_pairs={{0,2},{1,3},{2,4},{3,5},{4,6},{5,7},{6,0},{7,1},{8,10},{9,11},{10,... | collective-permute-start | bytes 73736 | tf_op jit(solution)/shard_map/ppermute | solution.py:480
  19.6 2.7 %collective-permute-start.5 = (bf16[2,48,128]{2,1,0:T(8,128)(2,1)S(1)}, bf16[2,48,128]{2,1,0:T(8,128)(2,1)S(1)}, u32[]{:S(2)}, u32[]{:S(2)}) collective-permute-start(bf16[2,48,128]{2,1,0:T(8,128)(2,1)S(1)} %pad_maximum_fusion.here_ref), channel_id=1, source_target_pairs={{0,4},{1,5},{2,6},{3,7},{4,0},{5,1},{6,2},{7,3},{8,12},{9,13},{10,... | collective-permute-start | bytes 73736 | tf_op jit(solution)/shard_map/ppermute | solution.py:480
  22.3 1.4 %collective-permute-start.4 = (bf16[2,48,128]{2,1,0:T(8,128)(2,1)S(1)}, bf16[2,48,128]{2,1,0:T(8,128)(2,1)S(1)}, u32[]{:S(2)}, u32[]{:S(2)}) collective-permute-start(bf16[2,48,128]{2,1,0:T(8,128)(2,1)S(1)} %pad_maximum_fusion.here_ref), channel_id=1, source_target_pairs={{0,6},{1,7},{2,0},{3,1},{4,2},{5,3},{6,4},{7,5},{8,14},{9,15},{10,... | collective-permute-start | bytes 73736 | tf_op jit(solution)/shard_map/ppermute | solution.py:480
  23.8 0.0 collective-permute-done.6.before_ref
  23.8 1.2 %collective-permute-done.5.across_ref = bf16[2,48,128]{2,1,0:T(8,128)(2,1)S(1)} collective-permute-done((bf16[2,48,128]{2,1,0:T(8,128)(2,1)S(1)}, bf16[2,48,128]{2,1,0:T(8,128)(2,1)S(1)}, u32[]{:S(2)}, u32[]{:S(2)}) %collective-permute-start.5) | collective-permute-done | bytes 24608 | tf_op jit(solution)/shard_map/ppermute | solution.py:480
  24.9 1.2 %collective-permute-done.4.next_ref = bf16[2,48,128]{2,1,0:T(8,128)(2,1)S(1)} collective-permute-done((bf16[2,48,128]{2,1,0:T(8,128)(2,1)S(1)}, bf16[2,48,128]{2,1,0:T(8,128)(2,1)S(1)}, u32[]{:S(2)}, u32[]{:S(2)}) %collective-permute-start.4) | collective-permute-done | bytes 24608 | tf_op jit(solution)/shard_map/ppermute | solution.py:480
  26.2 0.7 %shard_map.85 = (f32[2,16,128]{2,1,0:T(8,128)S(1)}, f32[2,8,128]{2,1,0:T(8,128)S(1)}, bf16[8,48,128]{2,1,0:T(8,128)(2,1)}) custom-call(bf16[2,48,128]{2,1,0:T(8,128)(2,1)S(1)} %pad_maximum_fusion.here_ref, bf16[2,48,128]{2,1,0:T(8,128)(2,1)S(1)} %collective-permute-done.4.next_ref, bf16[2,48,128]{2,1,0:T(8,128)(2,1)S(1)} %collective-permute-done.5.across_ref, ...), custom_call_target="tpu_custom_call" | custom-call | flops 16777216 | bytes 635392 | tf_op jit(solution)/shard_map/pallas_call | solution.py:30
  26.9 8.5 %all-to-all-start = ((bf16[8,48,128]{2,1,0:T(8,128)(2,1)}), bf16[8,48,128]{2,1,0:T(8,128)(2,1)S(1)}, u32[]{:S(2)}, u32[]{:S(2)}) async-start(bf16[8,48,128]{2,1,0:T(8,128)(2,1)} %get-tuple-element.42), calls=%async_computation | async-start | bytes 196608 | tf_op jit(solution)/shard_map/all_to_all | solution.py:505
  35.4 1.3 %collective-permute-start.7 = (bf16[256,128]{1,0:T(8,128)(2,1)S(1)}, bf16[256,128]{1,0:T(8,128)(2,1)S(1)}, u32[]{:S(2)}, u32[]{:S(2)}) collective-permute-start(bf16[256,128]{1,0:T(8,128)(2,1)S(1)} %get-tuple-element.49), channel_id=1, source_target_pairs={{0,64},{64,128},{128,192},{192,0},{1,65},{65,129},{129,193},{193,1... | collective-permute-start | bytes 196616 | tf_op jit(solution)/shard_map/ppermute | solution.py:416
  36.7 1.6 %collective-permute-start.8 = (bf16[256,128]{1,0:T(8,128)(2,1)S(1)}, bf16[256,128]{1,0:T(8,128)(2,1)S(1)}, u32[]{:S(2)}, u32[]{:S(2)}) collective-permute-start(bf16[256,128]{1,0:T(8,128)(2,1)S(1)} %get-tuple-element.50), channel_id=1, source_target_pairs={{0,128},{64,192},{128,0},{192,64},{1,129},{65,193},{129,1},{193,65... | collective-permute-start | bytes 196616 | tf_op jit(solution)/shard_map/ppermute | solution.py:416
  38.2 1.6 %collective-permute-start.9 = (bf16[256,128]{1,0:T(8,128)(2,1)S(1)}, bf16[256,128]{1,0:T(8,128)(2,1)S(1)}, u32[]{:S(2)}, u32[]{:S(2)}) collective-permute-start(bf16[256,128]{1,0:T(8,128)(2,1)S(1)} %get-tuple-element.51), channel_id=1, source_target_pairs={{0,192},{64,0},{128,64},{192,128},{1,193},{65,1},{129,65},{193,129... | collective-permute-start | bytes 196616 | tf_op jit(solution)/shard_map/ppermute | solution.py:416
  39.8 0.3 shard_map.86._.local_ref
  40.1 0.0 collective-permute-done.7.b_ref
  40.2 2.4 %collective-permute-done.8.c_ref = bf16[256,128]{1,0:T(8,128)(2,1)S(1)} collective-permute-done((bf16[256,128]{1,0:T(8,128)(2,1)S(1)}, bf16[256,128]{1,0:T(8,128)(2,1)S(1)}, u32[]{:S(2)}, u32[]{:S(2)}) %collective-permute-start.8) | collective-permute-done | bytes 65568 | tf_op jit(solution)/shard_map/ppermute | solution.py:416
  42.5 0.6 %collective-permute-done.9.d_ref = bf16[256,128]{1,0:T(8,128)(2,1)S(1)} collective-permute-done((bf16[256,128]{1,0:T(8,128)(2,1)S(1)}, bf16[256,128]{1,0:T(8,128)(2,1)S(1)}, u32[]{:S(2)}, u32[]{:S(2)}) %collective-permute-start.9) | collective-permute-done | bytes 65568 | tf_op jit(solution)/shard_map/ppermute | solution.py:416
  43.1 0.1 shard_map.87.gate_ref
  43.2 0.9 %all-to-all-done.got_ref = bf16[8,48,128]{2,1,0:T(8,128)(2,1)S(1)} async-done(((bf16[8,48,128]{2,1,0:T(8,128)(2,1)}), bf16[8,48,128]{2,1,0:T(8,128)(2,1)S(1)}, u32[]{:S(2)}, u32[]{:S(2)}) %all-to-all-start) | async-done | bytes 98336 | tf_op jit(solution)/shard_map/all_to_all | solution.py:505
  44.1 1.1 %shard_map.88 = bf16[128,256]{1,0:T(8,128)(2,1)} custom-call(bf16[8,48,128]{2,1,0:T(8,128)(2,1)S(1)} %all-to-all-done.got_ref, f32[8,2,16,128]{3,2,1,0:T(8,128)S(1)} %get-tuple-element.43.far_tab_ref, f32[2,8,128]{2,1,0:T(8,128)S(1)} %get-tuple-element.44._.rim_ref, f32[9,2,16,128]{3,2,1,0:T(8,128)S(1)} %get-tuple-element.41.plane_ref, ...), custom_call_target="tpu_custom_call" | custom-call | flops 134217728 | bytes 1132032 | tf_op jit(solution)/shard_map/pallas_call | solution.py:30
  (11 shorter events, 0.0 us)
Async XLA Ops:
  0.0 39.8 %copy-start.1 = (f32[128]{0:T(128)S(1)}, f32[128]{0:T(128)}, u32[]{:S(2)}) copy-start(f32[128]{0:T(128)} %param.15) | copy-start | bytes 1540
  0.0 1.2 %copy-start = (bf16[256,2048]{1,0:T(8,128)(2,1)S(1)}, bf16[256,2048]{1,0:T(8,128)(2,1)}, u32[]{:S(2)}) copy-start(bf16[256,2048]{1,0:T(8,128)(2,1)} %tok_hbm.1) | copy-start | bytes 3145732
  1.2 9.6 %copy-start.5 = (f32[128,3,3]{0,2,1:T(4,128)S(1)}, f32[128,3,3]{0,2,1:T(4,128)}, u32[]{:S(2)}) copy-start(f32[128,3,3]{0,2,1:T(4,128)} %param.11) | copy-start | bytes 13828
  1.2 9.6 %copy-start.2 = (f32[128,16]{0,1:T(8,128)S(1)}, f32[128,16]{0,1:T(8,128)}, u32[]{:S(2)}) copy-start(f32[128,16]{0,1:T(8,128)} %param.12) | copy-start | bytes 24580
  1.2 9.6 %copy-start.3 = (f32[128,16]{0,1:T(8,128)S(1)}, f32[128,16]{0,1:T(8,128)}, u32[]{:S(2)}) copy-start(f32[128,16]{0,1:T(8,128)} %param.13) | copy-start | bytes 24580
  1.2 9.6 %copy-start.4 = (f32[128,16]{0,1:T(8,128)S(1)}, f32[128,16]{0,1:T(8,128)}, u32[]{:S(2)}) copy-start(f32[128,16]{0,1:T(8,128)} %param.14) | copy-start | bytes 24580
  5.8 5.6 %collective-permute-start = (bf16[528,128]{1,0:T(8,128)(2,1)S(1)}, bf16[528,128]{1,0:T(8,128)(2,1)S(1)}, u32[]{:S(2)}, u32[]{:S(2)}) collective-permute-start(bf16[528,128]{1,0:T(8,128)(2,1)S(1)} %get-tuple-element.32), channel_id=1, source_target_pairs={{0,64},{64,128},{128,192},{192,0},{1,65},{65,129},{129,193},{193,1... | collective-permute-start | bytes 405512 | tf_op jit(solution)/shard_map/ppermute | solution.py:416
  7.5 8.0 %collective-permute-start.1 = (bf16[528,128]{1,0:T(8,128)(2,1)S(1)}, bf16[528,128]{1,0:T(8,128)(2,1)S(1)}, u32[]{:S(2)}, u32[]{:S(2)}) collective-permute-start(bf16[528,128]{1,0:T(8,128)(2,1)S(1)} %get-tuple-element.33), channel_id=1, source_target_pairs={{0,128},{64,192},{128,0},{192,64},{1,129},{65,193},{129,1},{193,65... | collective-permute-start | bytes 405512 | tf_op jit(solution)/shard_map/ppermute | solution.py:416
  10.2 6.1 %collective-permute-start.2 = (bf16[528,128]{1,0:T(8,128)(2,1)S(1)}, bf16[528,128]{1,0:T(8,128)(2,1)S(1)}, u32[]{:S(2)}, u32[]{:S(2)}) collective-permute-start(bf16[528,128]{1,0:T(8,128)(2,1)S(1)} %get-tuple-element.34), channel_id=1, source_target_pairs={{0,192},{64,0},{128,64},{192,128},{1,193},{65,1},{129,65},{193,129... | collective-permute-start | bytes 405512 | tf_op jit(solution)/shard_map/ppermute | solution.py:416
  16.8 1.3 %collective-permute-start.3 = (bf16[48,128]{1,0:T(8,128)(2,1)S(1)}, bf16[48,128]{1,0:T(8,128)(2,1)S(1)}, u32[]{:S(2)}, u32[]{:S(2)}) collective-permute-start(bf16[48,128]{1,0:T(8,128)(2,1)S(1)} %get-tuple-element.38), channel_id=1, source_target_pairs={{0,1},{1,0},{2,3},{3,2},{4,5},{5,4},{6,7},{7,6},{8,9},{9,8},{10,11... | collective-permute-start | bytes 36872 | tf_op jit(solution)/shard_map/ppermute | solution.py:477
  18.1 5.7 %collective-permute-start.6 = (bf16[2,48,128]{2,1,0:T(8,128)(2,1)S(1)}, bf16[2,48,128]{2,1,0:T(8,128)(2,1)S(1)}, u32[]{:S(2)}, u32[]{:S(2)}) collective-permute-start(bf16[2,48,128]{2,1,0:T(8,128)(2,1)S(1)} %pad_maximum_fusion.here_ref), channel_id=1, source_target_pairs={{0,2},{1,3},{2,4},{3,5},{4,6},{5,7},{6,0},{7,1},{8,10},{9,11},{10,... | collective-permute-start | bytes 73736 | tf_op jit(solution)/shard_map/ppermute | solution.py:480
  19.6 5.3 %collective-permute-start.5 = (bf16[2,48,128]{2,1,0:T(8,128)(2,1)S(1)}, bf16[2,48,128]{2,1,0:T(8,128)(2,1)S(1)}, u32[]{:S(2)}, u32[]{:S(2)}) collective-permute-start(bf16[2,48,128]{2,1,0:T(8,128)(2,1)S(1)} %pad_maximum_fusion.here_ref), channel_id=1, source_target_pairs={{0,4},{1,5},{2,6},{3,7},{4,0},{5,1},{6,2},{7,3},{8,12},{9,13},{10,... | collective-permute-start | bytes 73736 | tf_op jit(solution)/shard_map/ppermute | solution.py:480
  22.3 3.8 %collective-permute-start.4 = (bf16[2,48,128]{2,1,0:T(8,128)(2,1)S(1)}, bf16[2,48,128]{2,1,0:T(8,128)(2,1)S(1)}, u32[]{:S(2)}, u32[]{:S(2)}) collective-permute-start(bf16[2,48,128]{2,1,0:T(8,128)(2,1)S(1)} %pad_maximum_fusion.here_ref), channel_id=1, source_target_pairs={{0,6},{1,7},{2,0},{3,1},{4,2},{5,3},{6,4},{7,5},{8,14},{9,15},{10,... | collective-permute-start | bytes 73736 | tf_op jit(solution)/shard_map/ppermute | solution.py:480
  26.9 17.2 %all-to-all-start = ((bf16[8,48,128]{2,1,0:T(8,128)(2,1)}), bf16[8,48,128]{2,1,0:T(8,128)(2,1)S(1)}, u32[]{:S(2)}, u32[]{:S(2)}) async-start(bf16[8,48,128]{2,1,0:T(8,128)(2,1)} %get-tuple-element.42), calls=%async_computation | async-start | bytes 196608 | tf_op jit(solution)/shard_map/all_to_all | solution.py:505
  35.4 4.8 %collective-permute-start.7 = (bf16[256,128]{1,0:T(8,128)(2,1)S(1)}, bf16[256,128]{1,0:T(8,128)(2,1)S(1)}, u32[]{:S(2)}, u32[]{:S(2)}) collective-permute-start(bf16[256,128]{1,0:T(8,128)(2,1)S(1)} %get-tuple-element.49), channel_id=1, source_target_pairs={{0,64},{64,128},{128,192},{192,0},{1,65},{65,129},{129,193},{193,1... | collective-permute-start | bytes 196616 | tf_op jit(solution)/shard_map/ppermute | solution.py:416
  36.7 5.8 %collective-permute-start.8 = (bf16[256,128]{1,0:T(8,128)(2,1)S(1)}, bf16[256,128]{1,0:T(8,128)(2,1)S(1)}, u32[]{:S(2)}, u32[]{:S(2)}) collective-permute-start(bf16[256,128]{1,0:T(8,128)(2,1)S(1)} %get-tuple-element.50), channel_id=1, source_target_pairs={{0,128},{64,192},{128,0},{192,64},{1,129},{65,193},{129,1},{193,65... | collective-permute-start | bytes 196616 | tf_op jit(solution)/shard_map/ppermute | solution.py:416
  38.2 4.9 %collective-permute-start.9 = (bf16[256,128]{1,0:T(8,128)(2,1)S(1)}, bf16[256,128]{1,0:T(8,128)(2,1)S(1)}, u32[]{:S(2)}, u32[]{:S(2)}) collective-permute-start(bf16[256,128]{1,0:T(8,128)(2,1)S(1)} %get-tuple-element.51), channel_id=1, source_target_pairs={{0,192},{64,0},{128,64},{192,128},{1,193},{65,1},{129,65},{193,129... | collective-permute-start | bytes 196616 | tf_op jit(solution)/shard_map/ppermute | solution.py:416

commit v7 on v5

--- a/solution.py
+++ b/solution.py
@@ -143,7 +143,7 @@
     rows, cols = tok_ref.shape
     outs = (own_ref, one_ref, two_ref, three_ref)
     gates = (own_gate, one_gate, two_gate, three_gate)
-    pieces = 4
+    pieces = 8
     span = rows // pieces
     gain_copy = pltpu.make_async_copy(gain_hbm, gain_ref, sems.at[0])
     gain_copy.start()
@@ -159,7 +159,7 @@
     gain = gain_ref[...]
     for i in range(pieces):
         tok_copies[i].wait()
-        if i == 1:
+        if i == 3:
             w_copies[2].start(priority=0)
         for lo in range(i * span, (i + 1) * span, 32):
             x = tok_ref[pl.ds(lo, 32), :].astype(F32)
@@ -429,7 +429,7 @@
             pltpu.VMEM((rows, LANES), F32),
             pltpu.VMEM((EXTRA, LANES), F32),
             pltpu.VMEM((rows, 4 * LANES), F32),
-            pltpu.SemaphoreType.DMA((5,)),
+            pltpu.SemaphoreType.DMA((9,)),
             pltpu.SemaphoreType.DMA((3,)),
         ],
         limit=52 << 20,

time: 44.5 us -> 44.6 us (level)
  no operation moved by 1% of the time
where the time goes in v7:
time: 44.6 us; the launch traced here: 44.2 us
  starting transfers between devices  23.7 us (53%)
  waiting for transfers between devices  12.3 us (28%)
  Pallas kernels  8.16 us (18%)
    ppermute x6, starting transfers between devices, exchange(): lax.ppermute(parts[d - 1], 'fsdp', [(i, (i + d) % fsdp) for i in range(fs...  9.43 us
    all_to_all x1, starting transfers between devices, body(): got = lax.all_to_all(send, 'seq', 0, 0, axis_index_groups=line)  8.47 us
    pallas_call x7, Pallas kernels, call(): pl.pallas_call(kernel, out_shape=out_shape, in_specs=places or [VMEM] * l...  8.16 us
    ppermute x6, waiting for transfers between devices, exchange(): lax.ppermute(parts[d - 1], 'fsdp', [(i, (i + d) % fsdp) for i in range(fs...  7.82 us
    ppermute x3, starting transfers between devices, ahead(): lax.ppermute(here, 'seq', [(i, i // LOW * LOW + (i - 2 * d) % LOW) for i...  5.65 us
    ppermute x3, waiting for transfers between devices, ahead(): lax.ppermute(here, 'seq', [(i, i // LOW * LOW + (i - 2 * d) % LOW) for i...  2.39 us
    ppermute x1, waiting for transfers between devices, body(): lax.ppermute(send, 'seq', [(i, i ^ 1) for i in blocks])  1.16 us
    all_to_all x1, waiting for transfers between devices, body(): got = lax.all_to_all(send, 'seq', 0, 0, axis_index_groups=line)  0.91 us
  transfers between devices with their start and end apart: 11, of which 9 were waited for; matrix products, arithmetic and copies ran while one was open for 0% of the time, Pallas kernels for 2%

profile of v7, /device:TPU:8, one launch (start us, length us, event | category | flops | bytes accessed | tf_op | source)
XLA Modules:
  0.0 44.2 jit_solution(3538747602161991347)
XLA Ops:
  0.0 0.0 copy-start.1
  0.0 0.0 copy-start
  0.0 4.7 %shard_map.82 = (f32[528,128]{1,0:T(8,128)S(1)}, bf16[528,128]{1,0:T(8,128)(2,1)S(1)}, bf16[528,128]{1,0:T(8,128)(2,1)S(1)}, bf16[528,128]{1,0:T(8,128)(2,1)S(1)...) custom-call(bf16[256,2048]{1,0:T(8,128)(2,1)} %tok_hbm.1, ...), custom_call_target="tpu_custom_call" | custom-call | flops 1610612736 | bytes 8351744 | tf_op jit(solution)/shard_map/pallas_call | solution.py:30
  4.8 1.6 %collective-permute-start = (bf16[528,128]{1,0:T(8,128)(2,1)S(1)}, bf16[528,128]{1,0:T(8,128)(2,1)S(1)}, u32[]{:S(2)}, u32[]{:S(2)}) collective-permute-start(bf16[528,128]{1,0:T(8,128)(2,1)S(1)} %get-tuple-element.32), channel_id=1, source_target_pairs={{0,64},{64,128},{128,192},{192,0},{1,65},{65,129},{129,193},{193,1... | collective-permute-start | bytes 405512 | tf_op jit(solution)/shard_map/ppermute | solution.py:416
  6.4 2.7 %collective-permute-start.1 = (bf16[528,128]{1,0:T(8,128)(2,1)S(1)}, bf16[528,128]{1,0:T(8,128)(2,1)S(1)}, u32[]{:S(2)}, u32[]{:S(2)}) collective-permute-start(bf16[528,128]{1,0:T(8,128)(2,1)S(1)} %get-tuple-element.33), channel_id=1, source_target_pairs={{0,128},{64,192},{128,0},{192,64},{1,129},{65,193},{129,1},{193,65... | collective-permute-start | bytes 405512 | tf_op jit(solution)/shard_map/ppermute | solution.py:416
  9.1 0.7 %collective-permute-start.2 = (bf16[528,128]{1,0:T(8,128)(2,1)S(1)}, bf16[528,128]{1,0:T(8,128)(2,1)S(1)}, u32[]{:S(2)}, u32[]{:S(2)}) collective-permute-start(bf16[528,128]{1,0:T(8,128)(2,1)S(1)} %get-tuple-element.34), channel_id=1, source_target_pairs={{0,192},{64,0},{128,64},{192,128},{1,193},{65,1},{129,65},{193,129... | collective-permute-start | bytes 405512 | tf_op jit(solution)/shard_map/ppermute | solution.py:416
  9.8 0.0 copy-done.1
  9.8 0.5 %shard_map.83 = (f32[8,2,16,128]{3,2,1,0:T(8,128)S(1)}, f32[16,2,8,128]{3,2,1,0:T(8,128)S(1)}, f32[16,2,8,128]{3,2,1,0:T(8,128)S(1)}, f32[4,2,16,128]{3,2,1,0:T(...) custom-call(f32[16,128]{1,0:T(8,128)S(1)} %bitcast.12, ...), custom_call_target="tpu_custom_call" | custom-call | flops 134217728 | bytes 1057280 | tf_op jit(solution)/shard_map/pallas_call | solution.py:30
  10.4 0.1 collective-permute-done.b_ref
  10.4 4.0 %collective-permute-done.1.c_ref = bf16[528,128]{1,0:T(8,128)(2,1)S(1)} collective-permute-done((bf16[528,128]{1,0:T(8,128)(2,1)S(1)}, bf16[528,128]{1,0:T(8,128)(2,1)S(1)}, u32[]{:S(2)}, u32[]{:S(2)}) %collective-permute-start.1) | collective-permute-done | bytes 135200 | tf_op jit(solution)/shard_map/ppermute | solution.py:416
  14.4 0.8 %collective-permute-done.2.d_ref = bf16[528,128]{1,0:T(8,128)(2,1)S(1)} collective-permute-done((bf16[528,128]{1,0:T(8,128)(2,1)S(1)}, bf16[528,128]{1,0:T(8,128)(2,1)S(1)}, u32[]{:S(2)}, u32[]{:S(2)}) %collective-permute-start.2) | collective-permute-done | bytes 135200 | tf_op jit(solution)/shard_map/ppermute | solution.py:416
  15.2 0.6 %shard_map.84 = (f32[256,128]{1,0:T(8,128)S(1)}, f32[256,128]{1,0:T(8,128)S(1)}, f32[4,2,16,128]{3,2,1,0:T(8,128)S(1)}, bf16[48,128]{1,0:T(8,128)(2,1)S(1)}, f32[8,128]{1,0:T(8,128)S(1)}) custom-call(f32[528,128]{1,0:T(8,128)S(1)} %get-tuple-element.31.a_ref, bf16[528,128]{1,0:T(8,128)(2,1)S(1)} %collective-permute-done.b_ref, ...), custom_call_target="tpu_custom_call" | custom-call | flops 134217728 | bytes 1352192 | tf_op jit(solution)/shard_map/pallas_call | solution.py:30
  15.8 0.1 collective-permute-start.3
  15.9 1.2 %collective-permute-done.3 = bf16[48,128]{1,0:T(8,128)(2,1)S(1)} collective-permute-done((bf16[48,128]{1,0:T(8,128)(2,1)S(1)}, bf16[48,128]{1,0:T(8,128)(2,1)S(1)}, u32[]{:S(2)}, u32[]{:S(2)}) %collective-permute-start.3) | collective-permute-done | bytes 12320 | tf_op jit(solution)/shard_map/ppermute | solution.py:477
  17.1 1.5 %collective-permute-start.6 = (bf16[2,48,128]{2,1,0:T(8,128)(2,1)S(1)}, bf16[2,48,128]{2,1,0:T(8,128)(2,1)S(1)}, u32[]{:S(2)}, u32[]{:S(2)}) collective-permute-start(bf16[2,48,128]{2,1,0:T(8,128)(2,1)S(1)} %pad_maximum_fusion.here_ref), channel_id=1, source_target_pairs={{0,2},{1,3},{2,4},{3,5},{4,6},{5,7},{6,0},{7,1},{8,10},{9,11},{10,... | collective-permute-start | bytes 73736 | tf_op jit(solution)/shard_map/ppermute | solution.py:480
  18.6 2.7 %collective-permute-start.5 = (bf16[2,48,128]{2,1,0:T(8,128)(2,1)S(1)}, bf16[2,48,128]{2,1,0:T(8,128)(2,1)S(1)}, u32[]{:S(2)}, u32[]{:S(2)}) collective-permute-start(bf16[2,48,128]{2,1,0:T(8,128)(2,1)S(1)} %pad_maximum_fusion.here_ref), channel_id=1, source_target_pairs={{0,4},{1,5},{2,6},{3,7},{4,0},{5,1},{6,2},{7,3},{8,12},{9,13},{10,... | collective-permute-start | bytes 73736 | tf_op jit(solution)/shard_map/ppermute | solution.py:480
  21.3 1.4 %collective-permute-start.4 = (bf16[2,48,128]{2,1,0:T(8,128)(2,1)S(1)}, bf16[2,48,128]{2,1,0:T(8,128)(2,1)S(1)}, u32[]{:S(2)}, u32[]{:S(2)}) collective-permute-start(bf16[2,48,128]{2,1,0:T(8,128)(2,1)S(1)} %pad_maximum_fusion.here_ref), channel_id=1, source_target_pairs={{0,6},{1,7},{2,0},{3,1},{4,2},{5,3},{6,4},{7,5},{8,14},{9,15},{10,... | collective-permute-start | bytes 73736 | tf_op jit(solution)/shard_map/ppermute | solution.py:480
  22.7 0.0 collective-permute-done.6.before_ref
  22.7 1.2 %collective-permute-done.5.across_ref = bf16[2,48,128]{2,1,0:T(8,128)(2,1)S(1)} collective-permute-done((bf16[2,48,128]{2,1,0:T(8,128)(2,1)S(1)}, bf16[2,48,128]{2,1,0:T(8,128)(2,1)S(1)}, u32[]{:S(2)}, u32[]{:S(2)}) %collective-permute-start.5) | collective-permute-done | bytes 24608 | tf_op jit(solution)/shard_map/ppermute | solution.py:480
  23.9 1.2 %collective-permute-done.4.next_ref = bf16[2,48,128]{2,1,0:T(8,128)(2,1)S(1)} collective-permute-done((bf16[2,48,128]{2,1,0:T(8,128)(2,1)S(1)}, bf16[2,48,128]{2,1,0:T(8,128)(2,1)S(1)}, u32[]{:S(2)}, u32[]{:S(2)}) %collective-permute-start.4) | collective-permute-done | bytes 24608 | tf_op jit(solution)/shard_map/ppermute | solution.py:480
  25.1 0.7 %shard_map.85 = (f32[2,16,128]{2,1,0:T(8,128)S(1)}, f32[2,8,128]{2,1,0:T(8,128)S(1)}, bf16[8,48,128]{2,1,0:T(8,128)(2,1)}) custom-call(bf16[2,48,128]{2,1,0:T(8,128)(2,1)S(1)} %pad_maximum_fusion.here_ref, bf16[2,48,128]{2,1,0:T(8,128)(2,1)S(1)} %collective-permute-done.4.next_ref, bf16[2,48,128]{2,1,0:T(8,128)(2,1)S(1)} %collective-permute-done.5.across_ref, ...), custom_call_target="tpu_custom_call" | custom-call | flops 16777216 | bytes 635392 | tf_op jit(solution)/shard_map/pallas_call | solution.py:30
  25.9 8.5 %all-to-all-start = ((bf16[8,48,128]{2,1,0:T(8,128)(2,1)}), bf16[8,48,128]{2,1,0:T(8,128)(2,1)S(1)}, u32[]{:S(2)}, u32[]{:S(2)}) async-start(bf16[8,48,128]{2,1,0:T(8,128)(2,1)} %get-tuple-element.42), calls=%async_computation | async-start | bytes 196608 | tf_op jit(solution)/shard_map/all_to_all | solution.py:505
  34.4 1.3 %collective-permute-start.7 = (bf16[256,128]{1,0:T(8,128)(2,1)S(1)}, bf16[256,128]{1,0:T(8,128)(2,1)S(1)}, u32[]{:S(2)}, u32[]{:S(2)}) collective-permute-start(bf16[256,128]{1,0:T(8,128)(2,1)S(1)} %get-tuple-element.49), channel_id=1, source_target_pairs={{0,64},{64,128},{128,192},{192,0},{1,65},{65,129},{129,193},{193,1... | collective-permute-start | bytes 196616 | tf_op jit(solution)/shard_map/ppermute | solution.py:416
  35.6 1.6 %collective-permute-start.8 = (bf16[256,128]{1,0:T(8,128)(2,1)S(1)}, bf16[256,128]{1,0:T(8,128)(2,1)S(1)}, u32[]{:S(2)}, u32[]{:S(2)}) collective-permute-start(bf16[256,128]{1,0:T(8,128)(2,1)S(1)} %get-tuple-element.50), channel_id=1, source_target_pairs={{0,128},{64,192},{128,0},{192,64},{1,129},{65,193},{129,1},{193,65... | collective-permute-start | bytes 196616 | tf_op jit(solution)/shard_map/ppermute | solution.py:416
  37.2 1.6 %collective-permute-start.9 = (bf16[256,128]{1,0:T(8,128)(2,1)S(1)}, bf16[256,128]{1,0:T(8,128)(2,1)S(1)}, u32[]{:S(2)}, u32[]{:S(2)}) collective-permute-start(bf16[256,128]{1,0:T(8,128)(2,1)S(1)} %get-tuple-element.51), channel_id=1, source_target_pairs={{0,192},{64,0},{128,64},{192,128},{1,193},{65,1},{129,65},{193,129... | collective-permute-start | bytes 196616 | tf_op jit(solution)/shard_map/ppermute | solution.py:416
  38.8 0.3 shard_map.86._.local_ref
  39.1 0.0 collective-permute-done.7.b_ref
  39.1 2.3 %collective-permute-done.8.c_ref = bf16[256,128]{1,0:T(8,128)(2,1)S(1)} collective-permute-done((bf16[256,128]{1,0:T(8,128)(2,1)S(1)}, bf16[256,128]{1,0:T(8,128)(2,1)S(1)}, u32[]{:S(2)}, u32[]{:S(2)}) %collective-permute-start.8) | collective-permute-done | bytes 65568 | tf_op jit(solution)/shard_map/ppermute | solution.py:416
  41.5 0.6 %collective-permute-done.9.d_ref = bf16[256,128]{1,0:T(8,128)(2,1)S(1)} collective-permute-done((bf16[256,128]{1,0:T(8,128)(2,1)S(1)}, bf16[256,128]{1,0:T(8,128)(2,1)S(1)}, u32[]{:S(2)}, u32[]{:S(2)}) %collective-permute-start.9) | collective-permute-done | bytes 65568 | tf_op jit(solution)/shard_map/ppermute | solution.py:416
  42.1 0.1 shard_map.87.gate_ref
  42.2 0.9 %all-to-all-done.got_ref = bf16[8,48,128]{2,1,0:T(8,128)(2,1)S(1)} async-done(((bf16[8,48,128]{2,1,0:T(8,128)(2,1)}), bf16[8,48,128]{2,1,0:T(8,128)(2,1)S(1)}, u32[]{:S(2)}, u32[]{:S(2)}) %all-to-all-start) | async-done | bytes 98336 | tf_op jit(solution)/shard_map/all_to_all | solution.py:505
  43.1 1.1 %shard_map.88 = bf16[128,256]{1,0:T(8,128)(2,1)} custom-call(bf16[8,48,128]{2,1,0:T(8,128)(2,1)S(1)} %all-to-all-done.got_ref, f32[8,2,16,128]{3,2,1,0:T(8,128)S(1)} %get-tuple-element.43.far_tab_ref, f32[2,8,128]{2,1,0:T(8,128)S(1)} %get-tuple-element.44._.rim_ref, f32[9,2,16,128]{3,2,1,0:T(8,128)S(1)} %get-tuple-element.41.plane_ref, ...), custom_call_target="tpu_custom_call" | custom-call | flops 134217728 | bytes 1132032 | tf_op jit(solution)/shard_map/pallas_call | solution.py:30
  (9 shorter events, 0.0 us)
Async XLA Ops:
  0.0 9.8 %copy-start.4 = (f32[128,3,3]{0,2,1:T(4,128)S(1)}, f32[128,3,3]{0,2,1:T(4,128)}, u32[]{:S(2)}) copy-start(f32[128,3,3]{0,2,1:T(4,128)} %param.11) | copy-start | bytes 13828
  0.0 9.8 %copy-start.3 = (f32[128,16]{0,1:T(8,128)S(1)}, f32[128,16]{0,1:T(8,128)}, u32[]{:S(2)}) copy-start(f32[128,16]{0,1:T(8,128)} %param.14) | copy-start | bytes 24580
  0.0 9.8 %copy-start.2 = (f32[128,16]{0,1:T(8,128)S(1)}, f32[128,16]{0,1:T(8,128)}, u32[]{:S(2)}) copy-start(f32[128,16]{0,1:T(8,128)} %param.13) | copy-start | bytes 24580
  0.0 9.8 %copy-start.1 = (f32[128,16]{0,1:T(8,128)S(1)}, f32[128,16]{0,1:T(8,128)}, u32[]{:S(2)}) copy-start(f32[128,16]{0,1:T(8,128)} %param.12) | copy-start | bytes 24580
  0.0 38.7 %copy-start = (f32[128]{0:T(128)S(1)}, f32[128]{0:T(128)}, u32[]{:S(2)}) copy-start(f32[128]{0:T(128)} %param.15) | copy-start | bytes 1540
  4.8 5.6 %collective-permute-start = (bf16[528,128]{1,0:T(8,128)(2,1)S(1)}, bf16[528,128]{1,0:T(8,128)(2,1)S(1)}, u32[]{:S(2)}, u32[]{:S(2)}) collective-permute-start(bf16[528,128]{1,0:T(8,128)(2,1)S(1)} %get-tuple-element.32), channel_id=1, source_target_pairs={{0,64},{64,128},{128,192},{192,0},{1,65},{65,129},{129,193},{193,1... | collective-permute-start | bytes 405512 | tf_op jit(solution)/shard_map/ppermute | solution.py:416
  6.4 8.0 %collective-permute-start.1 = (bf16[528,128]{1,0:T(8,128)(2,1)S(1)}, bf16[528,128]{1,0:T(8,128)(2,1)S(1)}, u32[]{:S(2)}, u32[]{:S(2)}) collective-permute-start(bf16[528,128]{1,0:T(8,128)(2,1)S(1)} %get-tuple-element.33), channel_id=1, source_target_pairs={{0,128},{64,192},{128,0},{192,64},{1,129},{65,193},{129,1},{193,65... | collective-permute-start | bytes 405512 | tf_op jit(solution)/shard_map/ppermute | solution.py:416
  9.1 6.1 %collective-permute-start.2 = (bf16[528,128]{1,0:T(8,128)(2,1)S(1)}, bf16[528,128]{1,0:T(8,128)(2,1)S(1)}, u32[]{:S(2)}, u32[]{:S(2)}) collective-permute-start(bf16[528,128]{1,0:T(8,128)(2,1)S(1)} %get-tuple-element.34), channel_id=1, source_target_pairs={{0,192},{64,0},{128,64},{192,128},{1,193},{65,1},{129,65},{193,129... | collective-permute-start | bytes 405512 | tf_op jit(solution)/shard_map/ppermute | solution.py:416
  15.8 1.3 %collective-permute-start.3 = (bf16[48,128]{1,0:T(8,128)(2,1)S(1)}, bf16[48,128]{1,0:T(8,128)(2,1)S(1)}, u32[]{:S(2)}, u32[]{:S(2)}) collective-permute-start(bf16[48,128]{1,0:T(8,128)(2,1)S(1)} %get-tuple-element.38), channel_id=1, source_target_pairs={{0,1},{1,0},{2,3},{3,2},{4,5},{5,4},{6,7},{7,6},{8,9},{9,8},{10,11... | collective-permute-start | bytes 36872 | tf_op jit(solution)/shard_map/ppermute | solution.py:477
  17.1 5.7 %collective-permute-start.6 = (bf16[2,48,128]{2,1,0:T(8,128)(2,1)S(1)}, bf16[2,48,128]{2,1,0:T(8,128)(2,1)S(1)}, u32[]{:S(2)}, u32[]{:S(2)}) collective-permute-start(bf16[2,48,128]{2,1,0:T(8,128)(2,1)S(1)} %pad_maximum_fusion.here_ref), channel_id=1, source_target_pairs={{0,2},{1,3},{2,4},{3,5},{4,6},{5,7},{6,0},{7,1},{8,10},{9,11},{10,... | collective-permute-start | bytes 73736 | tf_op jit(solution)/shard_map/ppermute | solution.py:480
  18.6 5.3 %collective-permute-start.5 = (bf16[2,48,128]{2,1,0:T(8,128)(2,1)S(1)}, bf16[2,48,128]{2,1,0:T(8,128)(2,1)S(1)}, u32[]{:S(2)}, u32[]{:S(2)}) collective-permute-start(bf16[2,48,128]{2,1,0:T(8,128)(2,1)S(1)} %pad_maximum_fusion.here_ref), channel_id=1, source_target_pairs={{0,4},{1,5},{2,6},{3,7},{4,0},{5,1},{6,2},{7,3},{8,12},{9,13},{10,... | collective-permute-start | bytes 73736 | tf_op jit(solution)/shard_map/ppermute | solution.py:480
  21.3 3.8 %collective-permute-start.4 = (bf16[2,48,128]{2,1,0:T(8,128)(2,1)S(1)}, bf16[2,48,128]{2,1,0:T(8,128)(2,1)S(1)}, u32[]{:S(2)}, u32[]{:S(2)}) collective-permute-start(bf16[2,48,128]{2,1,0:T(8,128)(2,1)S(1)} %pad_maximum_fusion.here_ref), channel_id=1, source_target_pairs={{0,6},{1,7},{2,0},{3,1},{4,2},{5,3},{6,4},{7,5},{8,14},{9,15},{10,... | collective-permute-start | bytes 73736 | tf_op jit(solution)/shard_map/ppermute | solution.py:480
  25.9 17.2 %all-to-all-start = ((bf16[8,48,128]{2,1,0:T(8,128)(2,1)}), bf16[8,48,128]{2,1,0:T(8,128)(2,1)S(1)}, u32[]{:S(2)}, u32[]{:S(2)}) async-start(bf16[8,48,128]{2,1,0:T(8,128)(2,1)} %get-tuple-element.42), calls=%async_computation | async-start | bytes 196608 | tf_op jit(solution)/shard_map/all_to_all | solution.py:505
  34.4 4.8 %collective-permute-start.7 = (bf16[256,128]{1,0:T(8,128)(2,1)S(1)}, bf16[256,128]{1,0:T(8,128)(2,1)S(1)}, u32[]{:S(2)}, u32[]{:S(2)}) collective-permute-start(bf16[256,128]{1,0:T(8,128)(2,1)S(1)} %get-tuple-element.49), channel_id=1, source_target_pairs={{0,64},{64,128},{128,192},{192,0},{1,65},{65,129},{129,193},{193,1... | collective-permute-start | bytes 196616 | tf_op jit(solution)/shard_map/ppermute | solution.py:416
  35.6 5.8 %collective-permute-start.8 = (bf16[256,128]{1,0:T(8,128)(2,1)S(1)}, bf16[256,128]{1,0:T(8,128)(2,1)S(1)}, u32[]{:S(2)}, u32[]{:S(2)}) collective-permute-start(bf16[256,128]{1,0:T(8,128)(2,1)S(1)} %get-tuple-element.50), channel_id=1, source_target_pairs={{0,128},{64,192},{128,0},{192,64},{1,129},{65,193},{129,1},{193,65... | collective-permute-start | bytes 196616 | tf_op jit(solution)/shard_map/ppermute | solution.py:416
  37.2 4.9 %collective-permute-start.9 = (bf16[256,128]{1,0:T(8,128)(2,1)S(1)}, bf16[256,128]{1,0:T(8,128)(2,1)S(1)}, u32[]{:S(2)}, u32[]{:S(2)}) collective-permute-start(bf16[256,128]{1,0:T(8,128)(2,1)S(1)} %get-tuple-element.51), channel_id=1, source_target_pairs={{0,192},{64,0},{128,64},{192,128},{1,193},{65,1},{129,65},{193,129... | collective-permute-start | bytes 196616 | tf_op jit(solution)/shard_map/ppermute | solution.py:416
